TPU v7x, 32 devices: a whole 2x2x4 slice. The times are simulated.
32 devices in a mesh: dp: 4 (over x, core), seq: 8 (over z, y).
Axes of the slice: x: 2, y: 2, z: 4, core: 2. Of those that a mesh axis runs over, the one named last changes fastest.
Arguments:
- tokens: bfloat16 [24, 2048, 512], P('dp', 'seq'), may hold values from -6 to 6
- document_starts: int32 [24, 16], P('dp'), may hold values from 0 to 2047, as said below
- attention_in: bfloat16 [512, 1536], replicated, may hold values from -0.375 to 0.375
- attention_out: bfloat16 [512, 512], replicated, may hold values from -1 to 1
- feedforward_in: bfloat16 [512, 1536], replicated, may hold values from -0.25 to 0.25
- feedforward_out: bfloat16 [768, 512], replicated, may hold values from -0.21875 to 0.21875
- gain_first: float32 [512], replicated, may hold values from 0.1 to 1.9
- gain_second: float32 [512], replicated, may hold values from 0.1 to 1.9
- result_grad: bfloat16 [24, 2048, 512], P('dp', 'seq'), may hold values from -6 to 6
Outputs:
- activations: bfloat16 [24, 2048, 512], P('dp', 'seq')
- grad_tokens: float32 [24, 2048, 512], P('dp', 'seq')
- grad_attention_in: float32 [512, 1536], replicated
- grad_attention_out: float32 [512, 512], replicated
- grad_feedforward_in: float32 [512, 1536], replicated
- grad_feedforward_out: float32 [768, 512], replicated
- grad_gain_first: float32 [512], replicated
- grad_gain_second: float32 [512], replicated
Inputs may be any that keep to these rules, and one draw needn't show every extreme that they name: `document_starts`: in each row the 16 document starts rise strictly from 0.
All inputs are finite; a program needn't handle non-finite values.
Results may differ from a plain program's by a relative error of at most 0.014.
The roundings to bfloat16 on the way count: a program that leaves them out, or rounds other values in their place, can miss the bound.
Values may be sent and summed in bfloat16 or wider, within the bound.
No kernel may reach another device: no remote copies, remote signals or barrier semaphores. Data moves between devices by JAX's collectives and lax.ppermute only.
A program may use at most 192 MiB of HBM per device.

v0:
```python
import functools

import jax
import jax.numpy as jnp
import numpy as np
from jax import lax
from jax.experimental import pallas as pl
from jax.experimental.pallas import tpu as pltpu
from jax.sharding import PartitionSpec as P

HEADS = 8
HEAD_DIM = 64
HALF = HEAD_DIM // 2
HALF_WIN = 64
EPSILON = 1e-05
ROTARY_BASE = 10000.0
SCALE = HEAD_DIM**-0.5
BLOCKS = 32
GROUP = 4
WIDE = GROUP * HEAD_DIM
LANES = 128
MB = 1024 * 1024

F32 = jnp.float32
BF16 = jnp.bfloat16


def dot(a, b, contract):
    return lax.dot_general(a, b, ((contract[:1], contract[1:]), ((), ())), preferred_element_type=F32)


def nn(a, b):
    return dot(a, b, (1, 0))


def nt(a, b):
    return dot(a, b, (1, 1))


def tn(a, b):
    return dot(a, b, (0, 0))


def iota(shape, dim):
    return lax.broadcasted_iota(jnp.int32, shape, dim)


def flat(values):
    return values.reshape(-1, values.shape[-1])


def normalize(values):
    shifted = values - jnp.mean(values, axis=-1, keepdims=True)
    inverse = lax.rsqrt(jnp.mean(shifted * shifted, axis=-1, keepdims=True) + EPSILON)
    return shifted * inverse, inverse


def norm_back(scaled_grad, unit, inverse):
    return (
        scaled_grad
        - jnp.mean(scaled_grad, axis=-1, keepdims=True)
        - unit * jnp.mean(scaled_grad * unit, axis=-1, keepdims=True)
    ) * inverse


def halves_first():
    old, new = iota((WIDE, WIDE), 0), iota((WIDE, WIDE), 1)
    moved = (old % HEAD_DIM) // HALF * LANES + old // HEAD_DIM * HALF + old % HALF
    return (moved == new).astype(BF16)


def head_of(shape, halved):
    lane = iota(shape, 1)
    return lane % LANES // HALF if halved else lane // HEAD_DIM


def by_head(values, halved):
    head = head_of(values.shape, halved)
    zero = jnp.zeros_like(values)
    return jnp.concatenate([jnp.where(head == h, values, zero) for h in range(GROUP)], axis=0)


def pick_heads(stacked, halved):
    count = stacked.shape[0] // GROUP
    head = head_of((count, stacked.shape[1]), halved)
    out = stacked[:count]
    for h in range(1, GROUP):
        out = jnp.where(head == h, stacked[h * count : (h + 1) * count], out)
    return out


def turn(values, cosine, sines):
    first, second = values[:, :LANES], values[:, LANES:]
    return jnp.concatenate([first * cosine - second * sines, second * cosine + first * sines], axis=1)


def turn_back(values, cosine, sines):
    first, second = values[:, :LANES], values[:, LANES:]
    return jnp.concatenate([first * cosine + second * sines, second * cosine - first * sines], axis=1)


def load_kernel(tokens_ref, *refs):
    count = len(refs) // 2 - 1
    sources, (inner_ref, other_ref, *outs), sems = refs[:count], refs[count:-1], refs[-1]
    own_len, win = tokens_ref.shape[1], HALF_WIN
    odd = lax.axis_index("seq") % 2
    copies = []
    for k, (out, high) in enumerate(((inner_ref, odd == 0), (other_ref, odd == 1))):
        at = pl.multiple_of(jnp.where(high, own_len - win, 0), win)
        copies.append(pltpu.make_async_copy(tokens_ref.at[:, pl.ds(at, win)], out, sems.at[k]))
    for k, (source, out) in enumerate(zip(sources, outs, strict=True)):
        copies.append(pltpu.make_async_copy(source, out, sems.at[k + 2]))
    for copy in copies:
        copy.start()
    for copy in copies:
        copy.wait()


def by_side(inner, other):
    odd = lax.axis_index("seq") % 2 == 1
    return jnp.where(odd, inner, other), jnp.where(odd, other, inner)


def project_kernel(
    tokens_ref,
    starts_ref,
    in_ref,
    gain_ref,
    base_ref,
    table_ref,
    normed_ref,
    queries_ref,
    keys_ref,
    values_ref,
    weight_ref,
    angles_ref,
    bounds_ref,
):
    rows, own_len, width = tokens_ref.shape
    win = HALF_WIN
    place = lax.axis_index("seq")
    start = place * own_len
    row_len = own_len * lax.axis_size("seq")

    base_cos, base_sin = base_ref[place, 0:1], base_ref[place, 1:2]
    angles_ref[0] = base_cos * table_ref[0] - base_sin * table_ref[1]
    angles_ref[1] = base_sin * table_ref[0] + base_cos * table_ref[1]

    lane = iota((rows, own_len - 2 * win + 4 * win), 1)
    mid = own_len - 2 * win
    pos = start + jnp.where(
        lane < mid, lane + win, jnp.where(lane < mid + 2 * win, lane % win, own_len - win + lane % win)
    )
    first, last = jnp.maximum(pos - win, 0), jnp.minimum(pos + win, row_len - 1)
    for j in range(starts_ref.shape[1]):
        cut = starts_ref[:, j : j + 1]
        first = jnp.maximum(first, jnp.where(cut <= pos, cut, 0))
        last = jnp.minimum(last, jnp.where(cut > pos, cut - 1, row_len))
    for r in range(rows):
        bounds_ref[r, 0:1] = first[r : r + 1]
        bounds_ref[r, 1:2] = last[r : r + 1]

    order = halves_first()
    for c in range(0, 2 * width, WIDE):
        weight_ref[:, c : c + WIDE] = nn(in_ref[:, c : c + WIDE], order).astype(BF16)
    weight_ref[:, 2 * width :] = in_ref[:, 2 * width :]

    pair = 6
    cosine, sines = angles_ref[0, win : win + own_len], angles_ref[1, win : win + own_len]
    cosine, sines = jnp.concatenate([cosine] * pair), jnp.concatenate([sines] * pair)

    @pl.loop(0, rows // pair)
    def _(i):
        at = pl.ds(i * pair, pair)
        unit, _ = normalize(flat(tokens_ref[at]).astype(F32))
        normed = (unit * gain_ref[...]).astype(BF16)
        normed_ref[at] = normed.reshape(pair, own_len, width)
        queries, keys = nn(normed, weight_ref[:, :width]), nn(normed, weight_ref[:, width : 2 * width])
        for c in range(0, width, WIDE):
            part = turn(queries[:, c : c + WIDE], cosine * SCALE, sines * SCALE)
            queries_ref[at, :, c : c + WIDE] = part.astype(BF16).reshape(pair, own_len, WIDE)
            part = turn(keys[:, c : c + WIDE], cosine, sines)
            keys_ref[at, :, c : c + WIDE] = part.astype(BF16).reshape(pair, own_len, WIDE)
        values_ref[at] = nn(normed, weight_ref[:, 2 * width :]).astype(BF16).reshape(pair, own_len, width)


def halo_kernel(inner_ref, other_ref, weight_ref, gain_ref, angles_ref, normed_ref, keys_ref, values_ref):
    rows, win, width = inner_ref.shape
    pair = 3
    span = angles_ref.shape[1]
    cosine = jnp.concatenate([angles_ref[0, :win], angles_ref[0, span - win :]] * pair)
    sines = jnp.concatenate([angles_ref[1, :win], angles_ref[1, span - win :]] * pair)

    @pl.loop(0, rows // pair)
    def _(i):
        at = pl.ds(i * pair, pair)
        sides = by_side(inner_ref[at], other_ref[at])
        unit, _ = normalize(flat(jnp.concatenate(sides, axis=1)).astype(F32))
        normed = (unit * gain_ref[...]).astype(BF16)
        normed_ref[at] = normed.reshape(pair, 2 * win, width)
        keys = nn(normed, weight_ref[:, width : 2 * width])
        for c in range(0, width, WIDE):
            part = turn(keys[:, c : c + WIDE], cosine, sines)
            keys_ref[at, :, c : c + WIDE] = part.astype(BF16).reshape(pair, 2 * win, WIDE)
        values_ref[at] = nn(normed, weight_ref[:, 2 * width :]).astype(BF16).reshape(pair, 2 * win, width)


def bias_of(bounds_ref, row, lanes, first_key, keys):
    key = first_key + iota((keys, LANES), 0)
    first, last = bounds_ref[row, 0:1, lanes], bounds_ref[row, 1:2, lanes]
    return jnp.where((key >= first) & (key <= last), 0.0, -jnp.inf)


def probabilities(scores, bias):
    parts = []
    for c in range(0, scores.shape[1], LANES):
        part = scores[:, c : c + LANES] + bias
        part = jnp.exp(part - jnp.max(part, axis=0, keepdims=True))
        parts.append(part * (1.0 / jnp.sum(part, axis=0, keepdims=True)))
    return jnp.concatenate(parts, axis=1)


def attend_mid_kernel(queries_ref, keys_ref, values_ref, bounds_ref, attended_ref, probs_ref):
    rows, own_len, width = queries_ref.shape
    win = HALF_WIN
    mid = own_len - 2 * win
    start = lax.axis_index("seq") * own_len
    pair = 6

    @pl.loop(0, rows // pair)
    def _(i):
        for r in range(pair):
            row = i * pair + r
            bias = bias_of(bounds_ref, row, slice(0, mid), start, own_len)
            for g in range(width // WIDE):
                cols = slice(g * WIDE, (g + 1) * WIDE)
                probs = probabilities(
                    nt(keys_ref[row, :, cols], by_head(queries_ref[row, win : win + mid, cols], True)), bias
                )
                probs_ref[row, g] = probs
                out = tn(probs.astype(BF16), values_ref[row, :, cols])
                attended_ref[row, :, cols] = pick_heads(out, False).astype(BF16)


def wide_side(own, halo, side):
    win = HALF_WIN
    if side == 0:
        return jnp.concatenate([halo[:win], own[: 2 * win]], axis=0)
    return jnp.concatenate([own[own.shape[0] - 2 * win :], halo[win:]], axis=0)


def attend_out_kernel(
    queries_ref, keys_ref, values_ref, halo_keys_ref, halo_values_ref, bounds_ref, attended_ref, probs_ref
):
    rows, own_len, width = queries_ref.shape
    win = HALF_WIN
    mid = own_len - 2 * win
    start = lax.axis_index("seq") * own_len
    pair = 6

    @pl.loop(0, rows // pair)
    def _(i):
        for r in range(pair):
            row = i * pair + r
            for side in range(2):
                own = slice(0, win) if side == 0 else slice(own_len - win, own_len)
                lanes = slice(mid + side * LANES, mid + (side + 1) * LANES)
                bias = bias_of(bounds_ref, row, lanes, start + own.start - win, 3 * win)
                for g in range(width // WIDE):
                    cols = slice(g * WIDE, (g + 1) * WIDE)
                    keys = wide_side(keys_ref[row, :, cols], halo_keys_ref[row, :, cols], side)
                    values = wide_side(values_ref[row, :, cols], halo_values_ref[row, :, cols], side)
                    probs = probabilities(nt(keys, by_head(queries_ref[row, own, cols], True)), bias)
                    probs_ref[row, side, g] = probs
                    out = tn(probs.astype(BF16), values)
                    attended_ref[row, side * win : (side + 1) * win, cols] = pick_heads(out, False).astype(BF16)


def gelu_parts(gate):
    bell = jnp.exp(-0.5 * gate * gate)
    t = 1.0 / (1.0 + (0.3275911 * 0.7071067811865476) * jnp.abs(gate))
    tail = t * (
        0.5 * 0.254829592
        + t * (0.5 * -0.284496736 + t * (0.5 * 1.421413741 + t * (0.5 * -1.453152027 + t * (0.5 * 1.061405429))))
    )
    tail = tail * bell
    return jnp.where(gate < 0, tail, 1.0 - tail), gate * bell * 0.3989422804014327


def part_of(ref, at, outer):
    own_len, win = ref.shape[1], HALF_WIN
    if outer:
        return flat(jnp.concatenate([ref[at, :win], ref[at, own_len - win :]], axis=1))
    return flat(ref[at, win : own_len - win])


def dense_kernel(
    outer,
    tokens_ref,
    top_ref,
    attended_ref,
    out_ref,
    up_ref,
    down_ref,
    gain_ref,
    middle_ref,
    normed_ref,
    mixed_ref,
    grad_up_ref,
    grad_middle_ref,
    branch_ref,
    grad_attended_ref,
):
    rows, count, width = attended_ref.shape
    hidden = down_ref.shape[0]
    pair = 3

    @pl.loop(0, rows // pair)
    def _(i):
        at = pl.ds(i * pair, pair)

        def put(ref, values, cols=slice(None)):
            ref[at, :, cols] = values.reshape(pair, count, -1)

        top = part_of(top_ref, at, outer)
        middle = part_of(tokens_ref, at, outer).astype(F32) + nn(flat(attended_ref[at]), out_ref[...])
        put(middle_ref, middle)
        unit, inverse = normalize(middle)
        normed = (unit * gain_ref[...]).astype(BF16)
        put(normed_ref, normed)
        grad_hidden = [nt(top, down_ref[:512]), nt(top, down_ref[512:])]
        for c in range(0, hidden, 256):
            halves = [up_ref[:, c : c + 256], up_ref[:, hidden + c : hidden + c + 256]]
            both = nn(normed, jnp.concatenate(halves, axis=1))
            gate, lift = both[:, :256], both[:, 256:]
            grad_mixed = grad_hidden[c // 512][:, c % 512 : c % 512 + 256]
            phi, slope = gelu_parts(gate)
            active = gate * phi
            put(mixed_ref, (active * lift).astype(BF16), slice(c, c + 256))
            put(grad_up_ref, (grad_mixed * lift * (phi + slope)).astype(BF16), slice(c, c + 256))
            put(grad_up_ref, (grad_mixed * active).astype(BF16), slice(hidden + c, hidden + c + 256))
        grad_normed = nt(flat(grad_up_ref[at]), up_ref[...])
        grad_middle = top.astype(F32) + norm_back(grad_normed * gain_ref[...], unit, inverse)
        put(grad_middle_ref, grad_middle)
        branch = grad_middle.astype(BF16)
        put(branch_ref, branch)
        put(grad_attended_ref, nt(branch, out_ref[...]).astype(BF16))


def store_blocks(keep_ref, send_ref, store):
    seq, dp = lax.axis_index("seq"), lax.axis_index("dp")
    place = (dp % 2) * 16 + (dp // 2) * 8 + (seq % 2) * 4 + (seq // 2) % 2 * 2 + (seq // 4) % 2
    for ref, base in ((keep_ref, 0), (send_ref, BLOCKS // 2)):

        @pl.loop(0, BLOCKS // 2)
        def _(i):
            store(ref, i, place ^ (i + base))


def weights_kernel(
    outer,
    top_ref,
    normed_ref,
    grad_up_ref,
    mixed_ref,
    attended_ref,
    branch_ref,
    *refs,
):
    begun, (*sums,) = (refs[:3], refs[3:]) if outer else ((None,) * 3, refs)
    if outer:
        keep_ref, send_ref, *sums = sums
    up_sum, down_sum, out_sum = sums
    width = top_ref.shape[2]

    def add(part, ref, at):
        return part if ref is None else part + ref[at].astype(F32)

    normed = flat(normed_ref[...])
    for c in range(0, up_sum.shape[1], 512):
        at = (slice(None), slice(c, c + 512))
        up_sum[at] = add(tn(normed, flat(grad_up_ref[:, :, c : c + 512])), begun[0], at).astype(BF16)
    top = part_of(top_ref, slice(0, top_ref.shape[0]), outer)
    for c in range(0, down_sum.shape[0], 256):
        at = (slice(c, c + 256), slice(None))
        down_sum[at] = add(tn(flat(mixed_ref[:, :, c : c + 256]), top), begun[1], at).astype(down_sum.dtype)
    at = (slice(None), slice(None))
    out_sum[at] = add(tn(flat(attended_ref[...]), flat(branch_ref[...])), begun[2], at).astype(BF16)
    if not outer:
        return
    rows, down_rows = width // BLOCKS, down_sum.shape[0] // BLOCKS

    def store(ref, i, block):
        own = pl.ds(pl.multiple_of(block * rows, rows), rows)
        at = 0
        for c in range(0, up_sum.shape[1], width):
            ref[i, at : at + rows] = up_sum[own, c : c + width]
            at += rows
        ref[i, at : at + rows] = out_sum[own, :]
        at += rows
        ref[i, at:] = down_sum[pl.ds(pl.multiple_of(block * down_rows, down_rows), down_rows), :].astype(BF16)

    store_blocks(keep_ref, send_ref, store)


def attend_back_kernel(
    group,
    queries_ref,
    keys_ref,
    values_ref,
    halo_keys_ref,
    halo_values_ref,
    mid_grad_ref,
    out_grad_ref,
    mid_probs_ref,
    out_probs_ref,
    angles_ref,
    own_ref,
    halo_ref,
):
    rows, own_len, _ = queries_ref.shape
    win = HALF_WIN
    mid = own_len - 2 * win
    cols = slice(group * WIDE, (group + 1) * WIDE)
    cosine, sines = angles_ref[0], angles_ref[1]
    own_cos, own_sin = cosine[win : win + own_len], sines[win : win + own_len]
    halo_cos = jnp.concatenate([cosine[:win], cosine[win + own_len :]])
    halo_sin = jnp.concatenate([sines[:win], sines[win + own_len :]])
    pair = 2

    def unit(queries, keys, values, grads, probs):
        q4, g4 = by_head(queries, True), by_head(grads, False)
        grad_probs = nt(values, g4)
        lows, grad_scores = [], []
        for c in range(0, probs.shape[1], LANES):
            part, grad_part = probs[:, c : c + LANES], grad_probs[:, c : c + LANES]
            inner = jnp.sum(part * grad_part, axis=0, keepdims=True)
            lows.append(part.astype(BF16))
            grad_scores.append((part * (grad_part - inner)).astype(BF16))
        grad_scores = jnp.concatenate(grad_scores, axis=1)
        return (
            pick_heads(tn(grad_scores, keys), True),
            nn(grad_scores, q4),
            nn(jnp.concatenate(lows, axis=1), g4),
        )

    @pl.loop(0, rows // pair)
    def _(i):
        for r in range(pair):
            row = i * pair + r
            queries, keys, values = queries_ref[row, :, cols], keys_ref[row, :, cols], values_ref[row, :, cols]
            halo_keys, halo_values = halo_keys_ref[row, :, cols], halo_values_ref[row, :, cols]
            grads = out_grad_ref[row, :, cols]
            middle = unit(queries[win : win + mid], keys, values, mid_grad_ref[row, :, cols], mid_probs_ref[row, group])
            sides = [
                unit(
                    queries[:win] if side == 0 else queries[own_len - win :],
                    wide_side(keys, halo_keys, side),
                    wide_side(values, halo_values, side),
                    grads[side * win : (side + 1) * win],
                    out_probs_ref[row, side, group],
                )
                for side in range(2)
            ]
            low, high = sides
            own = [jnp.concatenate([low[0], middle[0], high[0]], axis=0) * SCALE]
            halo = []
            for k in (1, 2):
                own.append(middle[k] + jnp.concatenate([low[k][win:], high[k][: 2 * win]], axis=0))
                halo.append(jnp.concatenate([low[k][:win], high[k][2 * win :]], axis=0))
            own_ref[row, :, :WIDE] = turn_back(own[0], own_cos, own_sin).astype(BF16)
            own_ref[row, :, WIDE : 2 * WIDE] = turn_back(own[1], own_cos, own_sin).astype(BF16)
            own_ref[row, :, 2 * WIDE :] = own[2].astype(BF16)
            halo_ref[row, :, :WIDE] = turn_back(halo[0], halo_cos, halo_sin).astype(BF16)
            halo_ref[row, :, WIDE:] = halo[1].astype(BF16)


def weight_in_kernel(normed_ref, halo_normed_ref, *refs):
    *grads, total = refs
    width = normed_ref.shape[2]
    normed, halo_normed = flat(normed_ref[...]), flat(halo_normed_ref[...])
    order = halves_first()
    for k in range(3):
        part = tn(normed, jnp.concatenate([flat(own[:, :, k * WIDE : (k + 1) * WIDE]) for own in grads[::2]], axis=1))
        if k > 0:
            halo = [flat(halo[:, :, (k - 1) * WIDE : k * WIDE]) for halo in grads[1::2]]
            part = part + tn(halo_normed, jnp.concatenate(halo, axis=1))
        part = part.astype(BF16)
        if k < 2:
            part = [nt(part[:, c : c + WIDE], order).astype(BF16) for c in range(0, width, WIDE)]
            part = jnp.concatenate(part, axis=1)
        total[:, k * width : (k + 1) * width] = part


def split_kernel(total_ref, keep_ref, send_ref):
    rows, width = total_ref.shape[0] // BLOCKS, total_ref.shape[0]

    def store(ref, i, block):
        own = pl.ds(pl.multiple_of(block * rows, rows), rows)
        for k in range(3):
            ref[i, k * rows : (k + 1) * rows] = total_ref[own, k * width : (k + 1) * width]

    store_blocks(keep_ref, send_ref, store)


def grad_halo_kernel(weight_ref, *refs):
    *grads, inner_ref, other_ref = refs
    rows, win, width = inner_ref.shape
    total = None
    for g, ref in enumerate(grads):
        weight = jnp.concatenate(
            [weight_ref[:, k * width + g * WIDE : k * width + (g + 1) * WIDE] for k in (1, 2)], axis=1
        )
        part = nt(flat(ref[...]), weight)
        total = part if total is None else total + part
    total = total.astype(BF16).reshape(rows, 2 * win, width)
    inner_ref[...], other_ref[...] = by_side(total[:, :win], total[:, win:])


def backward_kernel(*refs):
    shared, (weight_ref, *grads, inner_ref, other_ref) = refs[:10], refs[10:]
    for group in range(len(grads) // 2):
        attend_back_kernel(group, *shared, *grads[2 * group : 2 * group + 2])
    grad_halo_kernel(weight_ref, *grads[1::2], inner_ref, other_ref)


def grad_own_kernel(weight_ref, *refs):
    *grads, out_ref = refs
    rows, own_len, width = out_ref.shape
    pair = 2
    groups = len(grads)

    @pl.loop(0, rows // pair)
    def _(i):
        at = pl.ds(i * pair, pair)
        grad = jnp.concatenate([flat(ref[at]) for ref in grads], axis=1)
        weight = jnp.concatenate(
            [
                weight_ref[:, k * width + g * WIDE : k * width + (g + 1) * WIDE]
                for g in range(groups)
                for k in range(3)
            ],
            axis=1,
        )
        out_ref[at] = nt(grad, weight).reshape(pair, own_len, width)


def result_kernel(mid_middle_ref, out_middle_ref, mid_mixed_ref, out_mixed_ref, down_ref, result_ref):
    own_len, win = result_ref.shape[1], HALF_WIN
    pair = 3

    @pl.loop(0, result_ref.shape[0] // pair)
    def _(i):
        at = pl.ds(i * pair, pair)

        def result(middle_ref, mixed_ref):
            total = flat(middle_ref[at]) + nn(flat(mixed_ref[at]), down_ref[...])
            return total.astype(BF16).reshape(middle_ref[at].shape)

        result_ref[at, win : own_len - win] = result(mid_middle_ref, mid_mixed_ref)
        outer = result(out_middle_ref, out_mixed_ref)
        result_ref[at, :win] = outer[:, :win]
        result_ref[at, own_len - win :] = outer[:, win:]


def finish_kernel(
    tokens_ref, own_ref, inner_ref, other_ref, mid_grad_ref, out_grad_ref, gain_ref, grad_ref
):
    own_len, win = tokens_ref.shape[1], HALF_WIN

    @pl.loop(0, tokens_ref.shape[0])
    def _(row):
        unit, inverse = normalize(tokens_ref[row].astype(F32))
        own = own_ref[row]
        low, high = by_side(inner_ref[row].astype(F32), other_ref[row].astype(F32))
        grads = jnp.concatenate(
            [own[:win] + low, own[win : own_len - win], own[own_len - win :] + high],
            axis=0,
        )
        outer = out_grad_ref[row]
        middle = jnp.concatenate([outer[:win], mid_grad_ref[row], outer[win:]], axis=0)
        grad_ref[row] = middle + norm_back(grads * gain_ref[...], unit, inverse)


def place_kernel(own_ref, other_ref, weight_ref, gain_ref, *out_refs):
    *out_refs, gain_grad_ref = out_refs

    def store(ref, i, block):
        at = 0
        for out in out_refs:
            rows = out.shape[0] // BLOCKS
            for c in range(0, out.shape[1], ref.shape[2]):
                out[pl.ds(pl.multiple_of(block * rows, rows), rows), c : c + ref.shape[2]] = ref[
                    i, at : at + rows
                ].astype(F32)
                at += rows

    store_blocks(own_ref, other_ref, store)
    total = None
    for c in range(0, weight_ref.shape[1], LANES):
        part = out_refs[0][:, c : c + LANES] * weight_ref[:, c : c + LANES].astype(F32)
        total = part if total is None else total + part
    gain_grad_ref[...] = jnp.sum(total.T, axis=0, keepdims=True) / gain_ref[...]


def add_kernel(count, *refs):
    parts, outs = refs[:count], refs[count:]
    size = parts[0].shape[0] // len(outs)
    for k, out in enumerate(outs):
        at = slice(k * size, (k + 1) * size)
        out[...] = sum(p[at].astype(F32) for p in parts).astype(BF16)


def join_kernel(*refs):
    *parts, out = refs
    size = parts[0].shape[0]
    for k, part in enumerate(parts):
        out[k * size : (k + 1) * size] = part[...]


def to_neighbours(inner, other):
    size = lax.axis_size("seq")
    pairs = [(i, i ^ 1) for i in range(size)]
    between = [p for i in range(1, size - 1, 2) for p in ((i, i + 1), (i + 1, i))]
    return lax.ppermute(inner, "seq", pairs), lax.ppermute(other, "seq", between)


def swap_route(core, x, y, z, rest):
    dp, seq = lax.axis_size("dp"), lax.axis_size("seq")

    def partner(i):
        d, s = divmod(i, seq)
        return (d ^ (core + 2 * x)) * seq + (s ^ (y + 2 * z + 8 * rest))

    return [(i, partner(i)) for i in range(dp * seq)]


def swap(values, core=0, x=0, y=0, z=0, rest=0):
    return lax.ppermute(values, ("dp", "seq"), swap_route(core, x, y, z, rest))


def shape(*dims, kind=BF16):
    return jax.ShapeDtypeStruct(dims, kind)


def call(name, kernel, outs, *args, after=(), token=False, grant=6, flops=1e9, scratch=()):
    outs = [*outs, shape(8, LANES, kind=F32)] if token else outs
    spec = pl.BlockSpec(memory_space=pltpu.VMEM)
    moved = sum(int(np.prod(a.shape)) * a.dtype.itemsize for a in (*args, *outs))

    def body(*refs):
        refs = refs[len(after) :]
        if token:
            at = len(args) + len(outs) - 1
            refs[at][...] = jnp.zeros_like(refs[at])
            refs = refs[:at] + refs[at + 1 :]
        return kernel(*refs)

    return pl.pallas_call(
        body,
        out_shape=outs,
        in_specs=[pl.BlockSpec(memory_space=pl.ANY)] * len(after) + [spec] * len(args),
        out_specs=[spec] * len(outs),
        scratch_shapes=scratch,
        compiler_params=pltpu.CompilerParams(vmem_limit_bytes=grant * MB),
        cost_estimate=pl.CostEstimate(flops=int(flops) // 100, bytes_accessed=moved // 100, transcendentals=0),
        name=name,
    )(*after, *args)


def add_up(parts, outs, after=()):
    return call("add", functools.partial(add_kernel, len(parts)), outs, *parts, after=after, grant=4, flops=1e6)


def join(parts, after=()):
    size = parts[0].shape
    out = shape(len(parts) * size[0], *size[1:])
    return call("join", join_kernel, [out], *parts, after=after, grant=4, flops=1e6)[0]


def swap_plane(parts):
    return [swap(parts[k], x=k >> 1, y=k & 1) for k in (1, 2, 3)]


def swap_rest(own):
    rest = 1
    while 8 * rest < lax.axis_size("seq"):
        (own,) = add_up([own, swap(own, rest=rest)], [shape(*own.shape)])
        rest *= 2
    return own


def angle_tables(own_len, pieces):
    inverse = ROTARY_BASE ** (-(np.arange(0, HEAD_DIM, 2) / HEAD_DIM))
    inverse = np.tile(inverse, LANES // HALF)
    base = np.arange(pieces)[:, None] * own_len * inverse
    local = (np.arange(own_len + 2 * HALF_WIN) - HALF_WIN)[:, None] * inverse
    return [jnp.asarray(np.stack([np.cos(a), np.sin(a)], axis=d), F32) for a, d in ((base, 1), (local, 0))]


def shards(
    tokens,
    document_starts,
    attention_in,
    attention_out,
    feedforward_in,
    feedforward_out,
    gain_first,
    gain_second,
    result_grad,
):
    rows, own_len, width = tokens.shape
    hidden = feedforward_out.shape[0]
    win = HALF_WIN
    mid = own_len - 2 * win
    seq = lax.axis_size("seq")
    groups = width // WIDE
    gain_one, gain_two = gain_first[None], gain_second[None]

    small = [document_starts, gain_one, attention_in, *angle_tables(own_len, seq)]
    outs = [pltpu.VMEM((rows, win, width), BF16)] * 2 + [pltpu.VMEM(a.shape, a.dtype) for a in small]
    inner_tokens, other_tokens, document_starts, gain_one, attention_in, *tables = pl.pallas_call(
        load_kernel,
        out_shape=outs,
        in_specs=[pl.BlockSpec(memory_space=pltpu.HBM)] * (1 + len(small)),
        out_specs=[pl.BlockSpec(memory_space=pltpu.VMEM)] * len(outs),
        scratch_shapes=[pltpu.SemaphoreType.DMA((len(outs),))],
        compiler_params=pltpu.CompilerParams(vmem_limit_bytes=MB),
        name="load",
    )(*[pltpu.with_memory_space_constraint(a, pltpu.HBM) for a in (tokens, *small)])
    inner_halo, other_halo = to_neighbours(inner_tokens, other_tokens)

    row_shape = shape(rows, own_len, width)
    normed, queries, keys, values, weight, angles, bounds = call(
        "project",
        project_kernel,
        [row_shape] * 4
        + [
            shape(*attention_in.shape),
            shape(2, own_len + 2 * win, LANES, kind=F32),
            shape(rows, 2, mid + 4 * win, kind=jnp.int32),
        ],
        tokens,
        document_starts,
        attention_in,
        gain_one,
        *tables,
        flops=3e9,
    )
    mid_attended, mid_probs = call(
        "attend_mid",
        attend_mid_kernel,
        [shape(rows, mid, width), shape(rows, groups, own_len, GROUP * mid, kind=F32)],
        queries,
        keys,
        values,
        bounds,
        flops=2e9,
    )

    def dense(name, outer, attended):
        count = attended.shape[1]
        return call(
            name,
            functools.partial(dense_kernel, outer),
            [
                shape(rows, count, width, kind=F32),
                shape(rows, count, width),
                shape(rows, count, hidden),
                shape(rows, count, 2 * hidden),
                shape(rows, count, width, kind=F32),
                shape(rows, count, width),
                shape(rows, count, width),
            ],
            tokens,
            result_grad,
            attended,
            attention_out,
            feedforward_in,
            feedforward_out,
            gain_two,
            flops=5e9,
            grant=14,
        )

    mid_middle, mid_normed, mid_mixed, mid_grad_up, mid_grad, mid_branch, mid_grad_attended = dense(
        "dense_mid", False, mid_attended
    )

    begun = call(
        "begin",
        functools.partial(weights_kernel, False),
        [shape(*w.shape) for w in (feedforward_in, feedforward_out, attention_out)],
        result_grad,
        mid_normed,
        mid_grad_up,
        mid_mixed,
        mid_attended,
        mid_branch,
        flops=3e9,
    )

    halo_normed, halo_keys, halo_values = call(
        "halo",
        halo_kernel,
        [shape(rows, 2 * win, width)] * 3,
        inner_halo,
        other_halo,
        weight,
        gain_one,
        angles,
        flops=1e9,
        after=[begun[2]],
    )
    out_attended, out_probs = call(
        "attend_out",
        attend_out_kernel,
        [shape(rows, 2 * win, width), shape(rows, 2, groups, 3 * win, GROUP * win, kind=F32)],
        queries,
        keys,
        values,
        halo_keys,
        halo_values,
        bounds,
        flops=2e9,
    )
    out_middle, out_normed, out_mixed, out_grad_up, out_grad, out_branch, out_grad_attended = dense(
        "dense_out", True, out_attended
    )

    piece = (feedforward_in.shape[1] // width * width + width + hidden) // BLOCKS
    keep_one, send_one = call(
        "weights",
        functools.partial(weights_kernel, True),
        [shape(BLOCKS // 2, piece, width)] * 2,
        result_grad,
        out_normed,
        out_grad_up,
        out_mixed,
        out_attended,
        out_branch,
        *begun,
        flops=5e9,
        scratch=[
            pltpu.VMEM(feedforward_in.shape, BF16),
            pltpu.VMEM(feedforward_out.shape, F32),
            pltpu.VMEM(attention_out.shape, BF16),
        ],
    )

    def cut(blocks, parts):
        return [shape(blocks.shape[0] // parts, *blocks.shape[1:])] * parts

    activations, done_result = call(
        "result",
        result_kernel,
        [row_shape],
        mid_middle,
        out_middle,
        mid_mixed,
        out_mixed,
        feedforward_out,
        flops=2e9,
        after=[keep_one],
        token=True,
    )
    chip_one = add_up([keep_one, swap(send_one, core=1)], cut(keep_one, 4), after=[done_result])
    from_plane = swap_plane(chip_one)
    grad_shapes = [shape(rows, own_len, 3 * WIDE), shape(rows, 2 * win, 2 * WIDE)] * groups
    *grads, inner_grad, other_grad = call(
        "backward",
        backward_kernel,
        [shape(rows, own_len, 3 * WIDE), shape(rows, 2 * win, 2 * WIDE)] * groups + [shape(rows, win, width)] * 2,
        queries,
        keys,
        values,
        halo_keys,
        halo_values,
        mid_grad_attended,
        out_grad_attended,
        mid_probs,
        out_probs,
        angles,
        weight,
        flops=12e9,
        after=[chip_one[0]],
    )
    inner_grad, other_grad = to_neighbours(inner_grad, other_grad)
    (total_in,) = call(
        "weight_in",
        weight_in_kernel,
        [shape(*attention_in.shape)],
        normed,
        halo_normed,
        *grads,
        flops=4e9,
    )
    plane_one = add_up([chip_one[0], *from_plane], cut(chip_one[0], 2), after=[total_in])
    keep_two, send_two = call(
        "split",
        split_kernel,
        [shape(BLOCKS // 2, attention_in.shape[1] // BLOCKS, width)] * 2,
        total_in,
        flops=1e9,
        after=[plane_one[0]],
    )
    chip_two = add_up([keep_two, swap(send_two, core=1)], cut(keep_two, 4))
    near_one = add_up([plane_one[0], swap(plane_one[1], z=1)], cut(plane_one[0], 2), after=[chip_two[0]])
    from_plane = swap_plane(chip_two)
    own_grad, done_own = call(
        "grad_own",
        grad_own_kernel,
        [shape(rows, own_len, width, kind=F32)],
        weight,
        *grads[::2],
        flops=2e9,
        after=[near_one[0]],
        token=True,
    )
    (line_one,) = add_up([near_one[0], swap(near_one[1], z=2)], cut(near_one[0], 1), after=[done_own])
    line_one = swap_rest(line_one)
    plane_two = add_up([chip_two[0], *from_plane], cut(chip_two[0], 2), after=[line_one, inner_grad])
    line_one = join([line_one, swap(line_one, z=2)], after=[plane_two[0]])
    near_two = add_up([plane_two[0], swap(plane_two[1], z=1)], cut(plane_two[0], 2), after=[line_one])
    line_one = join([line_one, swap(line_one, z=1)], after=[near_two[0]])
    from_plane = swap_plane([line_one] * 4)
    (line_two,) = add_up([near_two[0], swap(near_two[1], z=2)], cut(near_two[0], 1), after=[line_one])
    line_two = swap_rest(line_two)
    line_two = join([line_two, swap(line_two, z=2)])
    line_two = join([line_two, swap(line_two, z=1)], after=[other_grad])
    from_plane_two = swap_plane([line_two] * 4)
    whole_one = join([line_one, *from_plane], after=[line_two])
    grad_tokens, done_finish = call(
        "finish",
        finish_kernel,
        [shape(rows, own_len, width, kind=F32)],
        tokens,
        own_grad,
        inner_grad,
        other_grad,
        mid_grad,
        out_grad,
        gain_one,
        flops=1e8,
        after=[whole_one],
        token=True,
    )

    def placed(parts, gain, *weights):
        outs = [shape(*w.shape, kind=F32) for w in weights] + [shape(1, width, kind=F32)]
        return call("place", place_kernel, outs, *parts, weights[0], gain, flops=1e6)

    grad_up, grad_out, grad_down, grad_gain_two = placed(
        (whole_one, swap(whole_one, core=1)), gain_two, feedforward_in, attention_out, feedforward_out
    )
    whole_two = join([line_two, *from_plane_two], after=[grad_gain_two, done_finish])
    grad_in, grad_gain_one = placed((whole_two, swap(whole_two, core=1)), gain_one, attention_in)
    return activations, grad_tokens, grad_in, grad_out, grad_up, grad_down, grad_gain_one[0], grad_gain_two[0]


def solution(mesh):
    token, rest = P("dp", "seq", None), P()
    return jax.shard_map(
        shards,
        mesh=mesh,
        in_specs=(token, P("dp", None)) + (rest,) * 6 + (token,),
        out_specs=(token, token) + (rest,) * 6,
        check_vma=False,
    )
```

profile of v0, /device:TPU:0, one launch (start us, length us, event | category | flops | bytes accessed | tf_op | source)
XLA Modules:
  0.0 135.0 jit_solution(10714256652863777602)
XLA Ops:
  0.6 1.9 %load.1 = (bf16[6,64,512]{2,1,0:T(8,128)(2,1)S(1)}, bf16[6,64,512]{2,1,0:T(8,128)(2,1)S(1)}, s32[6,16]{1,0:T(8,128)S(1)}, f32[1,512]{1,0:T(1,128)S(1)}, bf16[512...) custom-call(bf16[6,256,512]{2,1,0:T(8,128)(2,1)} %refs_1_.5, s32[6,16]{1,0:T(8,128)} %refs_0_.6, ...), custom_call_target="tpu_custom_call" | custom-call | tf_op jit(solution)/shard_map/load/pallas_call | solution.py:722
  2.6 3.0 %collective-permute-start = (bf16[6,64,512]{2,1,0:T(8,128)(2,1)S(1)}, bf16[6,64,512]{2,1,0:T(8,128)(2,1)S(1)}, u32[]{:S(2)}, u32[]{:S(2)}) collective-permute-start(bf16[6,64,512]{2,1,0:T(8,128)(2,1)S(1)} %get-tuple-element.99), channel_id=1, source_target_pairs={{0,1},{1,0},{2,3},{3,2},{4,5},{5,4},{6,7},{7,6},{8,9},{9,8},{10,11... | collective-permute-start | bytes 1179656 | tf_op jit(solution)/shard_map/ppermute | solution.py:625
  5.6 0.7 collective-permute-start.1
  6.3 3.7 %project.1 = (bf16[6,256,512]{2,1,0:T(8,128)(2,1)S(1)}, bf16[6,256,512]{2,1,0:T(8,128)(2,1)S(1)}, bf16[6,256,512]{2,1,0:T(8,128)(2,1)S(1)}, bf16[6,256,512]{2,1,...) custom-call(bf16[6,256,512]{2,1,0:T(8,128)(2,1)S(1)} %copy-done, ...), custom_call_target="tpu_custom_call" | custom-call | flops 30000000 | bytes 118255 | tf_op jit(solution)/shard_map/project/pallas_call | solution.py:659
  10.1 3.2 %attend_mid.1 = (bf16[6,128,512]{2,1,0:T(8,128)(2,1)S(1)}, f32[6,2,256,512]{3,2,1,0:T(8,128)S(1)}) custom-call(bf16[6,256,512]{2,1,0:T(8,128)(2,1)S(1)} %get-tuple-element.89.refs_0_.refs_1_, bf16[6,256,512]{2,1,0:T(8,128)(2,1)S(1)} %get-tuple-element.90.refs_1_.refs_2_, bf16[6,256,512]{2,1,0:T(8,128)(2,1)S(1)} %get-tuple-element.91.refs_2_.refs_3_, ...), custom_call_target="tpu_custom_call" | custom-call | flops 20000000 | bytes 118149 | tf_op jit(solution)/shard_map/attend_mid/pallas_call | solution.py:659
  13.3 6.6 %dense_mid.1 = (f32[6,128,512]{2,1,0:T(8,128)S(1)}, bf16[6,128,512]{2,1,0:T(8,128)(2,1)S(1)}, bf16[6,128,768]{2,1,0:T(8,128)(2,1)S(1)}, bf16[6,128,1536]{2,1,0:T...) custom-call(bf16[6,256,512]{2,1,0:T(8,128)(2,1)S(1)} %copy-done, ...), custom_call_target="tpu_custom_call" | custom-call | flops 50000000 | bytes 158617 | tf_op jit(solution)/shard_map/dense_mid/pallas_call | solution.py:659
  19.9 2.4 %begin.1 = (bf16[512,1536]{1,0:T(8,128)(2,1)S(1)}, bf16[768,512]{1,0:T(8,128)(2,1)S(1)}, bf16[512,512]{1,0:T(8,128)(2,1)S(1)}) custom-call(bf16[6,256,512]{2,1,0:T(8,128)(2,1)S(1)} %copy-done.1, bf16[6,128,512]{2,1,0:T(8,128)(2,1)S(1)} %get-tuple-element.94.refs_1_, bf16[6,128,1536]{2,1,0:T(8,128)(2,1)S(1)} %get-tuple-element.95.refs_2_, ...), custom_call_target="tpu_custom_call" | custom-call | flops 30000000 | bytes 103546 | tf_op jit(solution)/shard_map/begin/pallas_call | solution.py:659
  22.4 1.7 %halo.1 = (bf16[6,128,512]{2,1,0:T(8,128)(2,1)S(1)}, bf16[6,128,512]{2,1,0:T(8,128)(2,1)S(1)}, bf16[6,128,512]{2,1,0:T(8,128)(2,1)S(1)}) custom-call(bf16[512,512]{1,0:T(8,128)(2,1)S(1)} %get-tuple-element.98.refs_0_.refs_8_, bf16[6,64,512]{2,1,0:T(8,128)(2,1)S(1)} %collective-permute-done.refs_1_, bf16[6,64,512]{2,1,0:T(8,128)(2,1)S(1)} %collective-permute-done.1.refs_2_, ...), custom_call_target="tpu_custom_call" | custom-call | flops 10000000 | bytes 51138 | tf_op jit(solution)/shard_map/halo/pallas_call | solution.py:659
  24.1 2.9 %attend_out.1 = (bf16[6,128,512]{2,1,0:T(8,128)(2,1)S(1)}, f32[6,2,2,192,256]{4,3,2,1,0:T(8,128)S(1)}) custom-call(bf16[6,256,512]{2,1,0:T(8,128)(2,1)S(1)} %get-tuple-element.89.refs_0_.refs_1_, bf16[6,256,512]{2,1,0:T(8,128)(2,1)S(1)} %get-tuple-element.90.refs_1_.refs_2_, bf16[6,256,512]{2,1,0:T(8,128)(2,1)S(1)} %get-tuple-element.91.refs_2_.refs_3_, ...), custom_call_target="tpu_custom_call" | custom-call | flops 20000000 | bytes 118149 | tf_op jit(solution)/shard_map/attend_out/pallas_call | solution.py:659
  27.0 6.7 %dense_out.1 = (f32[6,128,512]{2,1,0:T(8,128)S(1)}, bf16[6,128,512]{2,1,0:T(8,128)(2,1)S(1)}, bf16[6,128,768]{2,1,0:T(8,128)(2,1)S(1)}, bf16[6,128,1536]{2,1,0:T...) custom-call(bf16[6,256,512]{2,1,0:T(8,128)(2,1)S(1)} %copy-done, ...), custom_call_target="tpu_custom_call" | custom-call | flops 50000000 | bytes 158617 | tf_op jit(solution)/shard_map/dense_out/pallas_call | solution.py:659
  33.7 2.8 %weights.1 = (bf16[16,88,512]{2,1,0:T(8,128)(2,1)S(1)}, bf16[16,88,512]{2,1,0:T(8,128)(2,1)S(1)}) custom-call(bf16[6,256,512]{2,1,0:T(8,128)(2,1)S(1)} %copy-done.1, bf16[6,128,512]{2,1,0:T(8,128)(2,1)S(1)} %get-tuple-element.106.refs_1_, bf16[6,128,1536]{2,1,0:T(8,128)(2,1)S(1)} %get-tuple-element.107.refs_2_, ...), custom_call_target="tpu_custom_call" | custom-call | flops 50000000 | bytes 132382 | tf_op jit(solution)/shard_map/weights/pallas_call | solution.py:659
  36.6 2.7 %result.1 = (bf16[6,256,512]{2,1,0:T(8,128)(2,1)}, f32[8,128]{1,0:T(8,128)S(1)}) custom-call(bf16[16,88,512]{2,1,0:T(8,128)(2,1)S(1)} %get-tuple-element.112.refs_0_.refs_1_, f32[6,128,512]{2,1,0:T(8,128)S(1)} %get-tuple-element.113.refs_1_, f32[6,128,512]{2,1,0:T(8,128)S(1)} %get-tuple-element.114.refs_2_, ...), custom_call_target="tpu_custom_call" | custom-call | flops 20000000 | bytes 78684 | tf_op jit(solution)/shard_map/result/pallas_call | solution.py:659
  40.1 4.3 %collective-permute-start.4 = (bf16[4,88,512]{2,1,0:T(8,128)(2,1)S(1)}, bf16[4,88,512]{2,1,0:T(8,128)(2,1)S(1)}, u32[]{:S(2)}, u32[]{:S(2)}) collective-permute-start(bf16[4,88,512]{2,1,0:T(8,128)(2,1)S(1)} %get-tuple-element.130), channel_id=1, source_target_pairs={{0,1},{1,0},{2,3},{3,2},{4,5},{5,4},{6,7},{7,6},{8,9},{9,8},{10,11... | collective-permute-start | bytes 1081352 | tf_op jit(solution)/shard_map/ppermute | solution.py:639
  44.5 1.5 %collective-permute-start.5 = (bf16[4,88,512]{2,1,0:T(8,128)(2,1)S(1)}, bf16[4,88,512]{2,1,0:T(8,128)(2,1)S(1)}, u32[]{:S(2)}, u32[]{:S(2)}) collective-permute-start(bf16[4,88,512]{2,1,0:T(8,128)(2,1)S(1)} %get-tuple-element.131), channel_id=1, source_target_pairs={{0,16},{1,17},{2,18},{3,19},{4,20},{5,21},{6,22},{7,23},{8,24},{9,... | collective-permute-start | bytes 1081352 | tf_op jit(solution)/shard_map/ppermute | solution.py:639
  46.0 13.6 %backward.1 = (bf16[6,256,768]{2,1,0:T(8,128)(2,1)S(1)}, bf16[6,128,512]{2,1,0:T(8,128)(2,1)S(1)}, bf16[6,256,768]{2,1,0:T(8,128)(2,1)S(1)}, bf16[6,128,512]{2,1...) custom-call(bf16[4,88,512]{2,1,0:T(8,128)(2,1)S(1)} %get-tuple-element.118.refs_0_.refs_1_, ...), custom_call_target="tpu_custom_call" | custom-call | flops 120000000 | bytes 279183 | tf_op jit(solution)/shard_map/backward/pallas_call | solution.py:659
  59.6 3.7 %weight_in.1.refs_0_.refs_1_ = bf16[512,1536]{1,0:T(8,128)(2,1)S(1)} custom-call(bf16[6,256,512]{2,1,0:T(8,128)(2,1)S(1)} %get-tuple-element.124.refs_0_, bf16[6,128,512]{2,1,0:T(8,128)(2,1)S(1)} %get-tuple-element.125.refs_1_, bf16[6,256,768]{2,1,0:T(8,128)(2,1)S(1)} %get-tuple-element.126.refs_2_, bf16[6,128,512]{2,1,0:T(8,128)(2,1)S(1)} %get-tuple-element.127.refs_3_, ...), custom_call_target="tpu_custom_call" | custom-call | flops 40000000 | bytes 102236 | tf_op jit(solution)/shard_map/weight_in/pallas_call | solution.py:659
  63.9 2.0 %collective-permute-start.10 = (bf16[6,64,512]{2,1,0:T(8,128)(2,1)S(1)}, bf16[6,64,512]{2,1,0:T(8,128)(2,1)S(1)}, u32[]{:S(2)}, u32[]{:S(2)}) collective-permute-start(bf16[6,64,512]{2,1,0:T(8,128)(2,1)S(1)} %get-tuple-element.141), channel_id=1, source_target_pairs={{0,1},{1,0},{2,3},{3,2},{4,5},{5,4},{6,7},{7,6},{8,9},{9,8},{10,11... | collective-permute-start | bytes 1179656 | tf_op jit(solution)/shard_map/ppermute | solution.py:625
  66.0 1.6 %collective-permute-start.8 = (bf16[2,88,512]{2,1,0:T(8,128)(2,1)S(1)}, bf16[2,88,512]{2,1,0:T(8,128)(2,1)S(1)}, u32[]{:S(2)}, u32[]{:S(2)}) collective-permute-start(bf16[2,88,512]{2,1,0:T(8,128)(2,1)S(1)} %get-tuple-element.137), channel_id=1, source_target_pairs={{0,2},{1,3},{2,0},{3,1},{4,6},{5,7},{6,4},{7,5},{8,10},{9,11},{10,... | collective-permute-start | bytes 540680 | tf_op jit(solution)/shard_map/ppermute | solution.py:639
  67.7 0.7 collective-permute-start.11
  68.4 1.5 %collective-permute-start.12 = (bf16[4,48,512]{2,1,0:T(8,128)(2,1)S(1)}, bf16[4,48,512]{2,1,0:T(8,128)(2,1)S(1)}, u32[]{:S(2)}, u32[]{:S(2)}) collective-permute-start(bf16[4,48,512]{2,1,0:T(8,128)(2,1)S(1)} %get-tuple-element.143), channel_id=1, source_target_pairs={{0,16},{1,17},{2,18},{3,19},{4,20},{5,21},{6,22},{7,23},{8,24},{9,... | collective-permute-start | bytes 589832 | tf_op jit(solution)/shard_map/ppermute | solution.py:639
  69.9 1.4 %collective-permute-start.13 = (bf16[4,48,512]{2,1,0:T(8,128)(2,1)S(1)}, bf16[4,48,512]{2,1,0:T(8,128)(2,1)S(1)}, u32[]{:S(2)}, u32[]{:S(2)}) collective-permute-start(bf16[4,48,512]{2,1,0:T(8,128)(2,1)S(1)} %get-tuple-element.144), channel_id=1, source_target_pairs={{0,17},{1,16},{2,19},{3,18},{4,21},{5,20},{6,23},{7,22},{8,25},{9,... | collective-permute-start | bytes 589832 | tf_op jit(solution)/shard_map/ppermute | solution.py:639
  71.3 1.3 collective-permute-done.8.refs_2_
  72.6 2.6 %collective-permute-start.9 = (bf16[1,88,512]{2,1,0:T(8,128)(2,1)S(1)}, bf16[1,88,512]{2,1,0:T(8,128)(2,1)S(1)}, u32[]{:S(2)}, u32[]{:S(2)}) collective-permute-start(bf16[1,88,512]{2,1,0:T(8,128)(2,1)S(1)} %get-tuple-element.140), channel_id=1, source_target_pairs={{0,4},{1,5},{2,6},{3,7},{4,0},{5,1},{6,2},{7,3},{8,12},{9,13},{10,... | collective-permute-start | bytes 270344 | tf_op jit(solution)/shard_map/ppermute | solution.py:639
  75.3 3.0 %grad_own.1 = (f32[6,256,512]{2,1,0:T(8,128)S(1)}, f32[8,128]{1,0:T(8,128)S(1)}) custom-call(bf16[1,88,512]{2,1,0:T(8,128)(2,1)S(1)} %get-tuple-element.138.refs_0_.refs_1_, bf16[512,1536]{1,0:T(8,128)(2,1)S(1)} %get-tuple-element.101.refs_3_.refs_11_.refs_1_, bf16[6,256,768]{2,1,0:T(8,128)(2,1)S(1)} %get-tuple-element.126.refs_2_, ...), custom_call_target="tpu_custom_call" | custom-call | flops 20000000 | bytes 94412 | tf_op jit(solution)/shard_map/grad_own/pallas_call | solution.py:659
  78.3 1.1 collective-permute-done.9.refs_2_
  79.5 1.4 %collective-permute-start.14 = (bf16[1,88,512]{2,1,0:T(8,128)(2,1)S(1)}, bf16[1,88,512]{2,1,0:T(8,128)(2,1)S(1)}, u32[]{:S(2)}, u32[]{:S(2)}) collective-permute-start(bf16[1,88,512]{2,1,0:T(8,128)(2,1)S(1)} %add.12.refs_0_.refs_1_), channel_id=1, source_target_pairs={{0,4},{1,5},{2,6},{3,7},{4,0},{5,1},{6,2},{7,3},{8,12},{9,13},{10,... | collective-permute-start | bytes 270344 | tf_op jit(solution)/shard_map/ppermute | solution.py:639
  80.9 3.2 %collective-permute-done.11.refs_3_ = bf16[4,48,512]{2,1,0:T(8,128)(2,1)S(1)} collective-permute-done((bf16[4,48,512]{2,1,0:T(8,128)(2,1)S(1)}, bf16[4,48,512]{2,1,0:T(8,128)(2,1)S(1)}, u32[]{:S(2)}, u32[]{:S(2)}) %collective-permute-start.11) | collective-permute-done | bytes 196640 | tf_op jit(solution)/shard_map/ppermute | solution.py:639
  84.2 1.5 %collective-permute-done.14.refs_2_ = bf16[1,88,512]{2,1,0:T(8,128)(2,1)S(1)} collective-permute-done((bf16[1,88,512]{2,1,0:T(8,128)(2,1)S(1)}, bf16[1,88,512]{2,1,0:T(8,128)(2,1)S(1)}, u32[]{:S(2)}, u32[]{:S(2)}) %collective-permute-start.14) | collective-permute-done | bytes 90144 | tf_op jit(solution)/shard_map/ppermute | solution.py:639
  85.9 1.9 %collective-permute-start.15 = (bf16[2,48,512]{2,1,0:T(8,128)(2,1)S(1)}, bf16[2,48,512]{2,1,0:T(8,128)(2,1)S(1)}, u32[]{:S(2)}, u32[]{:S(2)}) collective-permute-start(bf16[2,48,512]{2,1,0:T(8,128)(2,1)S(1)} %get-tuple-element.146), channel_id=1, source_target_pairs={{0,2},{1,3},{2,0},{3,1},{4,6},{5,7},{6,4},{7,5},{8,10},{9,11},{10,... | collective-permute-start | bytes 294920 | tf_op jit(solution)/shard_map/ppermute | solution.py:639
  87.8 0.9 collective-permute-start.3
  88.8 5.4 %collective-permute-done.15.refs_2_ = bf16[2,48,512]{2,1,0:T(8,128)(2,1)S(1)} collective-permute-done((bf16[2,48,512]{2,1,0:T(8,128)(2,1)S(1)}, bf16[2,48,512]{2,1,0:T(8,128)(2,1)S(1)}, u32[]{:S(2)}, u32[]{:S(2)}) %collective-permute-start.15) | collective-permute-done | bytes 98336 | tf_op jit(solution)/shard_map/ppermute | solution.py:639
  94.2 1.6 %collective-permute-start.22 = (bf16[4,88,512]{2,1,0:T(8,128)(2,1)S(1)}, bf16[4,88,512]{2,1,0:T(8,128)(2,1)S(1)}, u32[]{:S(2)}, u32[]{:S(2)}) collective-permute-start(bf16[4,88,512]{2,1,0:T(8,128)(2,1)S(1)} %join.7.refs_0_.refs_1_), channel_id=1, source_target_pairs={{0,17},{1,16},{2,19},{3,18},{4,21},{5,20},{6,23},{7,22},{8,25},{9,... | collective-permute-start | bytes 1081352 | tf_op jit(solution)/shard_map/ppermute | solution.py:639
  95.8 0.6 collective-permute-start.21
  96.3 1.4 %collective-permute-start.20 = (bf16[4,88,512]{2,1,0:T(8,128)(2,1)S(1)}, bf16[4,88,512]{2,1,0:T(8,128)(2,1)S(1)}, u32[]{:S(2)}, u32[]{:S(2)}) collective-permute-start(bf16[4,88,512]{2,1,0:T(8,128)(2,1)S(1)} %join.7.refs_0_.refs_1_), channel_id=1, source_target_pairs={{0,1},{1,0},{2,3},{3,2},{4,5},{5,4},{6,7},{7,6},{8,9},{9,8},{10,11... | collective-permute-start | bytes 1081352 | tf_op jit(solution)/shard_map/ppermute | solution.py:639
  97.8 2.3 %collective-permute-start.17 = (bf16[1,48,512]{2,1,0:T(8,128)(2,1)S(1)}, bf16[1,48,512]{2,1,0:T(8,128)(2,1)S(1)}, u32[]{:S(2)}, u32[]{:S(2)}) collective-permute-start(bf16[1,48,512]{2,1,0:T(8,128)(2,1)S(1)} %get-tuple-element.148), channel_id=1, source_target_pairs={{0,4},{1,5},{2,6},{3,7},{4,0},{5,1},{6,2},{7,3},{8,12},{9,13},{10,... | collective-permute-start | bytes 147464 | tf_op jit(solution)/shard_map/ppermute | solution.py:639
  100.0 4.5 %collective-permute-done.17.refs_2_ = bf16[1,48,512]{2,1,0:T(8,128)(2,1)S(1)} collective-permute-done((bf16[1,48,512]{2,1,0:T(8,128)(2,1)S(1)}, bf16[1,48,512]{2,1,0:T(8,128)(2,1)S(1)}, u32[]{:S(2)}, u32[]{:S(2)}) %collective-permute-start.17) | collective-permute-done | bytes 49184 | tf_op jit(solution)/shard_map/ppermute | solution.py:639
  104.6 0.5 collective-permute-start.18
  105.1 4.5 %collective-permute-done.18.refs_1_ = bf16[1,48,512]{2,1,0:T(8,128)(2,1)S(1)} collective-permute-done((bf16[1,48,512]{2,1,0:T(8,128)(2,1)S(1)}, bf16[1,48,512]{2,1,0:T(8,128)(2,1)S(1)}, u32[]{:S(2)}, u32[]{:S(2)}) %collective-permute-start.18) | collective-permute-done | bytes 49184 | tf_op jit(solution)/shard_map/ppermute | solution.py:639
  109.6 5.1 %collective-permute-start.19 = (bf16[2,48,512]{2,1,0:T(8,128)(2,1)S(1)}, bf16[2,48,512]{2,1,0:T(8,128)(2,1)S(1)}, u32[]{:S(2)}, u32[]{:S(2)}) collective-permute-start(bf16[2,48,512]{2,1,0:T(8,128)(2,1)S(1)} %join.8.refs_1_), channel_id=1, source_target_pairs={{0,2},{1,3},{2,0},{3,1},{4,6},{5,7},{6,4},{7,5},{8,10},{9,11},{10,... | collective-permute-start | bytes 294920 | tf_op jit(solution)/shard_map/ppermute | solution.py:639
  114.7 2.6 %collective-permute-done.19.refs_2_ = bf16[2,48,512]{2,1,0:T(8,128)(2,1)S(1)} collective-permute-done((bf16[2,48,512]{2,1,0:T(8,128)(2,1)S(1)}, bf16[2,48,512]{2,1,0:T(8,128)(2,1)S(1)}, u32[]{:S(2)}, u32[]{:S(2)}) %collective-permute-start.19) | collective-permute-done | bytes 98336 | tf_op jit(solution)/shard_map/ppermute | solution.py:639
  117.5 2.4 %collective-permute-start.26 = (bf16[4,48,512]{2,1,0:T(8,128)(2,1)S(1)}, bf16[4,48,512]{2,1,0:T(8,128)(2,1)S(1)}, u32[]{:S(2)}, u32[]{:S(2)}) collective-permute-start(bf16[4,48,512]{2,1,0:T(8,128)(2,1)S(1)} %join.9.refs_0_.refs_2_), channel_id=1, source_target_pairs={{0,17},{1,16},{2,19},{3,18},{4,21},{5,20},{6,23},{7,22},{8,25},{9,... | collective-permute-start | bytes 589832 | tf_op jit(solution)/shard_map/ppermute | solution.py:639
  120.5 0.6 collective-permute-start.24
  121.1 3.9 %finish.1 = (f32[6,256,512]{2,1,0:T(8,128)}, f32[8,128]{1,0:T(8,128)S(1)}) custom-call(bf16[16,88,512]{2,1,0:T(8,128)(2,1)S(1)} %join.10.refs_0_, bf16[6,256,512]{2,1,0:T(8,128)(2,1)S(1)} %copy-done, f32[6,256,512]{2,1,0:T(8,128)S(1)} %get-tuple-element.149.refs_2_, bf16[6,64,512]{2,1,0:T(8,128)(2,1)S(1)} %collective-permute-done.10.refs_1_.refs_3_, ...), custom_call_target="tpu_custom_call" | custom-call | flops 1000000 | bytes 118026 | tf_op jit(solution)/shard_map/finish/pallas_call | solution.py:659
  125.0 3.0 %place.2 = (f32[512,1536]{1,0:T(8,128)}, f32[512,512]{1,0:T(8,128)}, f32[768,512]{1,0:T(8,128)}, f32[1,512]{1,0:T(1,128)}) custom-call(bf16[16,88,512]{2,1,0:T(8,128)(2,1)S(1)} %join.10.refs_0_, bf16[16,88,512]{2,1,0:T(8,128)(2,1)S(1)} %collective-permute-done.23.refs_1_, bf16[512,1536]{1,0:T(8,128)(2,1)S(1)} %copy-done.2, f32[1,512]{1,0:T(1,128)S(1)} %bitcast.6), custom_call_target="tpu_custom_call" | custom-call | flops 10000 | bytes 102277 | tf_op jit(solution)/shard_map/place/pallas_call | solution.py:659
  128.0 2.0 %collective-permute-done.25.refs_4_ = bf16[4,48,512]{2,1,0:T(8,128)(2,1)S(1)} collective-permute-done((bf16[4,48,512]{2,1,0:T(8,128)(2,1)S(1)}, bf16[4,48,512]{2,1,0:T(8,128)(2,1)S(1)}, u32[]{:S(2)}, u32[]{:S(2)}) %collective-permute-start.25) | collective-permute-done | bytes 196640 | tf_op jit(solution)/shard_map/ppermute | solution.py:639
  130.0 0.7 copy-done.6
  130.8 2.3 %collective-permute-done.27.refs_1_ = bf16[16,48,512]{2,1,0:T(8,128)(2,1)S(1)} collective-permute-done((bf16[16,48,512]{2,1,0:T(8,128)(2,1)S(1)}, bf16[16,48,512]{2,1,0:T(8,128)(2,1)S(1)}, u32[]{:S(2)}, u32[]{:S(2)}) %collective-permute-start.27) | collective-permute-done | bytes 786464 | tf_op jit(solution)/shard_map/ppermute | solution.py:639
  133.1 2.0 %place.3 = (f32[512,1536]{1,0:T(8,128)}, f32[1,512]{1,0:T(1,128)}) custom-call(bf16[16,48,512]{2,1,0:T(8,128)(2,1)S(1)} %join.11.refs_0_, bf16[16,48,512]{2,1,0:T(8,128)(2,1)S(1)} %collective-permute-done.27.refs_1_, bf16[512,1536]{1,0:T(8,128)(2,1)S(1)} %get-tuple-element.85.refs_2_, f32[1,512]{1,0:T(1,128)S(1)} %get-tuple-element.86.refs_3_.refs_4_.refs_7_), custom_call_target="tpu_custom_call" | custom-call | flops 10000 | bytes 62955 | tf_op jit(solution)/shard_map/place/pallas_call | solution.py:659
  (53 shorter events, 3.0 us)
Async XLA Ops:
  0.6 5.7 %copy-start = (bf16[6,256,512]{2,1,0:T(8,128)(2,1)S(1)}, bf16[6,256,512]{2,1,0:T(8,128)(2,1)}, u32[]{:S(2)}) copy-start(bf16[6,256,512]{2,1,0:T(8,128)(2,1)} %refs_1_.5) | copy-start | bytes 4718596
  2.6 19.8 %collective-permute-start = (bf16[6,64,512]{2,1,0:T(8,128)(2,1)S(1)}, bf16[6,64,512]{2,1,0:T(8,128)(2,1)S(1)}, u32[]{:S(2)}, u32[]{:S(2)}) collective-permute-start(bf16[6,64,512]{2,1,0:T(8,128)(2,1)S(1)} %get-tuple-element.99), channel_id=1, source_target_pairs={{0,1},{1,0},{2,3},{3,2},{4,5},{5,4},{6,7},{7,6},{8,9},{9,8},{10,11... | collective-permute-start | bytes 1179656 | tf_op jit(solution)/shard_map/ppermute | solution.py:625
  5.6 16.8 %collective-permute-start.1 = (bf16[6,64,512]{2,1,0:T(8,128)(2,1)S(1)}, bf16[6,64,512]{2,1,0:T(8,128)(2,1)S(1)}, u32[]{:S(2)}, u32[]{:S(2)}) collective-permute-start(bf16[6,64,512]{2,1,0:T(8,128)(2,1)S(1)} %get-tuple-element.100), channel_id=1, source_target_pairs={{1,2},{2,1},{3,4},{4,3},{5,6},{6,5},{9,10},{10,9},{11,12},{12,11},... | collective-permute-start | bytes 1179656 | tf_op jit(solution)/shard_map/ppermute | solution.py:625
  10.1 3.2 %copy-start.1 = (bf16[6,256,512]{2,1,0:T(8,128)(2,1)S(1)}, bf16[6,256,512]{2,1,0:T(8,128)(2,1)}, u32[]{:S(2)}) copy-start(bf16[6,256,512]{2,1,0:T(8,128)(2,1)} %refs_0_.11) | copy-start | bytes 4718596
  10.1 3.2 %copy-start.2 = (bf16[512,1536]{1,0:T(8,128)(2,1)S(1)}, bf16[512,1536]{1,0:T(8,128)(2,1)}, u32[]{:S(2)}) copy-start(bf16[512,1536]{1,0:T(8,128)(2,1)} %refs_2_.3) | copy-start | bytes 4718596
  10.1 3.2 %copy-start.3 = (bf16[768,512]{1,0:T(8,128)(2,1)S(1)}, bf16[768,512]{1,0:T(8,128)(2,1)}, u32[]{:S(2)}) copy-start(bf16[768,512]{1,0:T(8,128)(2,1)} %refs_5_.5) | copy-start | bytes 2359300
  10.1 3.2 %copy-start.4 = (bf16[512,512]{1,0:T(8,128)(2,1)S(1)}, bf16[512,512]{1,0:T(8,128)(2,1)}, u32[]{:S(2)}) copy-start(bf16[512,512]{1,0:T(8,128)(2,1)} %refs_3_.4) | copy-start | bytes 1572868
  10.1 3.2 %copy-start.5 = (f32[512]{0:T(512)S(1)}, f32[512]{0:T(512)}, u32[]{:S(2)}) copy-start(f32[512]{0:T(512)} %param.18) | copy-start | bytes 6148
  36.5 3.3 %collective-permute-start.2 = (bf16[16,88,512]{2,1,0:T(8,128)(2,1)S(1)}, bf16[16,88,512]{2,1,0:T(8,128)(2,1)S(1)}, u32[]{:S(2)}, u32[]{:S(2)}) collective-permute-start(bf16[16,88,512]{2,1,0:T(8,128)(2,1)S(1)} %get-tuple-element.117), channel_id=1, source_target_pairs={{0,8},{1,9},{2,10},{3,11},{4,12},{5,13},{6,14},{7,15},{8,0},{9,1},... | collective-permute-start | bytes 4325384 | tf_op jit(solution)/shard_map/ppermute | solution.py:639
  40.1 23.2 %collective-permute-start.4 = (bf16[4,88,512]{2,1,0:T(8,128)(2,1)S(1)}, bf16[4,88,512]{2,1,0:T(8,128)(2,1)S(1)}, u32[]{:S(2)}, u32[]{:S(2)}) collective-permute-start(bf16[4,88,512]{2,1,0:T(8,128)(2,1)S(1)} %get-tuple-element.130), channel_id=1, source_target_pairs={{0,1},{1,0},{2,3},{3,2},{4,5},{5,4},{6,7},{7,6},{8,9},{9,8},{10,11... | collective-permute-start | bytes 1081352 | tf_op jit(solution)/shard_map/ppermute | solution.py:639
  44.5 18.9 %collective-permute-start.5 = (bf16[4,88,512]{2,1,0:T(8,128)(2,1)S(1)}, bf16[4,88,512]{2,1,0:T(8,128)(2,1)S(1)}, u32[]{:S(2)}, u32[]{:S(2)}) collective-permute-start(bf16[4,88,512]{2,1,0:T(8,128)(2,1)S(1)} %get-tuple-element.131), channel_id=1, source_target_pairs={{0,16},{1,17},{2,18},{3,19},{4,20},{5,21},{6,22},{7,23},{8,24},{9,... | collective-permute-start | bytes 1081352 | tf_op jit(solution)/shard_map/ppermute | solution.py:639
  45.9 17.5 %collective-permute-start.6 = (bf16[4,88,512]{2,1,0:T(8,128)(2,1)S(1)}, bf16[4,88,512]{2,1,0:T(8,128)(2,1)S(1)}, u32[]{:S(2)}, u32[]{:S(2)}) collective-permute-start(bf16[4,88,512]{2,1,0:T(8,128)(2,1)S(1)} %get-tuple-element.132), channel_id=1, source_target_pairs={{0,17},{1,16},{2,19},{3,18},{4,21},{5,20},{6,23},{7,22},{8,25},{9,... | collective-permute-start | bytes 1081352 | tf_op jit(solution)/shard_map/ppermute | solution.py:639
  63.9 3.7 %collective-permute-start.7 = (bf16[16,48,512]{2,1,0:T(8,128)(2,1)S(1)}, bf16[16,48,512]{2,1,0:T(8,128)(2,1)S(1)}, u32[]{:S(2)}, u32[]{:S(2)}) collective-permute-start(bf16[16,48,512]{2,1,0:T(8,128)(2,1)S(1)} %get-tuple-element.135), channel_id=1, source_target_pairs={{0,8},{1,9},{2,10},{3,11},{4,12},{5,13},{6,14},{7,15},{8,0},{9,1},... | collective-permute-start | bytes 2359304 | tf_op jit(solution)/shard_map/ppermute | solution.py:639
  63.9 16.9 %collective-permute-start.10 = (bf16[6,64,512]{2,1,0:T(8,128)(2,1)S(1)}, bf16[6,64,512]{2,1,0:T(8,128)(2,1)S(1)}, u32[]{:S(2)}, u32[]{:S(2)}) collective-permute-start(bf16[6,64,512]{2,1,0:T(8,128)(2,1)S(1)} %get-tuple-element.141), channel_id=1, source_target_pairs={{0,1},{1,0},{2,3},{3,2},{4,5},{5,4},{6,7},{7,6},{8,9},{9,8},{10,11... | collective-permute-start | bytes 1179656 | tf_op jit(solution)/shard_map/ppermute | solution.py:625
  66.0 6.6 %collective-permute-start.8 = (bf16[2,88,512]{2,1,0:T(8,128)(2,1)S(1)}, bf16[2,88,512]{2,1,0:T(8,128)(2,1)S(1)}, u32[]{:S(2)}, u32[]{:S(2)}) collective-permute-start(bf16[2,88,512]{2,1,0:T(8,128)(2,1)S(1)} %get-tuple-element.137), channel_id=1, source_target_pairs={{0,2},{1,3},{2,0},{3,1},{4,6},{5,7},{6,4},{7,5},{8,10},{9,11},{10,... | collective-permute-start | bytes 540680 | tf_op jit(solution)/shard_map/ppermute | solution.py:639
  67.7 16.4 %collective-permute-start.11 = (bf16[4,48,512]{2,1,0:T(8,128)(2,1)S(1)}, bf16[4,48,512]{2,1,0:T(8,128)(2,1)S(1)}, u32[]{:S(2)}, u32[]{:S(2)}) collective-permute-start(bf16[4,48,512]{2,1,0:T(8,128)(2,1)S(1)} %get-tuple-element.142), channel_id=1, source_target_pairs={{0,1},{1,0},{2,3},{3,2},{4,5},{5,4},{6,7},{7,6},{8,9},{9,8},{10,11... | collective-permute-start | bytes 589832 | tf_op jit(solution)/shard_map/ppermute | solution.py:639
  68.4 15.7 %collective-permute-start.12 = (bf16[4,48,512]{2,1,0:T(8,128)(2,1)S(1)}, bf16[4,48,512]{2,1,0:T(8,128)(2,1)S(1)}, u32[]{:S(2)}, u32[]{:S(2)}) collective-permute-start(bf16[4,48,512]{2,1,0:T(8,128)(2,1)S(1)} %get-tuple-element.143), channel_id=1, source_target_pairs={{0,16},{1,17},{2,18},{3,19},{4,20},{5,21},{6,22},{7,23},{8,24},{9,... | collective-permute-start | bytes 589832 | tf_op jit(solution)/shard_map/ppermute | solution.py:639
  69.9 14.2 %collective-permute-start.13 = (bf16[4,48,512]{2,1,0:T(8,128)(2,1)S(1)}, bf16[4,48,512]{2,1,0:T(8,128)(2,1)S(1)}, u32[]{:S(2)}, u32[]{:S(2)}) collective-permute-start(bf16[4,48,512]{2,1,0:T(8,128)(2,1)S(1)} %get-tuple-element.144), channel_id=1, source_target_pairs={{0,17},{1,16},{2,19},{3,18},{4,21},{5,20},{6,23},{7,22},{8,25},{9,... | collective-permute-start | bytes 589832 | tf_op jit(solution)/shard_map/ppermute | solution.py:639
  72.6 6.8 %collective-permute-start.9 = (bf16[1,88,512]{2,1,0:T(8,128)(2,1)S(1)}, bf16[1,88,512]{2,1,0:T(8,128)(2,1)S(1)}, u32[]{:S(2)}, u32[]{:S(2)}) collective-permute-start(bf16[1,88,512]{2,1,0:T(8,128)(2,1)S(1)} %get-tuple-element.140), channel_id=1, source_target_pairs={{0,4},{1,5},{2,6},{3,7},{4,0},{5,1},{6,2},{7,3},{8,12},{9,13},{10,... | collective-permute-start | bytes 270344 | tf_op jit(solution)/shard_map/ppermute | solution.py:639
  79.5 6.3 %collective-permute-start.14 = (bf16[1,88,512]{2,1,0:T(8,128)(2,1)S(1)}, bf16[1,88,512]{2,1,0:T(8,128)(2,1)S(1)}, u32[]{:S(2)}, u32[]{:S(2)}) collective-permute-start(bf16[1,88,512]{2,1,0:T(8,128)(2,1)S(1)} %add.12.refs_0_.refs_1_), channel_id=1, source_target_pairs={{0,4},{1,5},{2,6},{3,7},{4,0},{5,1},{6,2},{7,3},{8,12},{9,13},{10,... | collective-permute-start | bytes 270344 | tf_op jit(solution)/shard_map/ppermute | solution.py:639
  85.7 8.4 %collective-permute-start.16 = (bf16[2,88,512]{2,1,0:T(8,128)(2,1)S(1)}, bf16[2,88,512]{2,1,0:T(8,128)(2,1)S(1)}, u32[]{:S(2)}, u32[]{:S(2)}) collective-permute-start(bf16[2,88,512]{2,1,0:T(8,128)(2,1)S(1)} %join.6.refs_0_.refs_1_), channel_id=1, source_target_pairs={{0,2},{1,3},{2,0},{3,1},{4,6},{5,7},{6,4},{7,5},{8,10},{9,11},{10,... | collective-permute-start | bytes 540680 | tf_op jit(solution)/shard_map/ppermute | solution.py:639
  85.9 8.2 %collective-permute-start.15 = (bf16[2,48,512]{2,1,0:T(8,128)(2,1)S(1)}, bf16[2,48,512]{2,1,0:T(8,128)(2,1)S(1)}, u32[]{:S(2)}, u32[]{:S(2)}) collective-permute-start(bf16[2,48,512]{2,1,0:T(8,128)(2,1)S(1)} %get-tuple-element.146), channel_id=1, source_target_pairs={{0,2},{1,3},{2,0},{3,1},{4,6},{5,7},{6,4},{7,5},{8,10},{9,11},{10,... | collective-permute-start | bytes 294920 | tf_op jit(solution)/shard_map/ppermute | solution.py:639
  87.8 26.9 %collective-permute-start.3 = (bf16[6,64,512]{2,1,0:T(8,128)(2,1)S(1)}, bf16[6,64,512]{2,1,0:T(8,128)(2,1)S(1)}, u32[]{:S(2)}, u32[]{:S(2)}) collective-permute-start(bf16[6,64,512]{2,1,0:T(8,128)(2,1)S(1)} %get-tuple-element.123), channel_id=1, source_target_pairs={{1,2},{2,1},{3,4},{4,3},{5,6},{6,5},{9,10},{10,9},{11,12},{12,11},... | collective-permute-start | bytes 1179656 | tf_op jit(solution)/shard_map/ppermute | solution.py:625
  94.2 23.1 %collective-permute-start.22 = (bf16[4,88,512]{2,1,0:T(8,128)(2,1)S(1)}, bf16[4,88,512]{2,1,0:T(8,128)(2,1)S(1)}, u32[]{:S(2)}, u32[]{:S(2)}) collective-permute-start(bf16[4,88,512]{2,1,0:T(8,128)(2,1)S(1)} %join.7.refs_0_.refs_1_), channel_id=1, source_target_pairs={{0,17},{1,16},{2,19},{3,18},{4,21},{5,20},{6,23},{7,22},{8,25},{9,... | collective-permute-start | bytes 1081352 | tf_op jit(solution)/shard_map/ppermute | solution.py:639
  95.8 21.6 %collective-permute-start.21 = (bf16[4,88,512]{2,1,0:T(8,128)(2,1)S(1)}, bf16[4,88,512]{2,1,0:T(8,128)(2,1)S(1)}, u32[]{:S(2)}, u32[]{:S(2)}) collective-permute-start(bf16[4,88,512]{2,1,0:T(8,128)(2,1)S(1)} %join.7.refs_0_.refs_1_), channel_id=1, source_target_pairs={{0,16},{1,17},{2,18},{3,19},{4,20},{5,21},{6,22},{7,23},{8,24},{9,... | collective-permute-start | bytes 1081352 | tf_op jit(solution)/shard_map/ppermute | solution.py:639
  96.3 21.0 %collective-permute-start.20 = (bf16[4,88,512]{2,1,0:T(8,128)(2,1)S(1)}, bf16[4,88,512]{2,1,0:T(8,128)(2,1)S(1)}, u32[]{:S(2)}, u32[]{:S(2)}) collective-permute-start(bf16[4,88,512]{2,1,0:T(8,128)(2,1)S(1)} %join.7.refs_0_.refs_1_), channel_id=1, source_target_pairs={{0,1},{1,0},{2,3},{3,2},{4,5},{5,4},{6,7},{7,6},{8,9},{9,8},{10,11... | collective-permute-start | bytes 1081352 | tf_op jit(solution)/shard_map/ppermute | solution.py:639
  97.8 6.8 %collective-permute-start.17 = (bf16[1,48,512]{2,1,0:T(8,128)(2,1)S(1)}, bf16[1,48,512]{2,1,0:T(8,128)(2,1)S(1)}, u32[]{:S(2)}, u32[]{:S(2)}) collective-permute-start(bf16[1,48,512]{2,1,0:T(8,128)(2,1)S(1)} %get-tuple-element.148), channel_id=1, source_target_pairs={{0,4},{1,5},{2,6},{3,7},{4,0},{5,1},{6,2},{7,3},{8,12},{9,13},{10,... | collective-permute-start | bytes 147464 | tf_op jit(solution)/shard_map/ppermute | solution.py:639
  104.6 5.1 %collective-permute-start.18 = (bf16[1,48,512]{2,1,0:T(8,128)(2,1)S(1)}, bf16[1,48,512]{2,1,0:T(8,128)(2,1)S(1)}, u32[]{:S(2)}, u32[]{:S(2)}) collective-permute-start(bf16[1,48,512]{2,1,0:T(8,128)(2,1)S(1)} %add.15.refs_0_), channel_id=1, source_target_pairs={{0,4},{1,5},{2,6},{3,7},{4,0},{5,1},{6,2},{7,3},{8,12},{9,13},{10,... | collective-permute-start | bytes 147464 | tf_op jit(solution)/shard_map/ppermute | solution.py:639
  109.6 7.7 %collective-permute-start.19 = (bf16[2,48,512]{2,1,0:T(8,128)(2,1)S(1)}, bf16[2,48,512]{2,1,0:T(8,128)(2,1)S(1)}, u32[]{:S(2)}, u32[]{:S(2)}) collective-permute-start(bf16[2,48,512]{2,1,0:T(8,128)(2,1)S(1)} %join.8.refs_1_), channel_id=1, source_target_pairs={{0,2},{1,3},{2,0},{3,1},{4,6},{5,7},{6,4},{7,5},{8,10},{9,11},{10,... | collective-permute-start | bytes 294920 | tf_op jit(solution)/shard_map/ppermute | solution.py:639
  117.5 7.5 %collective-permute-start.23 = (bf16[16,88,512]{2,1,0:T(8,128)(2,1)S(1)}, bf16[16,88,512]{2,1,0:T(8,128)(2,1)S(1)}, u32[]{:S(2)}, u32[]{:S(2)}) collective-permute-start(bf16[16,88,512]{2,1,0:T(8,128)(2,1)S(1)} %join.10.refs_0_), channel_id=1, source_target_pairs={{0,8},{1,9},{2,10},{3,11},{4,12},{5,13},{6,14},{7,15},{8,0},{9,1},... | collective-permute-start | bytes 4325384 | tf_op jit(solution)/shard_map/ppermute | solution.py:639
  117.5 10.5 %collective-permute-start.26 = (bf16[4,48,512]{2,1,0:T(8,128)(2,1)S(1)}, bf16[4,48,512]{2,1,0:T(8,128)(2,1)S(1)}, u32[]{:S(2)}, u32[]{:S(2)}) collective-permute-start(bf16[4,48,512]{2,1,0:T(8,128)(2,1)S(1)} %join.9.refs_0_.refs_2_), channel_id=1, source_target_pairs={{0,17},{1,16},{2,19},{3,18},{4,21},{5,20},{6,23},{7,22},{8,25},{9,... | collective-permute-start | bytes 589832 | tf_op jit(solution)/shard_map/ppermute | solution.py:639
  119.9 10.0 %collective-permute-start.25 = (bf16[4,48,512]{2,1,0:T(8,128)(2,1)S(1)}, bf16[4,48,512]{2,1,0:T(8,128)(2,1)S(1)}, u32[]{:S(2)}, u32[]{:S(2)}) collective-permute-start(bf16[4,48,512]{2,1,0:T(8,128)(2,1)S(1)} %join.9.refs_0_.refs_2_), channel_id=1, source_target_pairs={{0,16},{1,17},{2,18},{3,19},{4,20},{5,21},{6,22},{7,23},{8,24},{9,... | collective-permute-start | bytes 589832 | tf_op jit(solution)/shard_map/ppermute | solution.py:639
  120.5 9.5 %collective-permute-start.24 = (bf16[4,48,512]{2,1,0:T(8,128)(2,1)S(1)}, bf16[4,48,512]{2,1,0:T(8,128)(2,1)S(1)}, u32[]{:S(2)}, u32[]{:S(2)}) collective-permute-start(bf16[4,48,512]{2,1,0:T(8,128)(2,1)S(1)} %join.9.refs_0_.refs_2_), channel_id=1, source_target_pairs={{0,1},{1,0},{2,3},{3,2},{4,5},{5,4},{6,7},{7,6},{8,9},{9,8},{10,11... | collective-permute-start | bytes 589832 | tf_op jit(solution)/shard_map/ppermute | solution.py:639
  130.0 0.7 copy-start.6
  130.7 2.4 %collective-permute-start.27 = (bf16[16,48,512]{2,1,0:T(8,128)(2,1)S(1)}, bf16[16,48,512]{2,1,0:T(8,128)(2,1)S(1)}, u32[]{:S(2)}, u32[]{:S(2)}) collective-permute-start(bf16[16,48,512]{2,1,0:T(8,128)(2,1)S(1)} %join.11.refs_0_), channel_id=1, source_target_pairs={{0,8},{1,9},{2,10},{3,11},{4,12},{5,13},{6,14},{7,15},{8,0},{9,1},... | collective-permute-start | bytes 2359304 | tf_op jit(solution)/shard_map/ppermute | solution.py:639
where the time goes:
time: 135 us
  Pallas kernels  65.3 us (48%)
  starting transfers between devices  39.1 us (29%)
  waiting for transfers between devices  29 us (21%)
    pallas_call x30, Pallas kernels, call(): pl.pallas_call(body, out_shape=outs, in_specs=[pl.BlockSpec(memory_space=...  63.3 us
    ppermute x24, starting transfers between devices, swap(): return lax.ppermute(values, ('dp', 'seq'), swap_route(core, x, y, z, rest))  32.4 us
    ppermute x24, waiting for transfers between devices, swap(): return lax.ppermute(values, ('dp', 'seq'), swap_route(core, x, y, z, rest))  28.9 us
    ppermute x2, starting transfers between devices, to_neighbours(): lax.ppermute(inner, 'seq', pairs)  5.05 us
  transfers between devices with their start and end apart: 28, of which 11 were waited for; matrix products, arithmetic and copies ran while one was open for 0% of the time, Pallas kernels for 34%

commit v1 on v0

--- a/solution.py
+++ b/solution.py
@@ -905,8 +905,8 @@
         after=[plane_one[0]],
     )
     chip_two = add_up([keep_two, swap(send_two, core=1)], cut(keep_two, 4))
+    from_plane_rs = swap_plane(chip_two)
     near_one = add_up([plane_one[0], swap(plane_one[1], z=1)], cut(plane_one[0], 2), after=[chip_two[0]])
-    from_plane = swap_plane(chip_two)
     own_grad, done_own = call(
         "grad_own",
         grad_own_kernel,
@@ -917,19 +917,20 @@
         after=[near_one[0]],
         token=True,
     )
-    (line_one,) = add_up([near_one[0], swap(near_one[1], z=2)], cut(near_one[0], 1), after=[done_own])
-    line_one = swap_rest(line_one)
-    plane_two = add_up([chip_two[0], *from_plane], cut(chip_two[0], 2), after=[line_one, inner_grad])
-    line_one = join([line_one, swap(line_one, z=2)], after=[plane_two[0]])
-    near_two = add_up([plane_two[0], swap(plane_two[1], z=1)], cut(plane_two[0], 2), after=[line_one])
-    line_one = join([line_one, swap(line_one, z=1)], after=[near_two[0]])
-    from_plane = swap_plane([line_one] * 4)
-    (line_two,) = add_up([near_two[0], swap(near_two[1], z=2)], cut(near_two[0], 1), after=[line_one])
-    line_two = swap_rest(line_two)
-    line_two = join([line_two, swap(line_two, z=2)])
-    line_two = join([line_two, swap(line_two, z=1)], after=[other_grad])
-    from_plane_two = swap_plane([line_two] * 4)
-    whole_one = join([line_one, *from_plane], after=[line_two])
+    (line_one0,) = add_up([near_one[0], swap(near_one[1], z=2)], cut(near_one[0], 1), after=[done_own])
+    line_one0 = swap_rest(line_one0)
+    plane_two = add_up([chip_two[0], *from_plane_rs], cut(chip_two[0], 2), after=[inner_grad])
+    line_one6 = join([line_one0, swap(line_one0, z=2)], after=[done_own])
+    near_two = add_up([plane_two[0], swap(plane_two[1], z=1)], cut(plane_two[0], 2), after=[line_one6])
+    line_one7 = join([line_one6, swap(line_one6, z=1)], after=[near_two[0]])
+    from_plane = swap_plane([line_one7] * 4)
+    (line_two0,) = add_up([near_two[0], swap(near_two[1], z=2)], cut(near_two[0], 1), after=[line_one6])
+    line_two0 = swap_rest(line_two0)
+    line_two8 = join([line_two0, swap(line_two0, z=2)], after=[])
+    line_two9 = join([line_two8, swap(line_two8, z=1)], after=[other_grad])
+    from_plane_two = swap_plane([line_two9] * 4)
+    line_two = line_two9
+    whole_one = join([line_one7, *from_plane], after=[line_two9])
     grad_tokens, done_finish = call(
         "finish",
         finish_kernel,
@@ -948,13 +949,13 @@
 
     def placed(parts, gain, *weights):
         outs = [shape(*w.shape, kind=F32) for w in weights] + [shape(1, width, kind=F32)]
-        return call("place", place_kernel, outs, *parts, weights[0], gain, flops=1e6)
-
-    grad_up, grad_out, grad_down, grad_gain_two = placed(
+        return call("place", place_kernel, outs, *parts, weights[0], gain, flops=1e6, token=True)
+
+    grad_up, grad_out, grad_down, grad_gain_two, done_one = placed(
         (whole_one, swap(whole_one, core=1)), gain_two, feedforward_in, attention_out, feedforward_out
     )
-    whole_two = join([line_two, *from_plane_two], after=[grad_gain_two, done_finish])
-    grad_in, grad_gain_one = placed((whole_two, swap(whole_two, core=1)), gain_one, attention_in)
+    whole_two = join([line_two, *from_plane_two], after=[done_one, done_finish])
+    grad_in, grad_gain_one, _ = placed((whole_two, swap(whole_two, core=1)), gain_one, attention_in)
     return activations, grad_tokens, grad_in, grad_out, grad_up, grad_down, grad_gain_one[0], grad_gain_two[0]
 
 

time: 135 us -> 134 us (level)
  starting transfers between devices: 39.1 us -> 34.4 us
  waiting for transfers between devices: 29 us -> 33.3 us
    ppermute x24, starting transfers between devices: 32.4 us -> 27.8 us  [swap(): return lax.ppermute(values, ('dp', 'seq'), swap_route(core, x, y, z, rest))]
    ppermute x24, waiting for transfers between devices: 28.9 us -> 33.2 us  [swap(): return lax.ppermute(values, ('dp', 'seq'), swap_route(core, x, y, z, rest))]
  transfers between devices with their start and end apart: 28 -> 28, of which waited for: 11 -> 10; matrix products, arithmetic and copies ran while one was open for 0% -> 0% of each run, Pallas kernels for 34% -> 35%
where the time goes in v1:
time: 134 us
  Pallas kernels  65.3 us (49%)
  starting transfers between devices  34.4 us (26%)
  waiting for transfers between devices  33.3 us (25%)
    pallas_call x30, Pallas kernels, call(): pl.pallas_call(body, out_shape=outs, in_specs=[pl.BlockSpec(memory_space=...  63.3 us
    ppermute x24, waiting for transfers between devices, swap(): return lax.ppermute(values, ('dp', 'seq'), swap_route(core, x, y, z, rest))  33.2 us
    ppermute x24, starting transfers between devices, swap(): return lax.ppermute(values, ('dp', 'seq'), swap_route(core, x, y, z, rest))  27.8 us
    ppermute x2, starting transfers between devices, to_neighbours(): lax.ppermute(inner, 'seq', pairs)  4.98 us
  transfers between devices with their start and end apart: 28, of which 10 were waited for; matrix products, arithmetic and copies ran while one was open for 0% of the time, Pallas kernels for 35%

profile of v1, /device:TPU:0, one launch (start us, length us, event | category | flops | bytes accessed | tf_op | source)
XLA Modules:
  0.0 133.9 jit_solution(6955727341101318803)
XLA Ops:
  0.6 1.9 %load.1 = (bf16[6,64,512]{2,1,0:T(8,128)(2,1)S(1)}, bf16[6,64,512]{2,1,0:T(8,128)(2,1)S(1)}, s32[6,16]{1,0:T(8,128)S(1)}, f32[1,512]{1,0:T(1,128)S(1)}, bf16[512...) custom-call(bf16[6,256,512]{2,1,0:T(8,128)(2,1)} %refs_1_.5, s32[6,16]{1,0:T(8,128)} %refs_0_.6, ...), custom_call_target="tpu_custom_call" | custom-call | tf_op jit(solution)/shard_map/load/pallas_call | solution.py:722
  2.6 3.0 %collective-permute-start = (bf16[6,64,512]{2,1,0:T(8,128)(2,1)S(1)}, bf16[6,64,512]{2,1,0:T(8,128)(2,1)S(1)}, u32[]{:S(2)}, u32[]{:S(2)}) collective-permute-start(bf16[6,64,512]{2,1,0:T(8,128)(2,1)S(1)} %get-tuple-element.100), channel_id=1, source_target_pairs={{0,1},{1,0},{2,3},{3,2},{4,5},{5,4},{6,7},{7,6},{8,9},{9,8},{10,11... | collective-permute-start | bytes 1179656 | tf_op jit(solution)/shard_map/ppermute | solution.py:625
  5.6 0.7 collective-permute-start.1
  6.3 3.7 %project.1 = (bf16[6,256,512]{2,1,0:T(8,128)(2,1)S(1)}, bf16[6,256,512]{2,1,0:T(8,128)(2,1)S(1)}, bf16[6,256,512]{2,1,0:T(8,128)(2,1)S(1)}, bf16[6,256,512]{2,1,...) custom-call(bf16[6,256,512]{2,1,0:T(8,128)(2,1)S(1)} %copy-done, ...), custom_call_target="tpu_custom_call" | custom-call | flops 30000000 | bytes 118255 | tf_op jit(solution)/shard_map/project/pallas_call | solution.py:659
  10.1 3.2 %attend_mid.1 = (bf16[6,128,512]{2,1,0:T(8,128)(2,1)S(1)}, f32[6,2,256,512]{3,2,1,0:T(8,128)S(1)}) custom-call(bf16[6,256,512]{2,1,0:T(8,128)(2,1)S(1)} %get-tuple-element.90.refs_0_.refs_1_, bf16[6,256,512]{2,1,0:T(8,128)(2,1)S(1)} %get-tuple-element.91.refs_1_.refs_2_, bf16[6,256,512]{2,1,0:T(8,128)(2,1)S(1)} %get-tuple-element.92.refs_2_.refs_3_, ...), custom_call_target="tpu_custom_call" | custom-call | flops 20000000 | bytes 118149 | tf_op jit(solution)/shard_map/attend_mid/pallas_call | solution.py:659
  13.3 6.6 %dense_mid.1 = (f32[6,128,512]{2,1,0:T(8,128)S(1)}, bf16[6,128,512]{2,1,0:T(8,128)(2,1)S(1)}, bf16[6,128,768]{2,1,0:T(8,128)(2,1)S(1)}, bf16[6,128,1536]{2,1,0:T...) custom-call(bf16[6,256,512]{2,1,0:T(8,128)(2,1)S(1)} %copy-done, ...), custom_call_target="tpu_custom_call" | custom-call | flops 50000000 | bytes 158617 | tf_op jit(solution)/shard_map/dense_mid/pallas_call | solution.py:659
  19.9 2.4 %begin.1 = (bf16[512,1536]{1,0:T(8,128)(2,1)S(1)}, bf16[768,512]{1,0:T(8,128)(2,1)S(1)}, bf16[512,512]{1,0:T(8,128)(2,1)S(1)}) custom-call(bf16[6,256,512]{2,1,0:T(8,128)(2,1)S(1)} %copy-done.1, bf16[6,128,512]{2,1,0:T(8,128)(2,1)S(1)} %get-tuple-element.95.refs_1_, bf16[6,128,1536]{2,1,0:T(8,128)(2,1)S(1)} %get-tuple-element.96.refs_2_, ...), custom_call_target="tpu_custom_call" | custom-call | flops 30000000 | bytes 103546 | tf_op jit(solution)/shard_map/begin/pallas_call | solution.py:659
  22.4 1.7 %halo.1 = (bf16[6,128,512]{2,1,0:T(8,128)(2,1)S(1)}, bf16[6,128,512]{2,1,0:T(8,128)(2,1)S(1)}, bf16[6,128,512]{2,1,0:T(8,128)(2,1)S(1)}) custom-call(bf16[512,512]{1,0:T(8,128)(2,1)S(1)} %get-tuple-element.99.refs_0_.refs_8_, bf16[6,64,512]{2,1,0:T(8,128)(2,1)S(1)} %collective-permute-done.refs_1_, bf16[6,64,512]{2,1,0:T(8,128)(2,1)S(1)} %collective-permute-done.1.refs_2_, ...), custom_call_target="tpu_custom_call" | custom-call | flops 10000000 | bytes 51138 | tf_op jit(solution)/shard_map/halo/pallas_call | solution.py:659
  24.1 2.9 %attend_out.1 = (bf16[6,128,512]{2,1,0:T(8,128)(2,1)S(1)}, f32[6,2,2,192,256]{4,3,2,1,0:T(8,128)S(1)}) custom-call(bf16[6,256,512]{2,1,0:T(8,128)(2,1)S(1)} %get-tuple-element.90.refs_0_.refs_1_, bf16[6,256,512]{2,1,0:T(8,128)(2,1)S(1)} %get-tuple-element.91.refs_1_.refs_2_, bf16[6,256,512]{2,1,0:T(8,128)(2,1)S(1)} %get-tuple-element.92.refs_2_.refs_3_, ...), custom_call_target="tpu_custom_call" | custom-call | flops 20000000 | bytes 118149 | tf_op jit(solution)/shard_map/attend_out/pallas_call | solution.py:659
  27.0 6.7 %dense_out.1 = (f32[6,128,512]{2,1,0:T(8,128)S(1)}, bf16[6,128,512]{2,1,0:T(8,128)(2,1)S(1)}, bf16[6,128,768]{2,1,0:T(8,128)(2,1)S(1)}, bf16[6,128,1536]{2,1,0:T...) custom-call(bf16[6,256,512]{2,1,0:T(8,128)(2,1)S(1)} %copy-done, ...), custom_call_target="tpu_custom_call" | custom-call | flops 50000000 | bytes 158617 | tf_op jit(solution)/shard_map/dense_out/pallas_call | solution.py:659
  33.7 2.8 %weights.1 = (bf16[16,88,512]{2,1,0:T(8,128)(2,1)S(1)}, bf16[16,88,512]{2,1,0:T(8,128)(2,1)S(1)}) custom-call(bf16[6,256,512]{2,1,0:T(8,128)(2,1)S(1)} %copy-done.1, bf16[6,128,512]{2,1,0:T(8,128)(2,1)S(1)} %get-tuple-element.107.refs_1_, bf16[6,128,1536]{2,1,0:T(8,128)(2,1)S(1)} %get-tuple-element.108.refs_2_, ...), custom_call_target="tpu_custom_call" | custom-call | flops 50000000 | bytes 132382 | tf_op jit(solution)/shard_map/weights/pallas_call | solution.py:659
  36.6 2.7 %result.1 = (bf16[6,256,512]{2,1,0:T(8,128)(2,1)}, f32[8,128]{1,0:T(8,128)S(1)}) custom-call(bf16[16,88,512]{2,1,0:T(8,128)(2,1)S(1)} %get-tuple-element.113.refs_0_.refs_1_, f32[6,128,512]{2,1,0:T(8,128)S(1)} %get-tuple-element.114.refs_1_, f32[6,128,512]{2,1,0:T(8,128)S(1)} %get-tuple-element.115.refs_2_, ...), custom_call_target="tpu_custom_call" | custom-call | flops 20000000 | bytes 78684 | tf_op jit(solution)/shard_map/result/pallas_call | solution.py:659
  39.3 0.5 collective-permute-done.2.refs_2_
  39.8 0.3 add.8
  40.1 4.3 %collective-permute-start.4 = (bf16[4,88,512]{2,1,0:T(8,128)(2,1)S(1)}, bf16[4,88,512]{2,1,0:T(8,128)(2,1)S(1)}, u32[]{:S(2)}, u32[]{:S(2)}) collective-permute-start(bf16[4,88,512]{2,1,0:T(8,128)(2,1)S(1)} %get-tuple-element.131), channel_id=1, source_target_pairs={{0,1},{1,0},{2,3},{3,2},{4,5},{5,4},{6,7},{7,6},{8,9},{9,8},{10,11... | collective-permute-start | bytes 1081352 | tf_op jit(solution)/shard_map/ppermute | solution.py:639
  44.5 1.5 %collective-permute-start.5 = (bf16[4,88,512]{2,1,0:T(8,128)(2,1)S(1)}, bf16[4,88,512]{2,1,0:T(8,128)(2,1)S(1)}, u32[]{:S(2)}, u32[]{:S(2)}) collective-permute-start(bf16[4,88,512]{2,1,0:T(8,128)(2,1)S(1)} %get-tuple-element.132), channel_id=1, source_target_pairs={{0,16},{1,17},{2,18},{3,19},{4,20},{5,21},{6,22},{7,23},{8,24},{9,... | collective-permute-start | bytes 1081352 | tf_op jit(solution)/shard_map/ppermute | solution.py:639
  46.0 13.6 %backward.1 = (bf16[6,256,768]{2,1,0:T(8,128)(2,1)S(1)}, bf16[6,128,512]{2,1,0:T(8,128)(2,1)S(1)}, bf16[6,256,768]{2,1,0:T(8,128)(2,1)S(1)}, bf16[6,128,512]{2,1...) custom-call(bf16[4,88,512]{2,1,0:T(8,128)(2,1)S(1)} %get-tuple-element.119.refs_0_.refs_1_, ...), custom_call_target="tpu_custom_call" | custom-call | flops 120000000 | bytes 279183 | tf_op jit(solution)/shard_map/backward/pallas_call | solution.py:659
  59.6 3.7 %weight_in.1.refs_0_.refs_1_ = bf16[512,1536]{1,0:T(8,128)(2,1)S(1)} custom-call(bf16[6,256,512]{2,1,0:T(8,128)(2,1)S(1)} %get-tuple-element.125.refs_0_, bf16[6,128,512]{2,1,0:T(8,128)(2,1)S(1)} %get-tuple-element.126.refs_1_, bf16[6,256,768]{2,1,0:T(8,128)(2,1)S(1)} %get-tuple-element.127.refs_2_, bf16[6,128,512]{2,1,0:T(8,128)(2,1)S(1)} %get-tuple-element.128.refs_3_, ...), custom_call_target="tpu_custom_call" | custom-call | flops 40000000 | bytes 102236 | tf_op jit(solution)/shard_map/weight_in/pallas_call | solution.py:659
  63.6 0.3 split.1
  63.9 1.6 %collective-permute-start.8 = (bf16[2,88,512]{2,1,0:T(8,128)(2,1)S(1)}, bf16[2,88,512]{2,1,0:T(8,128)(2,1)S(1)}, u32[]{:S(2)}, u32[]{:S(2)}) collective-permute-start(bf16[2,88,512]{2,1,0:T(8,128)(2,1)S(1)} %get-tuple-element.138), channel_id=1, source_target_pairs={{0,2},{1,3},{2,0},{3,1},{4,6},{5,7},{6,4},{7,5},{8,10},{9,11},{10,... | collective-permute-start | bytes 540680 | tf_op jit(solution)/shard_map/ppermute | solution.py:639
  65.6 2.0 %collective-permute-start.11 = (bf16[6,64,512]{2,1,0:T(8,128)(2,1)S(1)}, bf16[6,64,512]{2,1,0:T(8,128)(2,1)S(1)}, u32[]{:S(2)}, u32[]{:S(2)}) collective-permute-start(bf16[6,64,512]{2,1,0:T(8,128)(2,1)S(1)} %get-tuple-element.142), channel_id=1, source_target_pairs={{0,1},{1,0},{2,3},{3,2},{4,5},{5,4},{6,7},{7,6},{8,9},{9,8},{10,11... | collective-permute-start | bytes 1179656 | tf_op jit(solution)/shard_map/ppermute | solution.py:625
  67.7 3.2 %collective-permute-done.8.refs_2_ = bf16[2,88,512]{2,1,0:T(8,128)(2,1)S(1)} collective-permute-done((bf16[2,88,512]{2,1,0:T(8,128)(2,1)S(1)}, bf16[2,88,512]{2,1,0:T(8,128)(2,1)S(1)}, u32[]{:S(2)}, u32[]{:S(2)}) %collective-permute-start.8) | collective-permute-done | bytes 180256 | tf_op jit(solution)/shard_map/ppermute | solution.py:639
  71.0 2.6 %collective-permute-start.9 = (bf16[1,88,512]{2,1,0:T(8,128)(2,1)S(1)}, bf16[1,88,512]{2,1,0:T(8,128)(2,1)S(1)}, u32[]{:S(2)}, u32[]{:S(2)}) collective-permute-start(bf16[1,88,512]{2,1,0:T(8,128)(2,1)S(1)} %get-tuple-element.141), channel_id=1, source_target_pairs={{0,4},{1,5},{2,6},{3,7},{4,0},{5,1},{6,2},{7,3},{8,12},{9,13},{10,... | collective-permute-start | bytes 270344 | tf_op jit(solution)/shard_map/ppermute | solution.py:639
  73.6 1.9 %collective-permute-start.12 = (bf16[4,48,512]{2,1,0:T(8,128)(2,1)S(1)}, bf16[4,48,512]{2,1,0:T(8,128)(2,1)S(1)}, u32[]{:S(2)}, u32[]{:S(2)}) collective-permute-start(bf16[4,48,512]{2,1,0:T(8,128)(2,1)S(1)} %get-tuple-element.143), channel_id=1, source_target_pairs={{0,1},{1,0},{2,3},{3,2},{4,5},{5,4},{6,7},{7,6},{8,9},{9,8},{10,11... | collective-permute-start | bytes 589832 | tf_op jit(solution)/shard_map/ppermute | solution.py:639
  75.5 1.5 %collective-permute-start.13 = (bf16[4,48,512]{2,1,0:T(8,128)(2,1)S(1)}, bf16[4,48,512]{2,1,0:T(8,128)(2,1)S(1)}, u32[]{:S(2)}, u32[]{:S(2)}) collective-permute-start(bf16[4,48,512]{2,1,0:T(8,128)(2,1)S(1)} %get-tuple-element.144), channel_id=1, source_target_pairs={{0,16},{1,17},{2,18},{3,19},{4,20},{5,21},{6,22},{7,23},{8,24},{9,... | collective-permute-start | bytes 589832 | tf_op jit(solution)/shard_map/ppermute | solution.py:639
  77.1 3.0 %grad_own.1 = (f32[6,256,512]{2,1,0:T(8,128)S(1)}, f32[8,128]{1,0:T(8,128)S(1)}) custom-call(bf16[1,88,512]{2,1,0:T(8,128)(2,1)S(1)} %get-tuple-element.139.refs_0_.refs_1_, bf16[512,1536]{1,0:T(8,128)(2,1)S(1)} %get-tuple-element.102.refs_3_.refs_11_.refs_1_, bf16[6,256,768]{2,1,0:T(8,128)(2,1)S(1)} %get-tuple-element.127.refs_2_, ...), custom_call_target="tpu_custom_call" | custom-call | flops 20000000 | bytes 94412 | tf_op jit(solution)/shard_map/grad_own/pallas_call | solution.py:659
  80.1 0.4 collective-permute-start.10
  80.6 6.0 %collective-permute-done.10.refs_2_ = bf16[1,88,512]{2,1,0:T(8,128)(2,1)S(1)} collective-permute-done((bf16[1,88,512]{2,1,0:T(8,128)(2,1)S(1)}, bf16[1,88,512]{2,1,0:T(8,128)(2,1)S(1)}, u32[]{:S(2)}, u32[]{:S(2)}) %collective-permute-start.10) | collective-permute-done | bytes 90144 | tf_op jit(solution)/shard_map/ppermute | solution.py:639
  86.9 2.0 %collective-permute-start.15 = (bf16[2,48,512]{2,1,0:T(8,128)(2,1)S(1)}, bf16[2,48,512]{2,1,0:T(8,128)(2,1)S(1)}, u32[]{:S(2)}, u32[]{:S(2)}) collective-permute-start(bf16[2,48,512]{2,1,0:T(8,128)(2,1)S(1)} %get-tuple-element.147), channel_id=1, source_target_pairs={{0,2},{1,3},{2,0},{3,1},{4,6},{5,7},{6,4},{7,5},{8,10},{9,11},{10,... | collective-permute-start | bytes 294920 | tf_op jit(solution)/shard_map/ppermute | solution.py:639
  88.9 0.9 collective-permute-start.3
  89.8 4.8 %collective-permute-done.15.refs_2_ = bf16[2,48,512]{2,1,0:T(8,128)(2,1)S(1)} collective-permute-done((bf16[2,48,512]{2,1,0:T(8,128)(2,1)S(1)}, bf16[2,48,512]{2,1,0:T(8,128)(2,1)S(1)}, u32[]{:S(2)}, u32[]{:S(2)}) %collective-permute-start.15) | collective-permute-done | bytes 98336 | tf_op jit(solution)/shard_map/ppermute | solution.py:639
  94.7 1.4 %collective-permute-start.22 = (bf16[4,88,512]{2,1,0:T(8,128)(2,1)S(1)}, bf16[4,88,512]{2,1,0:T(8,128)(2,1)S(1)}, u32[]{:S(2)}, u32[]{:S(2)}) collective-permute-start(bf16[4,88,512]{2,1,0:T(8,128)(2,1)S(1)} %join.9.refs_1_), channel_id=1, source_target_pairs={{0,17},{1,16},{2,19},{3,18},{4,21},{5,20},{6,23},{7,22},{8,25},{9,... | collective-permute-start | bytes 1081352 | tf_op jit(solution)/shard_map/ppermute | solution.py:639
  96.1 0.5 collective-permute-start.21
  96.6 1.6 %collective-permute-start.20 = (bf16[4,88,512]{2,1,0:T(8,128)(2,1)S(1)}, bf16[4,88,512]{2,1,0:T(8,128)(2,1)S(1)}, u32[]{:S(2)}, u32[]{:S(2)}) collective-permute-start(bf16[4,88,512]{2,1,0:T(8,128)(2,1)S(1)} %join.9.refs_1_), channel_id=1, source_target_pairs={{0,1},{1,0},{2,3},{3,2},{4,5},{5,4},{6,7},{7,6},{8,9},{9,8},{10,11... | collective-permute-start | bytes 1081352 | tf_op jit(solution)/shard_map/ppermute | solution.py:639
  98.2 0.7 collective-permute-start.16
  98.9 6.9 %collective-permute-done.16.refs_2_ = bf16[1,48,512]{2,1,0:T(8,128)(2,1)S(1)} collective-permute-done((bf16[1,48,512]{2,1,0:T(8,128)(2,1)S(1)}, bf16[1,48,512]{2,1,0:T(8,128)(2,1)S(1)}, u32[]{:S(2)}, u32[]{:S(2)}) %collective-permute-start.16) | collective-permute-done | bytes 49184 | tf_op jit(solution)/shard_map/ppermute | solution.py:639
  105.9 5.0 %collective-permute-done.17.refs_1_ = bf16[1,48,512]{2,1,0:T(8,128)(2,1)S(1)} collective-permute-done((bf16[1,48,512]{2,1,0:T(8,128)(2,1)S(1)}, bf16[1,48,512]{2,1,0:T(8,128)(2,1)S(1)}, u32[]{:S(2)}, u32[]{:S(2)}) %collective-permute-start.17) | collective-permute-done | bytes 49184 | tf_op jit(solution)/shard_map/ppermute | solution.py:639
  110.9 3.4 %collective-permute-start.18 = (bf16[2,48,512]{2,1,0:T(8,128)(2,1)S(1)}, bf16[2,48,512]{2,1,0:T(8,128)(2,1)S(1)}, u32[]{:S(2)}, u32[]{:S(2)}) collective-permute-start(bf16[2,48,512]{2,1,0:T(8,128)(2,1)S(1)} %join.7.refs_1_), channel_id=1, source_target_pairs={{0,2},{1,3},{2,0},{3,1},{4,6},{5,7},{6,4},{7,5},{8,10},{9,11},{10,... | collective-permute-start | bytes 294920 | tf_op jit(solution)/shard_map/ppermute | solution.py:639
  114.3 2.6 %collective-permute-done.18.refs_2_ = bf16[2,48,512]{2,1,0:T(8,128)(2,1)S(1)} collective-permute-done((bf16[2,48,512]{2,1,0:T(8,128)(2,1)S(1)}, bf16[2,48,512]{2,1,0:T(8,128)(2,1)S(1)}, u32[]{:S(2)}, u32[]{:S(2)}) %collective-permute-start.18) | collective-permute-done | bytes 98336 | tf_op jit(solution)/shard_map/ppermute | solution.py:639
  117.1 2.2 %collective-permute-start.26 = (bf16[4,48,512]{2,1,0:T(8,128)(2,1)S(1)}, bf16[4,48,512]{2,1,0:T(8,128)(2,1)S(1)}, u32[]{:S(2)}, u32[]{:S(2)}) collective-permute-start(bf16[4,48,512]{2,1,0:T(8,128)(2,1)S(1)} %join.8.refs_0_.refs_2_), channel_id=1, source_target_pairs={{0,17},{1,16},{2,19},{3,18},{4,21},{5,20},{6,23},{7,22},{8,25},{9,... | collective-permute-start | bytes 589832 | tf_op jit(solution)/shard_map/ppermute | solution.py:639
  119.3 0.5 collective-permute-start.25
  119.9 0.8 collective-permute-start.24
  120.7 3.9 %finish.1 = (f32[6,256,512]{2,1,0:T(8,128)}, f32[8,128]{1,0:T(8,128)S(1)}) custom-call(bf16[16,88,512]{2,1,0:T(8,128)(2,1)S(1)} %join.10.refs_0_, bf16[6,256,512]{2,1,0:T(8,128)(2,1)S(1)} %copy-done, f32[6,256,512]{2,1,0:T(8,128)S(1)} %get-tuple-element.150.refs_2_, bf16[6,64,512]{2,1,0:T(8,128)(2,1)S(1)} %collective-permute-done.11.refs_0_.refs_3_, ...), custom_call_target="tpu_custom_call" | custom-call | flops 1000000 | bytes 118026 | tf_op jit(solution)/shard_map/finish/pallas_call | solution.py:659
  124.6 3.0 %place.2 = (f32[512,1536]{1,0:T(8,128)}, f32[512,512]{1,0:T(8,128)}, f32[768,512]{1,0:T(8,128)}, f32[1,512]{1,0:T(1,128)}, f32[8,128]{1,0:T(8,128)S(1)}) custom-call(bf16[16,88,512]{2,1,0:T(8,128)(2,1)S(1)} %join.10.refs_0_, bf16[16,88,512]{2,1,0:T(8,128)(2,1)S(1)} %collective-permute-done.23.refs_1_, bf16[512,1536]{1,0:T(8,128)(2,1)S(1)} %copy-done.2, ...), custom_call_target="tpu_custom_call" | custom-call | flops 10000 | bytes 102318 | tf_op jit(solution)/shard_map/place/pallas_call | solution.py:659
  127.6 1.8 %collective-permute-done.25.refs_4_ = bf16[4,48,512]{2,1,0:T(8,128)(2,1)S(1)} collective-permute-done((bf16[4,48,512]{2,1,0:T(8,128)(2,1)S(1)}, bf16[4,48,512]{2,1,0:T(8,128)(2,1)S(1)}, u32[]{:S(2)}, u32[]{:S(2)}) %collective-permute-start.25) | collective-permute-done | bytes 196640 | tf_op jit(solution)/shard_map/ppermute | solution.py:639
  129.3 0.2 collective-permute-done.24.refs_3_
  129.7 2.3 %collective-permute-done.27.refs_1_ = bf16[16,48,512]{2,1,0:T(8,128)(2,1)S(1)} collective-permute-done((bf16[16,48,512]{2,1,0:T(8,128)(2,1)S(1)}, bf16[16,48,512]{2,1,0:T(8,128)(2,1)S(1)}, u32[]{:S(2)}, u32[]{:S(2)}) %collective-permute-start.27) | collective-permute-done | bytes 786464 | tf_op jit(solution)/shard_map/ppermute | solution.py:639
  132.0 2.0 %place.3 = (f32[512,1536]{1,0:T(8,128)}, f32[1,512]{1,0:T(1,128)}, f32[8,128]{1,0:T(8,128)}) custom-call(bf16[16,48,512]{2,1,0:T(8,128)(2,1)S(1)} %join.11.refs_0_, bf16[16,48,512]{2,1,0:T(8,128)(2,1)S(1)} %collective-permute-done.27.refs_1_, bf16[512,1536]{1,0:T(8,128)(2,1)S(1)} %get-tuple-element.86.refs_2_, ...), custom_call_target="tpu_custom_call" | custom-call | flops 10000 | bytes 62996 | tf_op jit(solution)/shard_map/place/pallas_call | solution.py:659
  (51 shorter events, 1.5 us)
Async XLA Ops:
  0.6 5.7 %copy-start = (bf16[6,256,512]{2,1,0:T(8,128)(2,1)S(1)}, bf16[6,256,512]{2,1,0:T(8,128)(2,1)}, u32[]{:S(2)}) copy-start(bf16[6,256,512]{2,1,0:T(8,128)(2,1)} %refs_1_.5) | copy-start | bytes 4718596
  2.6 19.8 %collective-permute-start = (bf16[6,64,512]{2,1,0:T(8,128)(2,1)S(1)}, bf16[6,64,512]{2,1,0:T(8,128)(2,1)S(1)}, u32[]{:S(2)}, u32[]{:S(2)}) collective-permute-start(bf16[6,64,512]{2,1,0:T(8,128)(2,1)S(1)} %get-tuple-element.100), channel_id=1, source_target_pairs={{0,1},{1,0},{2,3},{3,2},{4,5},{5,4},{6,7},{7,6},{8,9},{9,8},{10,11... | collective-permute-start | bytes 1179656 | tf_op jit(solution)/shard_map/ppermute | solution.py:625
  5.6 16.8 %collective-permute-start.1 = (bf16[6,64,512]{2,1,0:T(8,128)(2,1)S(1)}, bf16[6,64,512]{2,1,0:T(8,128)(2,1)S(1)}, u32[]{:S(2)}, u32[]{:S(2)}) collective-permute-start(bf16[6,64,512]{2,1,0:T(8,128)(2,1)S(1)} %get-tuple-element.101), channel_id=1, source_target_pairs={{1,2},{2,1},{3,4},{4,3},{5,6},{6,5},{9,10},{10,9},{11,12},{12,11},... | collective-permute-start | bytes 1179656 | tf_op jit(solution)/shard_map/ppermute | solution.py:625
  10.1 3.2 %copy-start.1 = (bf16[6,256,512]{2,1,0:T(8,128)(2,1)S(1)}, bf16[6,256,512]{2,1,0:T(8,128)(2,1)}, u32[]{:S(2)}) copy-start(bf16[6,256,512]{2,1,0:T(8,128)(2,1)} %refs_0_.11) | copy-start | bytes 4718596
  10.1 3.2 %copy-start.2 = (bf16[512,1536]{1,0:T(8,128)(2,1)S(1)}, bf16[512,1536]{1,0:T(8,128)(2,1)}, u32[]{:S(2)}) copy-start(bf16[512,1536]{1,0:T(8,128)(2,1)} %refs_2_.3) | copy-start | bytes 4718596
  10.1 3.2 %copy-start.3 = (bf16[768,512]{1,0:T(8,128)(2,1)S(1)}, bf16[768,512]{1,0:T(8,128)(2,1)}, u32[]{:S(2)}) copy-start(bf16[768,512]{1,0:T(8,128)(2,1)} %refs_5_.5) | copy-start | bytes 2359300
  10.1 3.2 %copy-start.4 = (bf16[512,512]{1,0:T(8,128)(2,1)S(1)}, bf16[512,512]{1,0:T(8,128)(2,1)}, u32[]{:S(2)}) copy-start(bf16[512,512]{1,0:T(8,128)(2,1)} %refs_3_.4) | copy-start | bytes 1572868
  10.1 3.2 %copy-start.5 = (f32[512]{0:T(512)S(1)}, f32[512]{0:T(512)}, u32[]{:S(2)}) copy-start(f32[512]{0:T(512)} %param.18) | copy-start | bytes 6148
  36.5 3.3 %collective-permute-start.2 = (bf16[16,88,512]{2,1,0:T(8,128)(2,1)S(1)}, bf16[16,88,512]{2,1,0:T(8,128)(2,1)S(1)}, u32[]{:S(2)}, u32[]{:S(2)}) collective-permute-start(bf16[16,88,512]{2,1,0:T(8,128)(2,1)S(1)} %get-tuple-element.118), channel_id=1, source_target_pairs={{0,8},{1,9},{2,10},{3,11},{4,12},{5,13},{6,14},{7,15},{8,0},{9,1},... | collective-permute-start | bytes 4325384 | tf_op jit(solution)/shard_map/ppermute | solution.py:639
  40.1 23.2 %collective-permute-start.4 = (bf16[4,88,512]{2,1,0:T(8,128)(2,1)S(1)}, bf16[4,88,512]{2,1,0:T(8,128)(2,1)S(1)}, u32[]{:S(2)}, u32[]{:S(2)}) collective-permute-start(bf16[4,88,512]{2,1,0:T(8,128)(2,1)S(1)} %get-tuple-element.131), channel_id=1, source_target_pairs={{0,1},{1,0},{2,3},{3,2},{4,5},{5,4},{6,7},{7,6},{8,9},{9,8},{10,11... | collective-permute-start | bytes 1081352 | tf_op jit(solution)/shard_map/ppermute | solution.py:639
  44.5 18.9 %collective-permute-start.5 = (bf16[4,88,512]{2,1,0:T(8,128)(2,1)S(1)}, bf16[4,88,512]{2,1,0:T(8,128)(2,1)S(1)}, u32[]{:S(2)}, u32[]{:S(2)}) collective-permute-start(bf16[4,88,512]{2,1,0:T(8,128)(2,1)S(1)} %get-tuple-element.132), channel_id=1, source_target_pairs={{0,16},{1,17},{2,18},{3,19},{4,20},{5,21},{6,22},{7,23},{8,24},{9,... | collective-permute-start | bytes 1081352 | tf_op jit(solution)/shard_map/ppermute | solution.py:639
  45.9 17.5 %collective-permute-start.6 = (bf16[4,88,512]{2,1,0:T(8,128)(2,1)S(1)}, bf16[4,88,512]{2,1,0:T(8,128)(2,1)S(1)}, u32[]{:S(2)}, u32[]{:S(2)}) collective-permute-start(bf16[4,88,512]{2,1,0:T(8,128)(2,1)S(1)} %get-tuple-element.133), channel_id=1, source_target_pairs={{0,17},{1,16},{2,19},{3,18},{4,21},{5,20},{6,23},{7,22},{8,25},{9,... | collective-permute-start | bytes 1081352 | tf_op jit(solution)/shard_map/ppermute | solution.py:639
  63.9 3.7 %collective-permute-start.7 = (bf16[16,48,512]{2,1,0:T(8,128)(2,1)S(1)}, bf16[16,48,512]{2,1,0:T(8,128)(2,1)S(1)}, u32[]{:S(2)}, u32[]{:S(2)}) collective-permute-start(bf16[16,48,512]{2,1,0:T(8,128)(2,1)S(1)} %get-tuple-element.136), channel_id=1, source_target_pairs={{0,8},{1,9},{2,10},{3,11},{4,12},{5,13},{6,14},{7,15},{8,0},{9,1},... | collective-permute-start | bytes 2359304 | tf_op jit(solution)/shard_map/ppermute | solution.py:639
  63.9 7.0 %collective-permute-start.8 = (bf16[2,88,512]{2,1,0:T(8,128)(2,1)S(1)}, bf16[2,88,512]{2,1,0:T(8,128)(2,1)S(1)}, u32[]{:S(2)}, u32[]{:S(2)}) collective-permute-start(bf16[2,88,512]{2,1,0:T(8,128)(2,1)S(1)} %get-tuple-element.138), channel_id=1, source_target_pairs={{0,2},{1,3},{2,0},{3,1},{4,6},{5,7},{6,4},{7,5},{8,10},{9,11},{10,... | collective-permute-start | bytes 540680 | tf_op jit(solution)/shard_map/ppermute | solution.py:639
  65.6 21.2 %collective-permute-start.11 = (bf16[6,64,512]{2,1,0:T(8,128)(2,1)S(1)}, bf16[6,64,512]{2,1,0:T(8,128)(2,1)S(1)}, u32[]{:S(2)}, u32[]{:S(2)}) collective-permute-start(bf16[6,64,512]{2,1,0:T(8,128)(2,1)S(1)} %get-tuple-element.142), channel_id=1, source_target_pairs={{0,1},{1,0},{2,3},{3,2},{4,5},{5,4},{6,7},{7,6},{8,9},{9,8},{10,11... | collective-permute-start | bytes 1179656 | tf_op jit(solution)/shard_map/ppermute | solution.py:625
  71.0 9.1 %collective-permute-start.9 = (bf16[1,88,512]{2,1,0:T(8,128)(2,1)S(1)}, bf16[1,88,512]{2,1,0:T(8,128)(2,1)S(1)}, u32[]{:S(2)}, u32[]{:S(2)}) collective-permute-start(bf16[1,88,512]{2,1,0:T(8,128)(2,1)S(1)} %get-tuple-element.141), channel_id=1, source_target_pairs={{0,4},{1,5},{2,6},{3,7},{4,0},{5,1},{6,2},{7,3},{8,12},{9,13},{10,... | collective-permute-start | bytes 270344 | tf_op jit(solution)/shard_map/ppermute | solution.py:639
  73.6 13.1 %collective-permute-start.12 = (bf16[4,48,512]{2,1,0:T(8,128)(2,1)S(1)}, bf16[4,48,512]{2,1,0:T(8,128)(2,1)S(1)}, u32[]{:S(2)}, u32[]{:S(2)}) collective-permute-start(bf16[4,48,512]{2,1,0:T(8,128)(2,1)S(1)} %get-tuple-element.143), channel_id=1, source_target_pairs={{0,1},{1,0},{2,3},{3,2},{4,5},{5,4},{6,7},{7,6},{8,9},{9,8},{10,11... | collective-permute-start | bytes 589832 | tf_op jit(solution)/shard_map/ppermute | solution.py:639
  75.5 11.2 %collective-permute-start.13 = (bf16[4,48,512]{2,1,0:T(8,128)(2,1)S(1)}, bf16[4,48,512]{2,1,0:T(8,128)(2,1)S(1)}, u32[]{:S(2)}, u32[]{:S(2)}) collective-permute-start(bf16[4,48,512]{2,1,0:T(8,128)(2,1)S(1)} %get-tuple-element.144), channel_id=1, source_target_pairs={{0,16},{1,17},{2,18},{3,19},{4,20},{5,21},{6,22},{7,23},{8,24},{9,... | collective-permute-start | bytes 589832 | tf_op jit(solution)/shard_map/ppermute | solution.py:639
  77.0 9.7 %collective-permute-start.14 = (bf16[4,48,512]{2,1,0:T(8,128)(2,1)S(1)}, bf16[4,48,512]{2,1,0:T(8,128)(2,1)S(1)}, u32[]{:S(2)}, u32[]{:S(2)}) collective-permute-start(bf16[4,48,512]{2,1,0:T(8,128)(2,1)S(1)} %get-tuple-element.145), channel_id=1, source_target_pairs={{0,17},{1,16},{2,19},{3,18},{4,21},{5,20},{6,23},{7,22},{8,25},{9,... | collective-permute-start | bytes 589832 | tf_op jit(solution)/shard_map/ppermute | solution.py:639
  80.1 6.5 %collective-permute-start.10 = (bf16[1,88,512]{2,1,0:T(8,128)(2,1)S(1)}, bf16[1,88,512]{2,1,0:T(8,128)(2,1)S(1)}, u32[]{:S(2)}, u32[]{:S(2)}) collective-permute-start(bf16[1,88,512]{2,1,0:T(8,128)(2,1)S(1)} %add.12.refs_1_), channel_id=1, source_target_pairs={{0,4},{1,5},{2,6},{3,7},{4,0},{5,1},{6,2},{7,3},{8,12},{9,13},{10,... | collective-permute-start | bytes 270344 | tf_op jit(solution)/shard_map/ppermute | solution.py:639
  86.6 8.0 %collective-permute-start.19 = (bf16[2,88,512]{2,1,0:T(8,128)(2,1)S(1)}, bf16[2,88,512]{2,1,0:T(8,128)(2,1)S(1)}, u32[]{:S(2)}, u32[]{:S(2)}) collective-permute-start(bf16[2,88,512]{2,1,0:T(8,128)(2,1)S(1)} %join.6.refs_0_.refs_1_), channel_id=1, source_target_pairs={{0,2},{1,3},{2,0},{3,1},{4,6},{5,7},{6,4},{7,5},{8,10},{9,11},{10,... | collective-permute-start | bytes 540680 | tf_op jit(solution)/shard_map/ppermute | solution.py:639
  86.9 7.7 %collective-permute-start.15 = (bf16[2,48,512]{2,1,0:T(8,128)(2,1)S(1)}, bf16[2,48,512]{2,1,0:T(8,128)(2,1)S(1)}, u32[]{:S(2)}, u32[]{:S(2)}) collective-permute-start(bf16[2,48,512]{2,1,0:T(8,128)(2,1)S(1)} %get-tuple-element.147), channel_id=1, source_target_pairs={{0,2},{1,3},{2,0},{3,1},{4,6},{5,7},{6,4},{7,5},{8,10},{9,11},{10,... | collective-permute-start | bytes 294920 | tf_op jit(solution)/shard_map/ppermute | solution.py:639
  88.9 25.4 %collective-permute-start.3 = (bf16[6,64,512]{2,1,0:T(8,128)(2,1)S(1)}, bf16[6,64,512]{2,1,0:T(8,128)(2,1)S(1)}, u32[]{:S(2)}, u32[]{:S(2)}) collective-permute-start(bf16[6,64,512]{2,1,0:T(8,128)(2,1)S(1)} %get-tuple-element.124), channel_id=1, source_target_pairs={{1,2},{2,1},{3,4},{4,3},{5,6},{6,5},{9,10},{10,9},{11,12},{12,11},... | collective-permute-start | bytes 1179656 | tf_op jit(solution)/shard_map/ppermute | solution.py:625
  94.7 22.2 %collective-permute-start.22 = (bf16[4,88,512]{2,1,0:T(8,128)(2,1)S(1)}, bf16[4,88,512]{2,1,0:T(8,128)(2,1)S(1)}, u32[]{:S(2)}, u32[]{:S(2)}) collective-permute-start(bf16[4,88,512]{2,1,0:T(8,128)(2,1)S(1)} %join.9.refs_1_), channel_id=1, source_target_pairs={{0,17},{1,16},{2,19},{3,18},{4,21},{5,20},{6,23},{7,22},{8,25},{9,... | collective-permute-start | bytes 1081352 | tf_op jit(solution)/shard_map/ppermute | solution.py:639
  96.1 20.8 %collective-permute-start.21 = (bf16[4,88,512]{2,1,0:T(8,128)(2,1)S(1)}, bf16[4,88,512]{2,1,0:T(8,128)(2,1)S(1)}, u32[]{:S(2)}, u32[]{:S(2)}) collective-permute-start(bf16[4,88,512]{2,1,0:T(8,128)(2,1)S(1)} %join.9.refs_1_), channel_id=1, source_target_pairs={{0,16},{1,17},{2,18},{3,19},{4,20},{5,21},{6,22},{7,23},{8,24},{9,... | collective-permute-start | bytes 1081352 | tf_op jit(solution)/shard_map/ppermute | solution.py:639
  96.6 20.3 %collective-permute-start.20 = (bf16[4,88,512]{2,1,0:T(8,128)(2,1)S(1)}, bf16[4,88,512]{2,1,0:T(8,128)(2,1)S(1)}, u32[]{:S(2)}, u32[]{:S(2)}) collective-permute-start(bf16[4,88,512]{2,1,0:T(8,128)(2,1)S(1)} %join.9.refs_1_), channel_id=1, source_target_pairs={{0,1},{1,0},{2,3},{3,2},{4,5},{5,4},{6,7},{7,6},{8,9},{9,8},{10,11... | collective-permute-start | bytes 1081352 | tf_op jit(solution)/shard_map/ppermute | solution.py:639
  98.2 7.6 %collective-permute-start.16 = (bf16[1,48,512]{2,1,0:T(8,128)(2,1)S(1)}, bf16[1,48,512]{2,1,0:T(8,128)(2,1)S(1)}, u32[]{:S(2)}, u32[]{:S(2)}) collective-permute-start(bf16[1,48,512]{2,1,0:T(8,128)(2,1)S(1)} %get-tuple-element.149), channel_id=1, source_target_pairs={{0,4},{1,5},{2,6},{3,7},{4,0},{5,1},{6,2},{7,3},{8,12},{9,13},{10,... | collective-permute-start | bytes 147464 | tf_op jit(solution)/shard_map/ppermute | solution.py:639
  105.8 5.1 %collective-permute-start.17 = (bf16[1,48,512]{2,1,0:T(8,128)(2,1)S(1)}, bf16[1,48,512]{2,1,0:T(8,128)(2,1)S(1)}, u32[]{:S(2)}, u32[]{:S(2)}) collective-permute-start(bf16[1,48,512]{2,1,0:T(8,128)(2,1)S(1)} %add.15.refs_0_), channel_id=1, source_target_pairs={{0,4},{1,5},{2,6},{3,7},{4,0},{5,1},{6,2},{7,3},{8,12},{9,13},{10,... | collective-permute-start | bytes 147464 | tf_op jit(solution)/shard_map/ppermute | solution.py:639
  110.9 6.0 %collective-permute-start.18 = (bf16[2,48,512]{2,1,0:T(8,128)(2,1)S(1)}, bf16[2,48,512]{2,1,0:T(8,128)(2,1)S(1)}, u32[]{:S(2)}, u32[]{:S(2)}) collective-permute-start(bf16[2,48,512]{2,1,0:T(8,128)(2,1)S(1)} %join.7.refs_1_), channel_id=1, source_target_pairs={{0,2},{1,3},{2,0},{3,1},{4,6},{5,7},{6,4},{7,5},{8,10},{9,11},{10,... | collective-permute-start | bytes 294920 | tf_op jit(solution)/shard_map/ppermute | solution.py:639
  117.0 7.5 %collective-permute-start.23 = (bf16[16,88,512]{2,1,0:T(8,128)(2,1)S(1)}, bf16[16,88,512]{2,1,0:T(8,128)(2,1)S(1)}, u32[]{:S(2)}, u32[]{:S(2)}) collective-permute-start(bf16[16,88,512]{2,1,0:T(8,128)(2,1)S(1)} %join.10.refs_0_), channel_id=1, source_target_pairs={{0,8},{1,9},{2,10},{3,11},{4,12},{5,13},{6,14},{7,15},{8,0},{9,1},... | collective-permute-start | bytes 4325384 | tf_op jit(solution)/shard_map/ppermute | solution.py:639
  117.1 10.5 %collective-permute-start.26 = (bf16[4,48,512]{2,1,0:T(8,128)(2,1)S(1)}, bf16[4,48,512]{2,1,0:T(8,128)(2,1)S(1)}, u32[]{:S(2)}, u32[]{:S(2)}) collective-permute-start(bf16[4,48,512]{2,1,0:T(8,128)(2,1)S(1)} %join.8.refs_0_.refs_2_), channel_id=1, source_target_pairs={{0,17},{1,16},{2,19},{3,18},{4,21},{5,20},{6,23},{7,22},{8,25},{9,... | collective-permute-start | bytes 589832 | tf_op jit(solution)/shard_map/ppermute | solution.py:639
  119.3 10.0 %collective-permute-start.25 = (bf16[4,48,512]{2,1,0:T(8,128)(2,1)S(1)}, bf16[4,48,512]{2,1,0:T(8,128)(2,1)S(1)}, u32[]{:S(2)}, u32[]{:S(2)}) collective-permute-start(bf16[4,48,512]{2,1,0:T(8,128)(2,1)S(1)} %join.8.refs_0_.refs_2_), channel_id=1, source_target_pairs={{0,16},{1,17},{2,18},{3,19},{4,20},{5,21},{6,22},{7,23},{8,24},{9,... | collective-permute-start | bytes 589832 | tf_op jit(solution)/shard_map/ppermute | solution.py:639
  119.9 9.7 %collective-permute-start.24 = (bf16[4,48,512]{2,1,0:T(8,128)(2,1)S(1)}, bf16[4,48,512]{2,1,0:T(8,128)(2,1)S(1)}, u32[]{:S(2)}, u32[]{:S(2)}) collective-permute-start(bf16[4,48,512]{2,1,0:T(8,128)(2,1)S(1)} %join.8.refs_0_.refs_2_), channel_id=1, source_target_pairs={{0,1},{1,0},{2,3},{3,2},{4,5},{5,4},{6,7},{7,6},{8,9},{9,8},{10,11... | collective-permute-start | bytes 589832 | tf_op jit(solution)/shard_map/ppermute | solution.py:639
  129.6 2.4 %collective-permute-start.27 = (bf16[16,48,512]{2,1,0:T(8,128)(2,1)S(1)}, bf16[16,48,512]{2,1,0:T(8,128)(2,1)S(1)}, u32[]{:S(2)}, u32[]{:S(2)}) collective-permute-start(bf16[16,48,512]{2,1,0:T(8,128)(2,1)S(1)} %join.11.refs_0_), channel_id=1, source_target_pairs={{0,8},{1,9},{2,10},{3,11},{4,12},{5,13},{6,14},{7,15},{8,0},{9,1},... | collective-permute-start | bytes 2359304 | tf_op jit(solution)/shard_map/ppermute | solution.py:639

commit v2 on v1

--- a/solution.py
+++ b/solution.py
@@ -682,6 +682,10 @@
     return [swap(parts[k], x=k >> 1, y=k & 1) for k in (1, 2, 3)]
 
 
+def swap_line(parts):
+    return [swap(parts[k], z=(k >> 1) + 2 * (k & 1)) for k in (1, 2, 3)]
+
+
 def swap_rest(own):
     rest = 1
     while 8 * rest < lax.axis_size("seq"):
@@ -895,7 +899,7 @@
         *grads,
         flops=4e9,
     )
-    plane_one = add_up([chip_one[0], *from_plane], cut(chip_one[0], 2), after=[total_in])
+    plane_one = add_up([chip_one[0], *from_plane], cut(chip_one[0], 4), after=[total_in])
     keep_two, send_two = call(
         "split",
         split_kernel,
@@ -906,7 +910,6 @@
     )
     chip_two = add_up([keep_two, swap(send_two, core=1)], cut(keep_two, 4))
     from_plane_rs = swap_plane(chip_two)
-    near_one = add_up([plane_one[0], swap(plane_one[1], z=1)], cut(plane_one[0], 2), after=[chip_two[0]])
     own_grad, done_own = call(
         "grad_own",
         grad_own_kernel,
@@ -914,10 +917,10 @@
         weight,
         *grads[::2],
         flops=2e9,
-        after=[near_one[0]],
+        after=[chip_two[0]],
         token=True,
     )
-    (line_one0,) = add_up([near_one[0], swap(near_one[1], z=2)], cut(near_one[0], 1), after=[done_own])
+    (line_one0,) = add_up([plane_one[0], *swap_line(plane_one)], cut(plane_one[0], 1), after=[])
     line_one0 = swap_rest(line_one0)
     plane_two = add_up([chip_two[0], *from_plane_rs], cut(chip_two[0], 2), after=[inner_grad])
     line_one6 = join([line_one0, swap(line_one0, z=2)], after=[done_own])

time: 134 us -> 132 us (0.985)
  starting transfers between devices: 34.4 us -> 30.9 us
  waiting for transfers between devices: 33.3 us -> 34.8 us
    ppermute x24 -> x25, starting transfers between devices: 27.8 us -> 24.3 us  [swap(): return lax.ppermute(values, ('dp', 'seq'), swap_route(core, x, y, z, rest))]
    ppermute x24 -> x25, waiting for transfers between devices: 33.2 us -> 34.8 us  [swap(): return lax.ppermute(values, ('dp', 'seq'), swap_route(core, x, y, z, rest))]
    pallas_call x30 -> x29, Pallas kernels: 63.3 us -> 63.3 us  [call(): pl.pallas_call(body, out_shape=outs, in_specs=[pl.BlockSpec(memory_space=...]
  transfers between devices with their start and end apart: 28 -> 29, of which waited for: 10 -> 12; matrix products, arithmetic and copies ran while one was open for 0% -> 0% of each run, Pallas kernels for 35% -> 35%
where the time goes in v2:
time: 132 us
  Pallas kernels  65.2 us (49%)
  waiting for transfers between devices  34.8 us (26%)
  starting transfers between devices  30.9 us (23%)
    pallas_call x29, Pallas kernels, call(): pl.pallas_call(body, out_shape=outs, in_specs=[pl.BlockSpec(memory_space=...  63.3 us
    ppermute x25, waiting for transfers between devices, swap(): return lax.ppermute(values, ('dp', 'seq'), swap_route(core, x, y, z, rest))  34.8 us
    ppermute x25, starting transfers between devices, swap(): return lax.ppermute(values, ('dp', 'seq'), swap_route(core, x, y, z, rest))  24.3 us
    ppermute x2, starting transfers between devices, to_neighbours(): lax.ppermute(inner, 'seq', pairs)  5.05 us
  transfers between devices with their start and end apart: 29, of which 12 were waited for; matrix products, arithmetic and copies ran while one was open for 0% of the time, Pallas kernels for 35%

profile of v2, /device:TPU:0, one launch (start us, length us, event | category | flops | bytes accessed | tf_op | source)
XLA Modules:
  0.0 132.0 jit_solution(12363484916060011778)
XLA Ops:
  0.6 1.9 %load.1 = (bf16[6,64,512]{2,1,0:T(8,128)(2,1)S(1)}, bf16[6,64,512]{2,1,0:T(8,128)(2,1)S(1)}, s32[6,16]{1,0:T(8,128)S(1)}, f32[1,512]{1,0:T(1,128)S(1)}, bf16[512...) custom-call(bf16[6,256,512]{2,1,0:T(8,128)(2,1)} %refs_1_.5, s32[6,16]{1,0:T(8,128)} %refs_0_.6, ...), custom_call_target="tpu_custom_call" | custom-call | tf_op jit(solution)/shard_map/load/pallas_call | solution.py:726
  2.6 3.0 %collective-permute-start = (bf16[6,64,512]{2,1,0:T(8,128)(2,1)S(1)}, bf16[6,64,512]{2,1,0:T(8,128)(2,1)S(1)}, u32[]{:S(2)}, u32[]{:S(2)}) collective-permute-start(bf16[6,64,512]{2,1,0:T(8,128)(2,1)S(1)} %get-tuple-element.100), channel_id=1, source_target_pairs={{0,1},{1,0},{2,3},{3,2},{4,5},{5,4},{6,7},{7,6},{8,9},{9,8},{10,11... | collective-permute-start | bytes 1179656 | tf_op jit(solution)/shard_map/ppermute | solution.py:625
  5.6 0.7 collective-permute-start.1
  6.3 3.7 %project.1 = (bf16[6,256,512]{2,1,0:T(8,128)(2,1)S(1)}, bf16[6,256,512]{2,1,0:T(8,128)(2,1)S(1)}, bf16[6,256,512]{2,1,0:T(8,128)(2,1)S(1)}, bf16[6,256,512]{2,1,...) custom-call(bf16[6,256,512]{2,1,0:T(8,128)(2,1)S(1)} %copy-done, ...), custom_call_target="tpu_custom_call" | custom-call | flops 30000000 | bytes 118255 | tf_op jit(solution)/shard_map/project/pallas_call | solution.py:659
  10.1 3.2 %attend_mid.1 = (bf16[6,128,512]{2,1,0:T(8,128)(2,1)S(1)}, f32[6,2,256,512]{3,2,1,0:T(8,128)S(1)}) custom-call(bf16[6,256,512]{2,1,0:T(8,128)(2,1)S(1)} %get-tuple-element.90.refs_0_.refs_1_, bf16[6,256,512]{2,1,0:T(8,128)(2,1)S(1)} %get-tuple-element.91.refs_1_.refs_2_, bf16[6,256,512]{2,1,0:T(8,128)(2,1)S(1)} %get-tuple-element.92.refs_2_.refs_3_, ...), custom_call_target="tpu_custom_call" | custom-call | flops 20000000 | bytes 118149 | tf_op jit(solution)/shard_map/attend_mid/pallas_call | solution.py:659
  13.3 6.6 %dense_mid.1 = (f32[6,128,512]{2,1,0:T(8,128)S(1)}, bf16[6,128,512]{2,1,0:T(8,128)(2,1)S(1)}, bf16[6,128,768]{2,1,0:T(8,128)(2,1)S(1)}, bf16[6,128,1536]{2,1,0:T...) custom-call(bf16[6,256,512]{2,1,0:T(8,128)(2,1)S(1)} %copy-done, ...), custom_call_target="tpu_custom_call" | custom-call | flops 50000000 | bytes 158617 | tf_op jit(solution)/shard_map/dense_mid/pallas_call | solution.py:659
  19.9 2.4 %begin.1 = (bf16[512,1536]{1,0:T(8,128)(2,1)S(1)}, bf16[768,512]{1,0:T(8,128)(2,1)S(1)}, bf16[512,512]{1,0:T(8,128)(2,1)S(1)}) custom-call(bf16[6,256,512]{2,1,0:T(8,128)(2,1)S(1)} %copy-done.1, bf16[6,128,512]{2,1,0:T(8,128)(2,1)S(1)} %get-tuple-element.95.refs_1_, bf16[6,128,1536]{2,1,0:T(8,128)(2,1)S(1)} %get-tuple-element.96.refs_2_, ...), custom_call_target="tpu_custom_call" | custom-call | flops 30000000 | bytes 103546 | tf_op jit(solution)/shard_map/begin/pallas_call | solution.py:659
  22.4 1.7 %halo.1 = (bf16[6,128,512]{2,1,0:T(8,128)(2,1)S(1)}, bf16[6,128,512]{2,1,0:T(8,128)(2,1)S(1)}, bf16[6,128,512]{2,1,0:T(8,128)(2,1)S(1)}) custom-call(bf16[512,512]{1,0:T(8,128)(2,1)S(1)} %get-tuple-element.99.refs_0_.refs_8_, bf16[6,64,512]{2,1,0:T(8,128)(2,1)S(1)} %collective-permute-done.refs_1_, bf16[6,64,512]{2,1,0:T(8,128)(2,1)S(1)} %collective-permute-done.1.refs_2_, ...), custom_call_target="tpu_custom_call" | custom-call | flops 10000000 | bytes 51138 | tf_op jit(solution)/shard_map/halo/pallas_call | solution.py:659
  24.1 2.9 %attend_out.1 = (bf16[6,128,512]{2,1,0:T(8,128)(2,1)S(1)}, f32[6,2,2,192,256]{4,3,2,1,0:T(8,128)S(1)}) custom-call(bf16[6,256,512]{2,1,0:T(8,128)(2,1)S(1)} %get-tuple-element.90.refs_0_.refs_1_, bf16[6,256,512]{2,1,0:T(8,128)(2,1)S(1)} %get-tuple-element.91.refs_1_.refs_2_, bf16[6,256,512]{2,1,0:T(8,128)(2,1)S(1)} %get-tuple-element.92.refs_2_.refs_3_, ...), custom_call_target="tpu_custom_call" | custom-call | flops 20000000 | bytes 118149 | tf_op jit(solution)/shard_map/attend_out/pallas_call | solution.py:659
  27.0 6.7 %dense_out.1 = (f32[6,128,512]{2,1,0:T(8,128)S(1)}, bf16[6,128,512]{2,1,0:T(8,128)(2,1)S(1)}, bf16[6,128,768]{2,1,0:T(8,128)(2,1)S(1)}, bf16[6,128,1536]{2,1,0:T...) custom-call(bf16[6,256,512]{2,1,0:T(8,128)(2,1)S(1)} %copy-done, ...), custom_call_target="tpu_custom_call" | custom-call | flops 50000000 | bytes 158617 | tf_op jit(solution)/shard_map/dense_out/pallas_call | solution.py:659
  33.7 2.8 %weights.1 = (bf16[16,88,512]{2,1,0:T(8,128)(2,1)S(1)}, bf16[16,88,512]{2,1,0:T(8,128)(2,1)S(1)}) custom-call(bf16[6,256,512]{2,1,0:T(8,128)(2,1)S(1)} %copy-done.1, bf16[6,128,512]{2,1,0:T(8,128)(2,1)S(1)} %get-tuple-element.107.refs_1_, bf16[6,128,1536]{2,1,0:T(8,128)(2,1)S(1)} %get-tuple-element.108.refs_2_, ...), custom_call_target="tpu_custom_call" | custom-call | flops 50000000 | bytes 132382 | tf_op jit(solution)/shard_map/weights/pallas_call | solution.py:659
  36.6 2.7 %result.1 = (bf16[6,256,512]{2,1,0:T(8,128)(2,1)}, f32[8,128]{1,0:T(8,128)S(1)}) custom-call(bf16[16,88,512]{2,1,0:T(8,128)(2,1)S(1)} %get-tuple-element.113.refs_0_.refs_1_, f32[6,128,512]{2,1,0:T(8,128)S(1)} %get-tuple-element.114.refs_1_, f32[6,128,512]{2,1,0:T(8,128)S(1)} %get-tuple-element.115.refs_2_, ...), custom_call_target="tpu_custom_call" | custom-call | flops 20000000 | bytes 78684 | tf_op jit(solution)/shard_map/result/pallas_call | solution.py:659
  39.3 0.5 collective-permute-done.2.refs_2_
  39.8 0.3 add.7
  40.1 4.3 %collective-permute-start.4 = (bf16[4,88,512]{2,1,0:T(8,128)(2,1)S(1)}, bf16[4,88,512]{2,1,0:T(8,128)(2,1)S(1)}, u32[]{:S(2)}, u32[]{:S(2)}) collective-permute-start(bf16[4,88,512]{2,1,0:T(8,128)(2,1)S(1)} %get-tuple-element.131), channel_id=1, source_target_pairs={{0,1},{1,0},{2,3},{3,2},{4,5},{5,4},{6,7},{7,6},{8,9},{9,8},{10,11... | collective-permute-start | bytes 1081352 | tf_op jit(solution)/shard_map/ppermute | solution.py:639
  44.5 1.5 %collective-permute-start.5 = (bf16[4,88,512]{2,1,0:T(8,128)(2,1)S(1)}, bf16[4,88,512]{2,1,0:T(8,128)(2,1)S(1)}, u32[]{:S(2)}, u32[]{:S(2)}) collective-permute-start(bf16[4,88,512]{2,1,0:T(8,128)(2,1)S(1)} %get-tuple-element.132), channel_id=1, source_target_pairs={{0,16},{1,17},{2,18},{3,19},{4,20},{5,21},{6,22},{7,23},{8,24},{9,... | collective-permute-start | bytes 1081352 | tf_op jit(solution)/shard_map/ppermute | solution.py:639
  46.0 13.6 %backward.1 = (bf16[6,256,768]{2,1,0:T(8,128)(2,1)S(1)}, bf16[6,128,512]{2,1,0:T(8,128)(2,1)S(1)}, bf16[6,256,768]{2,1,0:T(8,128)(2,1)S(1)}, bf16[6,128,512]{2,1...) custom-call(bf16[4,88,512]{2,1,0:T(8,128)(2,1)S(1)} %get-tuple-element.119.refs_0_.refs_1_, ...), custom_call_target="tpu_custom_call" | custom-call | flops 120000000 | bytes 279183 | tf_op jit(solution)/shard_map/backward/pallas_call | solution.py:659
  59.6 3.7 %weight_in.1.refs_0_.refs_1_ = bf16[512,1536]{1,0:T(8,128)(2,1)S(1)} custom-call(bf16[6,256,512]{2,1,0:T(8,128)(2,1)S(1)} %get-tuple-element.125.refs_0_, bf16[6,128,512]{2,1,0:T(8,128)(2,1)S(1)} %get-tuple-element.126.refs_1_, bf16[6,256,768]{2,1,0:T(8,128)(2,1)S(1)} %get-tuple-element.127.refs_2_, bf16[6,128,512]{2,1,0:T(8,128)(2,1)S(1)} %get-tuple-element.128.refs_3_, ...), custom_call_target="tpu_custom_call" | custom-call | flops 40000000 | bytes 102236 | tf_op jit(solution)/shard_map/weight_in/pallas_call | solution.py:659
  63.6 0.3 split.1
  63.9 2.0 %collective-permute-start.12 = (bf16[6,64,512]{2,1,0:T(8,128)(2,1)S(1)}, bf16[6,64,512]{2,1,0:T(8,128)(2,1)S(1)}, u32[]{:S(2)}, u32[]{:S(2)}) collective-permute-start(bf16[6,64,512]{2,1,0:T(8,128)(2,1)S(1)} %get-tuple-element.142), channel_id=1, source_target_pairs={{0,1},{1,0},{2,3},{3,2},{4,5},{5,4},{6,7},{7,6},{8,9},{9,8},{10,11... | collective-permute-start | bytes 1179656 | tf_op jit(solution)/shard_map/ppermute | solution.py:625
  66.0 2.6 %collective-permute-start.8 = (bf16[1,88,512]{2,1,0:T(8,128)(2,1)S(1)}, bf16[1,88,512]{2,1,0:T(8,128)(2,1)S(1)}, u32[]{:S(2)}, u32[]{:S(2)}) collective-permute-start(bf16[1,88,512]{2,1,0:T(8,128)(2,1)S(1)} %get-tuple-element.139), channel_id=1, source_target_pairs={{0,4},{1,5},{2,6},{3,7},{4,0},{5,1},{6,2},{7,3},{8,12},{9,13},{10,... | collective-permute-start | bytes 270344 | tf_op jit(solution)/shard_map/ppermute | solution.py:639
  68.5 1.8 %collective-permute-start.10 = (bf16[1,88,512]{2,1,0:T(8,128)(2,1)S(1)}, bf16[1,88,512]{2,1,0:T(8,128)(2,1)S(1)}, u32[]{:S(2)}, u32[]{:S(2)}) collective-permute-start(bf16[1,88,512]{2,1,0:T(8,128)(2,1)S(1)} %get-tuple-element.141), channel_id=1, source_target_pairs={{0,6},{1,7},{2,4},{3,5},{4,2},{5,3},{6,0},{7,1},{8,14},{9,15},{10,... | collective-permute-start | bytes 270344 | tf_op jit(solution)/shard_map/ppermute | solution.py:639
  70.7 3.9 %collective-permute-done.8.refs_1_ = bf16[1,88,512]{2,1,0:T(8,128)(2,1)S(1)} collective-permute-done((bf16[1,88,512]{2,1,0:T(8,128)(2,1)S(1)}, bf16[1,88,512]{2,1,0:T(8,128)(2,1)S(1)}, u32[]{:S(2)}, u32[]{:S(2)}) %collective-permute-start.8) | collective-permute-done | bytes 90144 | tf_op jit(solution)/shard_map/ppermute | solution.py:639
  74.6 1.5 %collective-permute-start.14 = (bf16[4,48,512]{2,1,0:T(8,128)(2,1)S(1)}, bf16[4,48,512]{2,1,0:T(8,128)(2,1)S(1)}, u32[]{:S(2)}, u32[]{:S(2)}) collective-permute-start(bf16[4,48,512]{2,1,0:T(8,128)(2,1)S(1)} %get-tuple-element.144), channel_id=1, source_target_pairs={{0,16},{1,17},{2,18},{3,19},{4,20},{5,21},{6,22},{7,23},{8,24},{9,... | collective-permute-start | bytes 589832 | tf_op jit(solution)/shard_map/ppermute | solution.py:639
  76.0 0.5 collective-permute-done.10.refs_3_
  76.6 0.4 collective-permute-start.11
  77.0 3.0 %grad_own.1 = (f32[6,256,512]{2,1,0:T(8,128)S(1)}, f32[8,128]{1,0:T(8,128)S(1)}) custom-call(bf16[4,48,512]{2,1,0:T(8,128)(2,1)S(1)} %get-tuple-element.137.refs_0_.refs_1_, bf16[512,1536]{1,0:T(8,128)(2,1)S(1)} %get-tuple-element.102.refs_3_.refs_11_.refs_1_, bf16[6,256,768]{2,1,0:T(8,128)(2,1)S(1)} %get-tuple-element.127.refs_2_, ...), custom_call_target="tpu_custom_call" | custom-call | flops 20000000 | bytes 94412 | tf_op jit(solution)/shard_map/grad_own/pallas_call | solution.py:659
  80.0 3.4 %collective-permute-done.11.refs_2_ = bf16[1,88,512]{2,1,0:T(8,128)(2,1)S(1)} collective-permute-done((bf16[1,88,512]{2,1,0:T(8,128)(2,1)S(1)}, bf16[1,88,512]{2,1,0:T(8,128)(2,1)S(1)}, u32[]{:S(2)}, u32[]{:S(2)}) %collective-permute-start.11) | collective-permute-done | bytes 90144 | tf_op jit(solution)/shard_map/ppermute | solution.py:639
  83.6 0.5 collective-permute-done.13.refs_2_
  84.2 1.6 %collective-permute-start.16 = (bf16[2,48,512]{2,1,0:T(8,128)(2,1)S(1)}, bf16[2,48,512]{2,1,0:T(8,128)(2,1)S(1)}, u32[]{:S(2)}, u32[]{:S(2)}) collective-permute-start(bf16[2,48,512]{2,1,0:T(8,128)(2,1)S(1)} %get-tuple-element.147), channel_id=1, source_target_pairs={{0,2},{1,3},{2,0},{3,1},{4,6},{5,7},{6,4},{7,5},{8,10},{9,11},{10,... | collective-permute-start | bytes 294920 | tf_op jit(solution)/shard_map/ppermute | solution.py:639
  85.8 0.9 collective-permute-start.3
  86.8 3.9 %collective-permute-done.16.refs_2_ = bf16[2,48,512]{2,1,0:T(8,128)(2,1)S(1)} collective-permute-done((bf16[2,48,512]{2,1,0:T(8,128)(2,1)S(1)}, bf16[2,48,512]{2,1,0:T(8,128)(2,1)S(1)}, u32[]{:S(2)}, u32[]{:S(2)}) %collective-permute-start.16) | collective-permute-done | bytes 98336 | tf_op jit(solution)/shard_map/ppermute | solution.py:639
  90.8 2.1 %collective-permute-start.23 = (bf16[4,88,512]{2,1,0:T(8,128)(2,1)S(1)}, bf16[4,88,512]{2,1,0:T(8,128)(2,1)S(1)}, u32[]{:S(2)}, u32[]{:S(2)}) collective-permute-start(bf16[4,88,512]{2,1,0:T(8,128)(2,1)S(1)} %join.9.refs_1_), channel_id=1, source_target_pairs={{0,17},{1,16},{2,19},{3,18},{4,21},{5,20},{6,23},{7,22},{8,25},{9,... | collective-permute-start | bytes 1081352 | tf_op jit(solution)/shard_map/ppermute | solution.py:639
  92.8 1.0 collective-permute-start.22
  93.9 0.4 collective-permute-start.21
  94.3 0.8 collective-permute-start.17
  95.1 10.1 %collective-permute-done.17.refs_2_ = bf16[1,48,512]{2,1,0:T(8,128)(2,1)S(1)} collective-permute-done((bf16[1,48,512]{2,1,0:T(8,128)(2,1)S(1)}, bf16[1,48,512]{2,1,0:T(8,128)(2,1)S(1)}, u32[]{:S(2)}, u32[]{:S(2)}) %collective-permute-start.17) | collective-permute-done | bytes 49184 | tf_op jit(solution)/shard_map/ppermute | solution.py:639
  105.2 5.0 %collective-permute-done.18.refs_1_ = bf16[1,48,512]{2,1,0:T(8,128)(2,1)S(1)} collective-permute-done((bf16[1,48,512]{2,1,0:T(8,128)(2,1)S(1)}, bf16[1,48,512]{2,1,0:T(8,128)(2,1)S(1)}, u32[]{:S(2)}, u32[]{:S(2)}) %collective-permute-start.18) | collective-permute-done | bytes 49184 | tf_op jit(solution)/shard_map/ppermute | solution.py:639
  110.3 1.9 %collective-permute-start.19 = (bf16[2,48,512]{2,1,0:T(8,128)(2,1)S(1)}, bf16[2,48,512]{2,1,0:T(8,128)(2,1)S(1)}, u32[]{:S(2)}, u32[]{:S(2)}) collective-permute-start(bf16[2,48,512]{2,1,0:T(8,128)(2,1)S(1)} %join.7.refs_1_), channel_id=1, source_target_pairs={{0,2},{1,3},{2,0},{3,1},{4,6},{5,7},{6,4},{7,5},{8,10},{9,11},{10,... | collective-permute-start | bytes 294920 | tf_op jit(solution)/shard_map/ppermute | solution.py:639
  112.2 2.8 %collective-permute-done.19.refs_2_ = bf16[2,48,512]{2,1,0:T(8,128)(2,1)S(1)} collective-permute-done((bf16[2,48,512]{2,1,0:T(8,128)(2,1)S(1)}, bf16[2,48,512]{2,1,0:T(8,128)(2,1)S(1)}, u32[]{:S(2)}, u32[]{:S(2)}) %collective-permute-start.19) | collective-permute-done | bytes 98336 | tf_op jit(solution)/shard_map/ppermute | solution.py:639
  115.2 2.2 %collective-permute-start.27 = (bf16[4,48,512]{2,1,0:T(8,128)(2,1)S(1)}, bf16[4,48,512]{2,1,0:T(8,128)(2,1)S(1)}, u32[]{:S(2)}, u32[]{:S(2)}) collective-permute-start(bf16[4,48,512]{2,1,0:T(8,128)(2,1)S(1)} %join.8.refs_0_.refs_2_), channel_id=1, source_target_pairs={{0,17},{1,16},{2,19},{3,18},{4,21},{5,20},{6,23},{7,22},{8,25},{9,... | collective-permute-start | bytes 589832 | tf_op jit(solution)/shard_map/ppermute | solution.py:639
  117.4 0.6 collective-permute-start.26
  117.9 0.8 collective-permute-start.25
  118.7 3.9 %finish.1 = (f32[6,256,512]{2,1,0:T(8,128)}, f32[8,128]{1,0:T(8,128)S(1)}) custom-call(bf16[16,88,512]{2,1,0:T(8,128)(2,1)S(1)} %join.10.refs_0_, bf16[6,256,512]{2,1,0:T(8,128)(2,1)S(1)} %copy-done, f32[6,256,512]{2,1,0:T(8,128)S(1)} %get-tuple-element.150.refs_2_, bf16[6,64,512]{2,1,0:T(8,128)(2,1)S(1)} %collective-permute-done.12.refs_0_.refs_3_, ...), custom_call_target="tpu_custom_call" | custom-call | flops 1000000 | bytes 118026 | tf_op jit(solution)/shard_map/finish/pallas_call | solution.py:659
  122.6 3.0 %place.2 = (f32[512,1536]{1,0:T(8,128)}, f32[512,512]{1,0:T(8,128)}, f32[768,512]{1,0:T(8,128)}, f32[1,512]{1,0:T(1,128)}, f32[8,128]{1,0:T(8,128)S(1)}) custom-call(bf16[16,88,512]{2,1,0:T(8,128)(2,1)S(1)} %join.10.refs_0_, bf16[16,88,512]{2,1,0:T(8,128)(2,1)S(1)} %collective-permute-done.24.refs_1_, bf16[512,1536]{1,0:T(8,128)(2,1)S(1)} %copy-done.2, ...), custom_call_target="tpu_custom_call" | custom-call | flops 10000 | bytes 102318 | tf_op jit(solution)/shard_map/place/pallas_call | solution.py:659
  125.6 1.8 %collective-permute-done.26.refs_4_ = bf16[4,48,512]{2,1,0:T(8,128)(2,1)S(1)} collective-permute-done((bf16[4,48,512]{2,1,0:T(8,128)(2,1)S(1)}, bf16[4,48,512]{2,1,0:T(8,128)(2,1)S(1)}, u32[]{:S(2)}, u32[]{:S(2)}) %collective-permute-start.26) | collective-permute-done | bytes 196640 | tf_op jit(solution)/shard_map/ppermute | solution.py:639
  127.8 2.3 %collective-permute-done.28.refs_1_ = bf16[16,48,512]{2,1,0:T(8,128)(2,1)S(1)} collective-permute-done((bf16[16,48,512]{2,1,0:T(8,128)(2,1)S(1)}, bf16[16,48,512]{2,1,0:T(8,128)(2,1)S(1)}, u32[]{:S(2)}, u32[]{:S(2)}) %collective-permute-start.28) | collective-permute-done | bytes 786464 | tf_op jit(solution)/shard_map/ppermute | solution.py:639
  130.0 2.0 %place.3 = (f32[512,1536]{1,0:T(8,128)}, f32[1,512]{1,0:T(1,128)}, f32[8,128]{1,0:T(8,128)}) custom-call(bf16[16,48,512]{2,1,0:T(8,128)(2,1)S(1)} %join.11.refs_0_, bf16[16,48,512]{2,1,0:T(8,128)(2,1)S(1)} %collective-permute-done.28.refs_1_, bf16[512,1536]{1,0:T(8,128)(2,1)S(1)} %get-tuple-element.86.refs_2_, ...), custom_call_target="tpu_custom_call" | custom-call | flops 10000 | bytes 62996 | tf_op jit(solution)/shard_map/place/pallas_call | solution.py:659
  (52 shorter events, 1.9 us)
Async XLA Ops:
  0.6 5.7 %copy-start = (bf16[6,256,512]{2,1,0:T(8,128)(2,1)S(1)}, bf16[6,256,512]{2,1,0:T(8,128)(2,1)}, u32[]{:S(2)}) copy-start(bf16[6,256,512]{2,1,0:T(8,128)(2,1)} %refs_1_.5) | copy-start | bytes 4718596
  2.6 19.8 %collective-permute-start = (bf16[6,64,512]{2,1,0:T(8,128)(2,1)S(1)}, bf16[6,64,512]{2,1,0:T(8,128)(2,1)S(1)}, u32[]{:S(2)}, u32[]{:S(2)}) collective-permute-start(bf16[6,64,512]{2,1,0:T(8,128)(2,1)S(1)} %get-tuple-element.100), channel_id=1, source_target_pairs={{0,1},{1,0},{2,3},{3,2},{4,5},{5,4},{6,7},{7,6},{8,9},{9,8},{10,11... | collective-permute-start | bytes 1179656 | tf_op jit(solution)/shard_map/ppermute | solution.py:625
  5.6 16.8 %collective-permute-start.1 = (bf16[6,64,512]{2,1,0:T(8,128)(2,1)S(1)}, bf16[6,64,512]{2,1,0:T(8,128)(2,1)S(1)}, u32[]{:S(2)}, u32[]{:S(2)}) collective-permute-start(bf16[6,64,512]{2,1,0:T(8,128)(2,1)S(1)} %get-tuple-element.101), channel_id=1, source_target_pairs={{1,2},{2,1},{3,4},{4,3},{5,6},{6,5},{9,10},{10,9},{11,12},{12,11},... | collective-permute-start | bytes 1179656 | tf_op jit(solution)/shard_map/ppermute | solution.py:625
  10.1 3.2 %copy-start.1 = (bf16[6,256,512]{2,1,0:T(8,128)(2,1)S(1)}, bf16[6,256,512]{2,1,0:T(8,128)(2,1)}, u32[]{:S(2)}) copy-start(bf16[6,256,512]{2,1,0:T(8,128)(2,1)} %refs_0_.11) | copy-start | bytes 4718596
  10.1 3.2 %copy-start.2 = (bf16[512,1536]{1,0:T(8,128)(2,1)S(1)}, bf16[512,1536]{1,0:T(8,128)(2,1)}, u32[]{:S(2)}) copy-start(bf16[512,1536]{1,0:T(8,128)(2,1)} %refs_2_.3) | copy-start | bytes 4718596
  10.1 3.2 %copy-start.3 = (bf16[768,512]{1,0:T(8,128)(2,1)S(1)}, bf16[768,512]{1,0:T(8,128)(2,1)}, u32[]{:S(2)}) copy-start(bf16[768,512]{1,0:T(8,128)(2,1)} %refs_5_.5) | copy-start | bytes 2359300
  10.1 3.2 %copy-start.4 = (bf16[512,512]{1,0:T(8,128)(2,1)S(1)}, bf16[512,512]{1,0:T(8,128)(2,1)}, u32[]{:S(2)}) copy-start(bf16[512,512]{1,0:T(8,128)(2,1)} %refs_3_.4) | copy-start | bytes 1572868
  10.1 3.2 %copy-start.5 = (f32[512]{0:T(512)S(1)}, f32[512]{0:T(512)}, u32[]{:S(2)}) copy-start(f32[512]{0:T(512)} %param.18) | copy-start | bytes 6148
  36.5 3.3 %collective-permute-start.2 = (bf16[16,88,512]{2,1,0:T(8,128)(2,1)S(1)}, bf16[16,88,512]{2,1,0:T(8,128)(2,1)S(1)}, u32[]{:S(2)}, u32[]{:S(2)}) collective-permute-start(bf16[16,88,512]{2,1,0:T(8,128)(2,1)S(1)} %get-tuple-element.118), channel_id=1, source_target_pairs={{0,8},{1,9},{2,10},{3,11},{4,12},{5,13},{6,14},{7,15},{8,0},{9,1},... | collective-permute-start | bytes 4325384 | tf_op jit(solution)/shard_map/ppermute | solution.py:639
  40.1 23.2 %collective-permute-start.4 = (bf16[4,88,512]{2,1,0:T(8,128)(2,1)S(1)}, bf16[4,88,512]{2,1,0:T(8,128)(2,1)S(1)}, u32[]{:S(2)}, u32[]{:S(2)}) collective-permute-start(bf16[4,88,512]{2,1,0:T(8,128)(2,1)S(1)} %get-tuple-element.131), channel_id=1, source_target_pairs={{0,1},{1,0},{2,3},{3,2},{4,5},{5,4},{6,7},{7,6},{8,9},{9,8},{10,11... | collective-permute-start | bytes 1081352 | tf_op jit(solution)/shard_map/ppermute | solution.py:639
  44.5 18.9 %collective-permute-start.5 = (bf16[4,88,512]{2,1,0:T(8,128)(2,1)S(1)}, bf16[4,88,512]{2,1,0:T(8,128)(2,1)S(1)}, u32[]{:S(2)}, u32[]{:S(2)}) collective-permute-start(bf16[4,88,512]{2,1,0:T(8,128)(2,1)S(1)} %get-tuple-element.132), channel_id=1, source_target_pairs={{0,16},{1,17},{2,18},{3,19},{4,20},{5,21},{6,22},{7,23},{8,24},{9,... | collective-permute-start | bytes 1081352 | tf_op jit(solution)/shard_map/ppermute | solution.py:639
  45.9 17.5 %collective-permute-start.6 = (bf16[4,88,512]{2,1,0:T(8,128)(2,1)S(1)}, bf16[4,88,512]{2,1,0:T(8,128)(2,1)S(1)}, u32[]{:S(2)}, u32[]{:S(2)}) collective-permute-start(bf16[4,88,512]{2,1,0:T(8,128)(2,1)S(1)} %get-tuple-element.133), channel_id=1, source_target_pairs={{0,17},{1,16},{2,19},{3,18},{4,21},{5,20},{6,23},{7,22},{8,25},{9,... | collective-permute-start | bytes 1081352 | tf_op jit(solution)/shard_map/ppermute | solution.py:639
  63.9 6.5 %collective-permute-start.7 = (bf16[16,48,512]{2,1,0:T(8,128)(2,1)S(1)}, bf16[16,48,512]{2,1,0:T(8,128)(2,1)S(1)}, u32[]{:S(2)}, u32[]{:S(2)}) collective-permute-start(bf16[16,48,512]{2,1,0:T(8,128)(2,1)S(1)} %get-tuple-element.136), channel_id=1, source_target_pairs={{0,8},{1,9},{2,10},{3,11},{4,12},{5,13},{6,14},{7,15},{8,0},{9,1},... | collective-permute-start | bytes 2359304 | tf_op jit(solution)/shard_map/ppermute | solution.py:639
  63.9 19.7 %collective-permute-start.12 = (bf16[6,64,512]{2,1,0:T(8,128)(2,1)S(1)}, bf16[6,64,512]{2,1,0:T(8,128)(2,1)S(1)}, u32[]{:S(2)}, u32[]{:S(2)}) collective-permute-start(bf16[6,64,512]{2,1,0:T(8,128)(2,1)S(1)} %get-tuple-element.142), channel_id=1, source_target_pairs={{0,1},{1,0},{2,3},{3,2},{4,5},{5,4},{6,7},{7,6},{8,9},{9,8},{10,11... | collective-permute-start | bytes 1179656 | tf_op jit(solution)/shard_map/ppermute | solution.py:625
  66.0 8.6 %collective-permute-start.8 = (bf16[1,88,512]{2,1,0:T(8,128)(2,1)S(1)}, bf16[1,88,512]{2,1,0:T(8,128)(2,1)S(1)}, u32[]{:S(2)}, u32[]{:S(2)}) collective-permute-start(bf16[1,88,512]{2,1,0:T(8,128)(2,1)S(1)} %get-tuple-element.139), channel_id=1, source_target_pairs={{0,4},{1,5},{2,6},{3,7},{4,0},{5,1},{6,2},{7,3},{8,12},{9,13},{10,... | collective-permute-start | bytes 270344 | tf_op jit(solution)/shard_map/ppermute | solution.py:639
  68.5 7.5 %collective-permute-start.9 = (bf16[1,88,512]{2,1,0:T(8,128)(2,1)S(1)}, bf16[1,88,512]{2,1,0:T(8,128)(2,1)S(1)}, u32[]{:S(2)}, u32[]{:S(2)}) collective-permute-start(bf16[1,88,512]{2,1,0:T(8,128)(2,1)S(1)} %get-tuple-element.140), channel_id=1, source_target_pairs={{0,2},{1,3},{2,0},{3,1},{4,6},{5,7},{6,4},{7,5},{8,10},{9,11},{10,... | collective-permute-start | bytes 270344 | tf_op jit(solution)/shard_map/ppermute | solution.py:639
  68.5 8.0 %collective-permute-start.10 = (bf16[1,88,512]{2,1,0:T(8,128)(2,1)S(1)}, bf16[1,88,512]{2,1,0:T(8,128)(2,1)S(1)}, u32[]{:S(2)}, u32[]{:S(2)}) collective-permute-start(bf16[1,88,512]{2,1,0:T(8,128)(2,1)S(1)} %get-tuple-element.141), channel_id=1, source_target_pairs={{0,6},{1,7},{2,4},{3,5},{4,2},{5,3},{6,0},{7,1},{8,14},{9,15},{10,... | collective-permute-start | bytes 270344 | tf_op jit(solution)/shard_map/ppermute | solution.py:639
  70.5 13.6 %collective-permute-start.13 = (bf16[4,48,512]{2,1,0:T(8,128)(2,1)S(1)}, bf16[4,48,512]{2,1,0:T(8,128)(2,1)S(1)}, u32[]{:S(2)}, u32[]{:S(2)}) collective-permute-start(bf16[4,48,512]{2,1,0:T(8,128)(2,1)S(1)} %get-tuple-element.143), channel_id=1, source_target_pairs={{0,1},{1,0},{2,3},{3,2},{4,5},{5,4},{6,7},{7,6},{8,9},{9,8},{10,11... | collective-permute-start | bytes 589832 | tf_op jit(solution)/shard_map/ppermute | solution.py:639
  74.6 9.5 %collective-permute-start.14 = (bf16[4,48,512]{2,1,0:T(8,128)(2,1)S(1)}, bf16[4,48,512]{2,1,0:T(8,128)(2,1)S(1)}, u32[]{:S(2)}, u32[]{:S(2)}) collective-permute-start(bf16[4,48,512]{2,1,0:T(8,128)(2,1)S(1)} %get-tuple-element.144), channel_id=1, source_target_pairs={{0,16},{1,17},{2,18},{3,19},{4,20},{5,21},{6,22},{7,23},{8,24},{9,... | collective-permute-start | bytes 589832 | tf_op jit(solution)/shard_map/ppermute | solution.py:639
  76.0 8.1 %collective-permute-start.15 = (bf16[4,48,512]{2,1,0:T(8,128)(2,1)S(1)}, bf16[4,48,512]{2,1,0:T(8,128)(2,1)S(1)}, u32[]{:S(2)}, u32[]{:S(2)}) collective-permute-start(bf16[4,48,512]{2,1,0:T(8,128)(2,1)S(1)} %get-tuple-element.145), channel_id=1, source_target_pairs={{0,17},{1,16},{2,19},{3,18},{4,21},{5,20},{6,23},{7,22},{8,25},{9,... | collective-permute-start | bytes 589832 | tf_op jit(solution)/shard_map/ppermute | solution.py:639
  76.6 6.8 %collective-permute-start.11 = (bf16[1,88,512]{2,1,0:T(8,128)(2,1)S(1)}, bf16[1,88,512]{2,1,0:T(8,128)(2,1)S(1)}, u32[]{:S(2)}, u32[]{:S(2)}) collective-permute-start(bf16[1,88,512]{2,1,0:T(8,128)(2,1)S(1)} %add.10.refs_1_), channel_id=1, source_target_pairs={{0,4},{1,5},{2,6},{3,7},{4,0},{5,1},{6,2},{7,3},{8,12},{9,13},{10,... | collective-permute-start | bytes 270344 | tf_op jit(solution)/shard_map/ppermute | solution.py:639
  83.4 7.3 %collective-permute-start.20 = (bf16[2,88,512]{2,1,0:T(8,128)(2,1)S(1)}, bf16[2,88,512]{2,1,0:T(8,128)(2,1)S(1)}, u32[]{:S(2)}, u32[]{:S(2)}) collective-permute-start(bf16[2,88,512]{2,1,0:T(8,128)(2,1)S(1)} %join.6.refs_0_.refs_1_), channel_id=1, source_target_pairs={{0,2},{1,3},{2,0},{3,1},{4,6},{5,7},{6,4},{7,5},{8,10},{9,11},{10,... | collective-permute-start | bytes 540680 | tf_op jit(solution)/shard_map/ppermute | solution.py:639
  84.2 6.5 %collective-permute-start.16 = (bf16[2,48,512]{2,1,0:T(8,128)(2,1)S(1)}, bf16[2,48,512]{2,1,0:T(8,128)(2,1)S(1)}, u32[]{:S(2)}, u32[]{:S(2)}) collective-permute-start(bf16[2,48,512]{2,1,0:T(8,128)(2,1)S(1)} %get-tuple-element.147), channel_id=1, source_target_pairs={{0,2},{1,3},{2,0},{3,1},{4,6},{5,7},{6,4},{7,5},{8,10},{9,11},{10,... | collective-permute-start | bytes 294920 | tf_op jit(solution)/shard_map/ppermute | solution.py:639
  85.8 26.3 %collective-permute-start.3 = (bf16[6,64,512]{2,1,0:T(8,128)(2,1)S(1)}, bf16[6,64,512]{2,1,0:T(8,128)(2,1)S(1)}, u32[]{:S(2)}, u32[]{:S(2)}) collective-permute-start(bf16[6,64,512]{2,1,0:T(8,128)(2,1)S(1)} %get-tuple-element.124), channel_id=1, source_target_pairs={{1,2},{2,1},{3,4},{4,3},{5,6},{6,5},{9,10},{10,9},{11,12},{12,11},... | collective-permute-start | bytes 1179656 | tf_op jit(solution)/shard_map/ppermute | solution.py:625
  90.8 24.2 %collective-permute-start.23 = (bf16[4,88,512]{2,1,0:T(8,128)(2,1)S(1)}, bf16[4,88,512]{2,1,0:T(8,128)(2,1)S(1)}, u32[]{:S(2)}, u32[]{:S(2)}) collective-permute-start(bf16[4,88,512]{2,1,0:T(8,128)(2,1)S(1)} %join.9.refs_1_), channel_id=1, source_target_pairs={{0,17},{1,16},{2,19},{3,18},{4,21},{5,20},{6,23},{7,22},{8,25},{9,... | collective-permute-start | bytes 1081352 | tf_op jit(solution)/shard_map/ppermute | solution.py:639
  92.8 22.1 %collective-permute-start.22 = (bf16[4,88,512]{2,1,0:T(8,128)(2,1)S(1)}, bf16[4,88,512]{2,1,0:T(8,128)(2,1)S(1)}, u32[]{:S(2)}, u32[]{:S(2)}) collective-permute-start(bf16[4,88,512]{2,1,0:T(8,128)(2,1)S(1)} %join.9.refs_1_), channel_id=1, source_target_pairs={{0,16},{1,17},{2,18},{3,19},{4,20},{5,21},{6,22},{7,23},{8,24},{9,... | collective-permute-start | bytes 1081352 | tf_op jit(solution)/shard_map/ppermute | solution.py:639
  93.9 21.1 %collective-permute-start.21 = (bf16[4,88,512]{2,1,0:T(8,128)(2,1)S(1)}, bf16[4,88,512]{2,1,0:T(8,128)(2,1)S(1)}, u32[]{:S(2)}, u32[]{:S(2)}) collective-permute-start(bf16[4,88,512]{2,1,0:T(8,128)(2,1)S(1)} %join.9.refs_1_), channel_id=1, source_target_pairs={{0,1},{1,0},{2,3},{3,2},{4,5},{5,4},{6,7},{7,6},{8,9},{9,8},{10,11... | collective-permute-start | bytes 1081352 | tf_op jit(solution)/shard_map/ppermute | solution.py:639
  94.3 10.8 %collective-permute-start.17 = (bf16[1,48,512]{2,1,0:T(8,128)(2,1)S(1)}, bf16[1,48,512]{2,1,0:T(8,128)(2,1)S(1)}, u32[]{:S(2)}, u32[]{:S(2)}) collective-permute-start(bf16[1,48,512]{2,1,0:T(8,128)(2,1)S(1)} %get-tuple-element.149), channel_id=1, source_target_pairs={{0,4},{1,5},{2,6},{3,7},{4,0},{5,1},{6,2},{7,3},{8,12},{9,13},{10,... | collective-permute-start | bytes 147464 | tf_op jit(solution)/shard_map/ppermute | solution.py:639
  105.2 5.1 %collective-permute-start.18 = (bf16[1,48,512]{2,1,0:T(8,128)(2,1)S(1)}, bf16[1,48,512]{2,1,0:T(8,128)(2,1)S(1)}, u32[]{:S(2)}, u32[]{:S(2)}) collective-permute-start(bf16[1,48,512]{2,1,0:T(8,128)(2,1)S(1)} %add.13.refs_0_), channel_id=1, source_target_pairs={{0,4},{1,5},{2,6},{3,7},{4,0},{5,1},{6,2},{7,3},{8,12},{9,13},{10,... | collective-permute-start | bytes 147464 | tf_op jit(solution)/shard_map/ppermute | solution.py:639
  110.3 4.7 %collective-permute-start.19 = (bf16[2,48,512]{2,1,0:T(8,128)(2,1)S(1)}, bf16[2,48,512]{2,1,0:T(8,128)(2,1)S(1)}, u32[]{:S(2)}, u32[]{:S(2)}) collective-permute-start(bf16[2,48,512]{2,1,0:T(8,128)(2,1)S(1)} %join.7.refs_1_), channel_id=1, source_target_pairs={{0,2},{1,3},{2,0},{3,1},{4,6},{5,7},{6,4},{7,5},{8,10},{9,11},{10,... | collective-permute-start | bytes 294920 | tf_op jit(solution)/shard_map/ppermute | solution.py:639
  115.1 7.5 %collective-permute-start.24 = (bf16[16,88,512]{2,1,0:T(8,128)(2,1)S(1)}, bf16[16,88,512]{2,1,0:T(8,128)(2,1)S(1)}, u32[]{:S(2)}, u32[]{:S(2)}) collective-permute-start(bf16[16,88,512]{2,1,0:T(8,128)(2,1)S(1)} %join.10.refs_0_), channel_id=1, source_target_pairs={{0,8},{1,9},{2,10},{3,11},{4,12},{5,13},{6,14},{7,15},{8,0},{9,1},... | collective-permute-start | bytes 4325384 | tf_op jit(solution)/shard_map/ppermute | solution.py:639
  115.2 10.5 %collective-permute-start.27 = (bf16[4,48,512]{2,1,0:T(8,128)(2,1)S(1)}, bf16[4,48,512]{2,1,0:T(8,128)(2,1)S(1)}, u32[]{:S(2)}, u32[]{:S(2)}) collective-permute-start(bf16[4,48,512]{2,1,0:T(8,128)(2,1)S(1)} %join.8.refs_0_.refs_2_), channel_id=1, source_target_pairs={{0,17},{1,16},{2,19},{3,18},{4,21},{5,20},{6,23},{7,22},{8,25},{9,... | collective-permute-start | bytes 589832 | tf_op jit(solution)/shard_map/ppermute | solution.py:639
  117.4 10.0 %collective-permute-start.26 = (bf16[4,48,512]{2,1,0:T(8,128)(2,1)S(1)}, bf16[4,48,512]{2,1,0:T(8,128)(2,1)S(1)}, u32[]{:S(2)}, u32[]{:S(2)}) collective-permute-start(bf16[4,48,512]{2,1,0:T(8,128)(2,1)S(1)} %join.8.refs_0_.refs_2_), channel_id=1, source_target_pairs={{0,16},{1,17},{2,18},{3,19},{4,20},{5,21},{6,22},{7,23},{8,24},{9,... | collective-permute-start | bytes 589832 | tf_op jit(solution)/shard_map/ppermute | solution.py:639
  117.9 9.7 %collective-permute-start.25 = (bf16[4,48,512]{2,1,0:T(8,128)(2,1)S(1)}, bf16[4,48,512]{2,1,0:T(8,128)(2,1)S(1)}, u32[]{:S(2)}, u32[]{:S(2)}) collective-permute-start(bf16[4,48,512]{2,1,0:T(8,128)(2,1)S(1)} %join.8.refs_0_.refs_2_), channel_id=1, source_target_pairs={{0,1},{1,0},{2,3},{3,2},{4,5},{5,4},{6,7},{7,6},{8,9},{9,8},{10,11... | collective-permute-start | bytes 589832 | tf_op jit(solution)/shard_map/ppermute | solution.py:639
  127.7 2.4 %collective-permute-start.28 = (bf16[16,48,512]{2,1,0:T(8,128)(2,1)S(1)}, bf16[16,48,512]{2,1,0:T(8,128)(2,1)S(1)}, u32[]{:S(2)}, u32[]{:S(2)}) collective-permute-start(bf16[16,48,512]{2,1,0:T(8,128)(2,1)S(1)} %join.11.refs_0_), channel_id=1, source_target_pairs={{0,8},{1,9},{2,10},{3,11},{4,12},{5,13},{6,14},{7,15},{8,0},{9,1},... | collective-permute-start | bytes 2359304 | tf_op jit(solution)/shard_map/ppermute | solution.py:639

commit v3 on v2

--- a/solution.py
+++ b/solution.py
@@ -186,7 +186,7 @@
 
 def halo_kernel(inner_ref, other_ref, weight_ref, gain_ref, angles_ref, normed_ref, keys_ref, values_ref):
     rows, win, width = inner_ref.shape
-    pair = 3
+    pair = 6
     span = angles_ref.shape[1]
     cosine = jnp.concatenate([angles_ref[0, :win], angles_ref[0, span - win :]] * pair)
     sines = jnp.concatenate([angles_ref[1, :win], angles_ref[1, span - win :]] * pair)
@@ -924,7 +924,7 @@
     line_one0 = swap_rest(line_one0)
     plane_two = add_up([chip_two[0], *from_plane_rs], cut(chip_two[0], 2), after=[inner_grad])
     line_one6 = join([line_one0, swap(line_one0, z=2)], after=[done_own])
-    near_two = add_up([plane_two[0], swap(plane_two[1], z=1)], cut(plane_two[0], 2), after=[line_one6])
+    near_two = add_up([plane_two[0], swap(plane_two[1], z=1)], cut(plane_two[0], 2), after=[])
     line_one7 = join([line_one6, swap(line_one6, z=1)], after=[near_two[0]])
     from_plane = swap_plane([line_one7] * 4)
     (line_two0,) = add_up([near_two[0], swap(near_two[1], z=2)], cut(near_two[0], 1), after=[line_one6])

time: 132 us -> 132 us (level)
  no operation moved by 1% of the time
where the time goes in v3:
time: 132 us
  Pallas kernels  65 us (49%)
  waiting for transfers between devices  34.8 us (26%)
  starting transfers between devices  30.9 us (23%)
    pallas_call x29, Pallas kernels, call(): pl.pallas_call(body, out_shape=outs, in_specs=[pl.BlockSpec(memory_space=...  63 us
    ppermute x25, waiting for transfers between devices, swap(): return lax.ppermute(values, ('dp', 'seq'), swap_route(core, x, y, z, rest))  34.8 us
    ppermute x25, starting transfers between devices, swap(): return lax.ppermute(values, ('dp', 'seq'), swap_route(core, x, y, z, rest))  24.3 us
    ppermute x2, starting transfers between devices, to_neighbours(): lax.ppermute(inner, 'seq', pairs)  5.05 us
  transfers between devices with their start and end apart: 29, of which 12 were waited for; matrix products, arithmetic and copies ran while one was open for 0% of the time, Pallas kernels for 35%

profile of v3, /device:TPU:0, one launch (start us, length us, event | category | flops | bytes accessed | tf_op | source)
XLA Modules:
  0.0 131.7 jit_solution(18054523321112751056)
XLA Ops:
  0.6 1.9 %load.1 = (bf16[6,64,512]{2,1,0:T(8,128)(2,1)S(1)}, bf16[6,64,512]{2,1,0:T(8,128)(2,1)S(1)}, s32[6,16]{1,0:T(8,128)S(1)}, f32[1,512]{1,0:T(1,128)S(1)}, bf16[512...) custom-call(bf16[6,256,512]{2,1,0:T(8,128)(2,1)} %refs_1_.5, s32[6,16]{1,0:T(8,128)} %refs_0_.6, ...), custom_call_target="tpu_custom_call" | custom-call | tf_op jit(solution)/shard_map/load/pallas_call | solution.py:726
  2.6 3.0 %collective-permute-start = (bf16[6,64,512]{2,1,0:T(8,128)(2,1)S(1)}, bf16[6,64,512]{2,1,0:T(8,128)(2,1)S(1)}, u32[]{:S(2)}, u32[]{:S(2)}) collective-permute-start(bf16[6,64,512]{2,1,0:T(8,128)(2,1)S(1)} %get-tuple-element.100), channel_id=1, source_target_pairs={{0,1},{1,0},{2,3},{3,2},{4,5},{5,4},{6,7},{7,6},{8,9},{9,8},{10,11... | collective-permute-start | bytes 1179656 | tf_op jit(solution)/shard_map/ppermute | solution.py:625
  5.6 0.7 collective-permute-start.1
  6.3 3.7 %project.1 = (bf16[6,256,512]{2,1,0:T(8,128)(2,1)S(1)}, bf16[6,256,512]{2,1,0:T(8,128)(2,1)S(1)}, bf16[6,256,512]{2,1,0:T(8,128)(2,1)S(1)}, bf16[6,256,512]{2,1,...) custom-call(bf16[6,256,512]{2,1,0:T(8,128)(2,1)S(1)} %copy-done, ...), custom_call_target="tpu_custom_call" | custom-call | flops 30000000 | bytes 118255 | tf_op jit(solution)/shard_map/project/pallas_call | solution.py:659
  10.1 3.2 %attend_mid.1 = (bf16[6,128,512]{2,1,0:T(8,128)(2,1)S(1)}, f32[6,2,256,512]{3,2,1,0:T(8,128)S(1)}) custom-call(bf16[6,256,512]{2,1,0:T(8,128)(2,1)S(1)} %get-tuple-element.90.refs_0_.refs_1_, bf16[6,256,512]{2,1,0:T(8,128)(2,1)S(1)} %get-tuple-element.91.refs_1_.refs_2_, bf16[6,256,512]{2,1,0:T(8,128)(2,1)S(1)} %get-tuple-element.92.refs_2_.refs_3_, ...), custom_call_target="tpu_custom_call" | custom-call | flops 20000000 | bytes 118149 | tf_op jit(solution)/shard_map/attend_mid/pallas_call | solution.py:659
  13.3 6.6 %dense_mid.1 = (f32[6,128,512]{2,1,0:T(8,128)S(1)}, bf16[6,128,512]{2,1,0:T(8,128)(2,1)S(1)}, bf16[6,128,768]{2,1,0:T(8,128)(2,1)S(1)}, bf16[6,128,1536]{2,1,0:T...) custom-call(bf16[6,256,512]{2,1,0:T(8,128)(2,1)S(1)} %copy-done, ...), custom_call_target="tpu_custom_call" | custom-call | flops 50000000 | bytes 158617 | tf_op jit(solution)/shard_map/dense_mid/pallas_call | solution.py:659
  19.9 2.4 %begin.1 = (bf16[512,1536]{1,0:T(8,128)(2,1)S(1)}, bf16[768,512]{1,0:T(8,128)(2,1)S(1)}, bf16[512,512]{1,0:T(8,128)(2,1)S(1)}) custom-call(bf16[6,256,512]{2,1,0:T(8,128)(2,1)S(1)} %copy-done.1, bf16[6,128,512]{2,1,0:T(8,128)(2,1)S(1)} %get-tuple-element.95.refs_1_, bf16[6,128,1536]{2,1,0:T(8,128)(2,1)S(1)} %get-tuple-element.96.refs_2_, ...), custom_call_target="tpu_custom_call" | custom-call | flops 30000000 | bytes 103546 | tf_op jit(solution)/shard_map/begin/pallas_call | solution.py:659
  22.4 1.4 %halo.1 = (bf16[6,128,512]{2,1,0:T(8,128)(2,1)S(1)}, bf16[6,128,512]{2,1,0:T(8,128)(2,1)S(1)}, bf16[6,128,512]{2,1,0:T(8,128)(2,1)S(1)}) custom-call(bf16[512,512]{1,0:T(8,128)(2,1)S(1)} %get-tuple-element.99.refs_0_.refs_8_, bf16[6,64,512]{2,1,0:T(8,128)(2,1)S(1)} %collective-permute-done.refs_1_, bf16[6,64,512]{2,1,0:T(8,128)(2,1)S(1)} %collective-permute-done.1.refs_2_, ...), custom_call_target="tpu_custom_call" | custom-call | flops 10000000 | bytes 51138 | tf_op jit(solution)/shard_map/halo/pallas_call | solution.py:659
  23.8 2.9 %attend_out.1 = (bf16[6,128,512]{2,1,0:T(8,128)(2,1)S(1)}, f32[6,2,2,192,256]{4,3,2,1,0:T(8,128)S(1)}) custom-call(bf16[6,256,512]{2,1,0:T(8,128)(2,1)S(1)} %get-tuple-element.90.refs_0_.refs_1_, bf16[6,256,512]{2,1,0:T(8,128)(2,1)S(1)} %get-tuple-element.91.refs_1_.refs_2_, bf16[6,256,512]{2,1,0:T(8,128)(2,1)S(1)} %get-tuple-element.92.refs_2_.refs_3_, ...), custom_call_target="tpu_custom_call" | custom-call | flops 20000000 | bytes 118149 | tf_op jit(solution)/shard_map/attend_out/pallas_call | solution.py:659
  26.7 6.7 %dense_out.1 = (f32[6,128,512]{2,1,0:T(8,128)S(1)}, bf16[6,128,512]{2,1,0:T(8,128)(2,1)S(1)}, bf16[6,128,768]{2,1,0:T(8,128)(2,1)S(1)}, bf16[6,128,1536]{2,1,0:T...) custom-call(bf16[6,256,512]{2,1,0:T(8,128)(2,1)S(1)} %copy-done, ...), custom_call_target="tpu_custom_call" | custom-call | flops 50000000 | bytes 158617 | tf_op jit(solution)/shard_map/dense_out/pallas_call | solution.py:659
  33.4 2.8 %weights.1 = (bf16[16,88,512]{2,1,0:T(8,128)(2,1)S(1)}, bf16[16,88,512]{2,1,0:T(8,128)(2,1)S(1)}) custom-call(bf16[6,256,512]{2,1,0:T(8,128)(2,1)S(1)} %copy-done.1, bf16[6,128,512]{2,1,0:T(8,128)(2,1)S(1)} %get-tuple-element.107.refs_1_, bf16[6,128,1536]{2,1,0:T(8,128)(2,1)S(1)} %get-tuple-element.108.refs_2_, ...), custom_call_target="tpu_custom_call" | custom-call | flops 50000000 | bytes 132382 | tf_op jit(solution)/shard_map/weights/pallas_call | solution.py:659
  36.3 2.7 %result.1 = (bf16[6,256,512]{2,1,0:T(8,128)(2,1)}, f32[8,128]{1,0:T(8,128)S(1)}) custom-call(bf16[16,88,512]{2,1,0:T(8,128)(2,1)S(1)} %get-tuple-element.113.refs_0_.refs_1_, f32[6,128,512]{2,1,0:T(8,128)S(1)} %get-tuple-element.114.refs_1_, f32[6,128,512]{2,1,0:T(8,128)S(1)} %get-tuple-element.115.refs_2_, ...), custom_call_target="tpu_custom_call" | custom-call | flops 20000000 | bytes 78684 | tf_op jit(solution)/shard_map/result/pallas_call | solution.py:659
  39.0 0.5 collective-permute-done.2.refs_2_
  39.5 0.3 add.7
  39.8 4.3 %collective-permute-start.4 = (bf16[4,88,512]{2,1,0:T(8,128)(2,1)S(1)}, bf16[4,88,512]{2,1,0:T(8,128)(2,1)S(1)}, u32[]{:S(2)}, u32[]{:S(2)}) collective-permute-start(bf16[4,88,512]{2,1,0:T(8,128)(2,1)S(1)} %get-tuple-element.131), channel_id=1, source_target_pairs={{0,1},{1,0},{2,3},{3,2},{4,5},{5,4},{6,7},{7,6},{8,9},{9,8},{10,11... | collective-permute-start | bytes 1081352 | tf_op jit(solution)/shard_map/ppermute | solution.py:639
  44.2 1.5 %collective-permute-start.5 = (bf16[4,88,512]{2,1,0:T(8,128)(2,1)S(1)}, bf16[4,88,512]{2,1,0:T(8,128)(2,1)S(1)}, u32[]{:S(2)}, u32[]{:S(2)}) collective-permute-start(bf16[4,88,512]{2,1,0:T(8,128)(2,1)S(1)} %get-tuple-element.132), channel_id=1, source_target_pairs={{0,16},{1,17},{2,18},{3,19},{4,20},{5,21},{6,22},{7,23},{8,24},{9,... | collective-permute-start | bytes 1081352 | tf_op jit(solution)/shard_map/ppermute | solution.py:639
  45.7 13.6 %backward.1 = (bf16[6,256,768]{2,1,0:T(8,128)(2,1)S(1)}, bf16[6,128,512]{2,1,0:T(8,128)(2,1)S(1)}, bf16[6,256,768]{2,1,0:T(8,128)(2,1)S(1)}, bf16[6,128,512]{2,1...) custom-call(bf16[4,88,512]{2,1,0:T(8,128)(2,1)S(1)} %get-tuple-element.119.refs_0_.refs_1_, ...), custom_call_target="tpu_custom_call" | custom-call | flops 120000000 | bytes 279183 | tf_op jit(solution)/shard_map/backward/pallas_call | solution.py:659
  59.4 3.7 %weight_in.1.refs_0_.refs_1_ = bf16[512,1536]{1,0:T(8,128)(2,1)S(1)} custom-call(bf16[6,256,512]{2,1,0:T(8,128)(2,1)S(1)} %get-tuple-element.125.refs_0_, bf16[6,128,512]{2,1,0:T(8,128)(2,1)S(1)} %get-tuple-element.126.refs_1_, bf16[6,256,768]{2,1,0:T(8,128)(2,1)S(1)} %get-tuple-element.127.refs_2_, bf16[6,128,512]{2,1,0:T(8,128)(2,1)S(1)} %get-tuple-element.128.refs_3_, ...), custom_call_target="tpu_custom_call" | custom-call | flops 40000000 | bytes 102236 | tf_op jit(solution)/shard_map/weight_in/pallas_call | solution.py:659
  63.3 0.3 split.1
  63.7 2.0 %collective-permute-start.12 = (bf16[6,64,512]{2,1,0:T(8,128)(2,1)S(1)}, bf16[6,64,512]{2,1,0:T(8,128)(2,1)S(1)}, u32[]{:S(2)}, u32[]{:S(2)}) collective-permute-start(bf16[6,64,512]{2,1,0:T(8,128)(2,1)S(1)} %get-tuple-element.142), channel_id=1, source_target_pairs={{0,1},{1,0},{2,3},{3,2},{4,5},{5,4},{6,7},{7,6},{8,9},{9,8},{10,11... | collective-permute-start | bytes 1179656 | tf_op jit(solution)/shard_map/ppermute | solution.py:625
  65.7 2.6 %collective-permute-start.8 = (bf16[1,88,512]{2,1,0:T(8,128)(2,1)S(1)}, bf16[1,88,512]{2,1,0:T(8,128)(2,1)S(1)}, u32[]{:S(2)}, u32[]{:S(2)}) collective-permute-start(bf16[1,88,512]{2,1,0:T(8,128)(2,1)S(1)} %get-tuple-element.139), channel_id=1, source_target_pairs={{0,4},{1,5},{2,6},{3,7},{4,0},{5,1},{6,2},{7,3},{8,12},{9,13},{10,... | collective-permute-start | bytes 270344 | tf_op jit(solution)/shard_map/ppermute | solution.py:639
  68.2 1.8 %collective-permute-start.10 = (bf16[1,88,512]{2,1,0:T(8,128)(2,1)S(1)}, bf16[1,88,512]{2,1,0:T(8,128)(2,1)S(1)}, u32[]{:S(2)}, u32[]{:S(2)}) collective-permute-start(bf16[1,88,512]{2,1,0:T(8,128)(2,1)S(1)} %get-tuple-element.141), channel_id=1, source_target_pairs={{0,6},{1,7},{2,4},{3,5},{4,2},{5,3},{6,0},{7,1},{8,14},{9,15},{10,... | collective-permute-start | bytes 270344 | tf_op jit(solution)/shard_map/ppermute | solution.py:639
  70.4 3.9 %collective-permute-done.8.refs_1_ = bf16[1,88,512]{2,1,0:T(8,128)(2,1)S(1)} collective-permute-done((bf16[1,88,512]{2,1,0:T(8,128)(2,1)S(1)}, bf16[1,88,512]{2,1,0:T(8,128)(2,1)S(1)}, u32[]{:S(2)}, u32[]{:S(2)}) %collective-permute-start.8) | collective-permute-done | bytes 90144 | tf_op jit(solution)/shard_map/ppermute | solution.py:639
  74.3 1.5 %collective-permute-start.14 = (bf16[4,48,512]{2,1,0:T(8,128)(2,1)S(1)}, bf16[4,48,512]{2,1,0:T(8,128)(2,1)S(1)}, u32[]{:S(2)}, u32[]{:S(2)}) collective-permute-start(bf16[4,48,512]{2,1,0:T(8,128)(2,1)S(1)} %get-tuple-element.144), channel_id=1, source_target_pairs={{0,16},{1,17},{2,18},{3,19},{4,20},{5,21},{6,22},{7,23},{8,24},{9,... | collective-permute-start | bytes 589832 | tf_op jit(solution)/shard_map/ppermute | solution.py:639
  75.7 0.5 collective-permute-done.10.refs_3_
  76.3 0.4 collective-permute-start.11
  76.7 3.0 %grad_own.1 = (f32[6,256,512]{2,1,0:T(8,128)S(1)}, f32[8,128]{1,0:T(8,128)S(1)}) custom-call(bf16[4,48,512]{2,1,0:T(8,128)(2,1)S(1)} %get-tuple-element.137.refs_0_.refs_1_, bf16[512,1536]{1,0:T(8,128)(2,1)S(1)} %get-tuple-element.102.refs_3_.refs_11_.refs_1_, bf16[6,256,768]{2,1,0:T(8,128)(2,1)S(1)} %get-tuple-element.127.refs_2_, ...), custom_call_target="tpu_custom_call" | custom-call | flops 20000000 | bytes 94412 | tf_op jit(solution)/shard_map/grad_own/pallas_call | solution.py:659
  79.7 3.4 %collective-permute-done.11.refs_2_ = bf16[1,88,512]{2,1,0:T(8,128)(2,1)S(1)} collective-permute-done((bf16[1,88,512]{2,1,0:T(8,128)(2,1)S(1)}, bf16[1,88,512]{2,1,0:T(8,128)(2,1)S(1)}, u32[]{:S(2)}, u32[]{:S(2)}) %collective-permute-start.11) | collective-permute-done | bytes 90144 | tf_op jit(solution)/shard_map/ppermute | solution.py:639
  83.3 0.5 collective-permute-done.13.refs_2_
  83.9 1.6 %collective-permute-start.16 = (bf16[2,48,512]{2,1,0:T(8,128)(2,1)S(1)}, bf16[2,48,512]{2,1,0:T(8,128)(2,1)S(1)}, u32[]{:S(2)}, u32[]{:S(2)}) collective-permute-start(bf16[2,48,512]{2,1,0:T(8,128)(2,1)S(1)} %get-tuple-element.147), channel_id=1, source_target_pairs={{0,2},{1,3},{2,0},{3,1},{4,6},{5,7},{6,4},{7,5},{8,10},{9,11},{10,... | collective-permute-start | bytes 294920 | tf_op jit(solution)/shard_map/ppermute | solution.py:639
  85.6 0.9 collective-permute-start.3
  86.5 3.9 %collective-permute-done.16.refs_1_ = bf16[2,48,512]{2,1,0:T(8,128)(2,1)S(1)} collective-permute-done((bf16[2,48,512]{2,1,0:T(8,128)(2,1)S(1)}, bf16[2,48,512]{2,1,0:T(8,128)(2,1)S(1)}, u32[]{:S(2)}, u32[]{:S(2)}) %collective-permute-start.16) | collective-permute-done | bytes 98336 | tf_op jit(solution)/shard_map/ppermute | solution.py:639
  90.5 2.1 %collective-permute-start.23 = (bf16[4,88,512]{2,1,0:T(8,128)(2,1)S(1)}, bf16[4,88,512]{2,1,0:T(8,128)(2,1)S(1)}, u32[]{:S(2)}, u32[]{:S(2)}) collective-permute-start(bf16[4,88,512]{2,1,0:T(8,128)(2,1)S(1)} %join.9.refs_1_), channel_id=1, source_target_pairs={{0,17},{1,16},{2,19},{3,18},{4,21},{5,20},{6,23},{7,22},{8,25},{9,... | collective-permute-start | bytes 1081352 | tf_op jit(solution)/shard_map/ppermute | solution.py:639
  92.6 1.0 collective-permute-start.22
  93.6 0.4 collective-permute-start.21
  94.0 0.8 collective-permute-start.17
  94.8 10.1 %collective-permute-done.17.refs_2_ = bf16[1,48,512]{2,1,0:T(8,128)(2,1)S(1)} collective-permute-done((bf16[1,48,512]{2,1,0:T(8,128)(2,1)S(1)}, bf16[1,48,512]{2,1,0:T(8,128)(2,1)S(1)}, u32[]{:S(2)}, u32[]{:S(2)}) %collective-permute-start.17) | collective-permute-done | bytes 49184 | tf_op jit(solution)/shard_map/ppermute | solution.py:639
  105.0 5.0 %collective-permute-done.18.refs_1_ = bf16[1,48,512]{2,1,0:T(8,128)(2,1)S(1)} collective-permute-done((bf16[1,48,512]{2,1,0:T(8,128)(2,1)S(1)}, bf16[1,48,512]{2,1,0:T(8,128)(2,1)S(1)}, u32[]{:S(2)}, u32[]{:S(2)}) %collective-permute-start.18) | collective-permute-done | bytes 49184 | tf_op jit(solution)/shard_map/ppermute | solution.py:639
  110.0 1.9 %collective-permute-start.19 = (bf16[2,48,512]{2,1,0:T(8,128)(2,1)S(1)}, bf16[2,48,512]{2,1,0:T(8,128)(2,1)S(1)}, u32[]{:S(2)}, u32[]{:S(2)}) collective-permute-start(bf16[2,48,512]{2,1,0:T(8,128)(2,1)S(1)} %join.7.refs_1_), channel_id=1, source_target_pairs={{0,2},{1,3},{2,0},{3,1},{4,6},{5,7},{6,4},{7,5},{8,10},{9,11},{10,... | collective-permute-start | bytes 294920 | tf_op jit(solution)/shard_map/ppermute | solution.py:639
  111.9 2.8 %collective-permute-done.19.refs_2_ = bf16[2,48,512]{2,1,0:T(8,128)(2,1)S(1)} collective-permute-done((bf16[2,48,512]{2,1,0:T(8,128)(2,1)S(1)}, bf16[2,48,512]{2,1,0:T(8,128)(2,1)S(1)}, u32[]{:S(2)}, u32[]{:S(2)}) %collective-permute-start.19) | collective-permute-done | bytes 98336 | tf_op jit(solution)/shard_map/ppermute | solution.py:639
  114.9 2.2 %collective-permute-start.27 = (bf16[4,48,512]{2,1,0:T(8,128)(2,1)S(1)}, bf16[4,48,512]{2,1,0:T(8,128)(2,1)S(1)}, u32[]{:S(2)}, u32[]{:S(2)}) collective-permute-start(bf16[4,48,512]{2,1,0:T(8,128)(2,1)S(1)} %join.8.refs_0_.refs_2_), channel_id=1, source_target_pairs={{0,17},{1,16},{2,19},{3,18},{4,21},{5,20},{6,23},{7,22},{8,25},{9,... | collective-permute-start | bytes 589832 | tf_op jit(solution)/shard_map/ppermute | solution.py:639
  117.1 0.6 collective-permute-start.26
  117.7 0.8 collective-permute-start.25
  118.5 3.9 %finish.1 = (f32[6,256,512]{2,1,0:T(8,128)}, f32[8,128]{1,0:T(8,128)S(1)}) custom-call(bf16[16,88,512]{2,1,0:T(8,128)(2,1)S(1)} %join.10.refs_0_, bf16[6,256,512]{2,1,0:T(8,128)(2,1)S(1)} %copy-done, f32[6,256,512]{2,1,0:T(8,128)S(1)} %get-tuple-element.150.refs_2_, bf16[6,64,512]{2,1,0:T(8,128)(2,1)S(1)} %collective-permute-done.12.refs_0_.refs_3_, ...), custom_call_target="tpu_custom_call" | custom-call | flops 1000000 | bytes 118026 | tf_op jit(solution)/shard_map/finish/pallas_call | solution.py:659
  122.3 3.0 %place.2 = (f32[512,1536]{1,0:T(8,128)}, f32[512,512]{1,0:T(8,128)}, f32[768,512]{1,0:T(8,128)}, f32[1,512]{1,0:T(1,128)}, f32[8,128]{1,0:T(8,128)S(1)}) custom-call(bf16[16,88,512]{2,1,0:T(8,128)(2,1)S(1)} %join.10.refs_0_, bf16[16,88,512]{2,1,0:T(8,128)(2,1)S(1)} %collective-permute-done.24.refs_1_, bf16[512,1536]{1,0:T(8,128)(2,1)S(1)} %copy-done.2, ...), custom_call_target="tpu_custom_call" | custom-call | flops 10000 | bytes 102318 | tf_op jit(solution)/shard_map/place/pallas_call | solution.py:659
  125.4 1.8 %collective-permute-done.26.refs_4_ = bf16[4,48,512]{2,1,0:T(8,128)(2,1)S(1)} collective-permute-done((bf16[4,48,512]{2,1,0:T(8,128)(2,1)S(1)}, bf16[4,48,512]{2,1,0:T(8,128)(2,1)S(1)}, u32[]{:S(2)}, u32[]{:S(2)}) %collective-permute-start.26) | collective-permute-done | bytes 196640 | tf_op jit(solution)/shard_map/ppermute | solution.py:639
  127.5 2.3 %collective-permute-done.28.refs_1_ = bf16[16,48,512]{2,1,0:T(8,128)(2,1)S(1)} collective-permute-done((bf16[16,48,512]{2,1,0:T(8,128)(2,1)S(1)}, bf16[16,48,512]{2,1,0:T(8,128)(2,1)S(1)}, u32[]{:S(2)}, u32[]{:S(2)}) %collective-permute-start.28) | collective-permute-done | bytes 786464 | tf_op jit(solution)/shard_map/ppermute | solution.py:639
  129.7 2.0 %place.3 = (f32[512,1536]{1,0:T(8,128)}, f32[1,512]{1,0:T(1,128)}, f32[8,128]{1,0:T(8,128)}) custom-call(bf16[16,48,512]{2,1,0:T(8,128)(2,1)S(1)} %join.11.refs_0_, bf16[16,48,512]{2,1,0:T(8,128)(2,1)S(1)} %collective-permute-done.28.refs_1_, bf16[512,1536]{1,0:T(8,128)(2,1)S(1)} %get-tuple-element.86.refs_2_, ...), custom_call_target="tpu_custom_call" | custom-call | flops 10000 | bytes 62996 | tf_op jit(solution)/shard_map/place/pallas_call | solution.py:659
  (52 shorter events, 1.9 us)
Async XLA Ops:
  0.6 5.7 %copy-start = (bf16[6,256,512]{2,1,0:T(8,128)(2,1)S(1)}, bf16[6,256,512]{2,1,0:T(8,128)(2,1)}, u32[]{:S(2)}) copy-start(bf16[6,256,512]{2,1,0:T(8,128)(2,1)} %refs_1_.5) | copy-start | bytes 4718596
  2.6 19.8 %collective-permute-start = (bf16[6,64,512]{2,1,0:T(8,128)(2,1)S(1)}, bf16[6,64,512]{2,1,0:T(8,128)(2,1)S(1)}, u32[]{:S(2)}, u32[]{:S(2)}) collective-permute-start(bf16[6,64,512]{2,1,0:T(8,128)(2,1)S(1)} %get-tuple-element.100), channel_id=1, source_target_pairs={{0,1},{1,0},{2,3},{3,2},{4,5},{5,4},{6,7},{7,6},{8,9},{9,8},{10,11... | collective-permute-start | bytes 1179656 | tf_op jit(solution)/shard_map/ppermute | solution.py:625
  5.6 16.8 %collective-permute-start.1 = (bf16[6,64,512]{2,1,0:T(8,128)(2,1)S(1)}, bf16[6,64,512]{2,1,0:T(8,128)(2,1)S(1)}, u32[]{:S(2)}, u32[]{:S(2)}) collective-permute-start(bf16[6,64,512]{2,1,0:T(8,128)(2,1)S(1)} %get-tuple-element.101), channel_id=1, source_target_pairs={{1,2},{2,1},{3,4},{4,3},{5,6},{6,5},{9,10},{10,9},{11,12},{12,11},... | collective-permute-start | bytes 1179656 | tf_op jit(solution)/shard_map/ppermute | solution.py:625
  10.1 3.2 %copy-start.1 = (bf16[6,256,512]{2,1,0:T(8,128)(2,1)S(1)}, bf16[6,256,512]{2,1,0:T(8,128)(2,1)}, u32[]{:S(2)}) copy-start(bf16[6,256,512]{2,1,0:T(8,128)(2,1)} %refs_0_.11) | copy-start | bytes 4718596
  10.1 3.2 %copy-start.2 = (bf16[512,1536]{1,0:T(8,128)(2,1)S(1)}, bf16[512,1536]{1,0:T(8,128)(2,1)}, u32[]{:S(2)}) copy-start(bf16[512,1536]{1,0:T(8,128)(2,1)} %refs_2_.3) | copy-start | bytes 4718596
  10.1 3.2 %copy-start.3 = (bf16[768,512]{1,0:T(8,128)(2,1)S(1)}, bf16[768,512]{1,0:T(8,128)(2,1)}, u32[]{:S(2)}) copy-start(bf16[768,512]{1,0:T(8,128)(2,1)} %refs_5_.5) | copy-start | bytes 2359300
  10.1 3.2 %copy-start.4 = (bf16[512,512]{1,0:T(8,128)(2,1)S(1)}, bf16[512,512]{1,0:T(8,128)(2,1)}, u32[]{:S(2)}) copy-start(bf16[512,512]{1,0:T(8,128)(2,1)} %refs_3_.4) | copy-start | bytes 1572868
  10.1 3.2 %copy-start.5 = (f32[512]{0:T(512)S(1)}, f32[512]{0:T(512)}, u32[]{:S(2)}) copy-start(f32[512]{0:T(512)} %param.18) | copy-start | bytes 6148
  36.2 3.3 %collective-permute-start.2 = (bf16[16,88,512]{2,1,0:T(8,128)(2,1)S(1)}, bf16[16,88,512]{2,1,0:T(8,128)(2,1)S(1)}, u32[]{:S(2)}, u32[]{:S(2)}) collective-permute-start(bf16[16,88,512]{2,1,0:T(8,128)(2,1)S(1)} %get-tuple-element.118), channel_id=1, source_target_pairs={{0,8},{1,9},{2,10},{3,11},{4,12},{5,13},{6,14},{7,15},{8,0},{9,1},... | collective-permute-start | bytes 4325384 | tf_op jit(solution)/shard_map/ppermute | solution.py:639
  39.8 23.2 %collective-permute-start.4 = (bf16[4,88,512]{2,1,0:T(8,128)(2,1)S(1)}, bf16[4,88,512]{2,1,0:T(8,128)(2,1)S(1)}, u32[]{:S(2)}, u32[]{:S(2)}) collective-permute-start(bf16[4,88,512]{2,1,0:T(8,128)(2,1)S(1)} %get-tuple-element.131), channel_id=1, source_target_pairs={{0,1},{1,0},{2,3},{3,2},{4,5},{5,4},{6,7},{7,6},{8,9},{9,8},{10,11... | collective-permute-start | bytes 1081352 | tf_op jit(solution)/shard_map/ppermute | solution.py:639
  44.2 18.9 %collective-permute-start.5 = (bf16[4,88,512]{2,1,0:T(8,128)(2,1)S(1)}, bf16[4,88,512]{2,1,0:T(8,128)(2,1)S(1)}, u32[]{:S(2)}, u32[]{:S(2)}) collective-permute-start(bf16[4,88,512]{2,1,0:T(8,128)(2,1)S(1)} %get-tuple-element.132), channel_id=1, source_target_pairs={{0,16},{1,17},{2,18},{3,19},{4,20},{5,21},{6,22},{7,23},{8,24},{9,... | collective-permute-start | bytes 1081352 | tf_op jit(solution)/shard_map/ppermute | solution.py:639
  45.6 17.5 %collective-permute-start.6 = (bf16[4,88,512]{2,1,0:T(8,128)(2,1)S(1)}, bf16[4,88,512]{2,1,0:T(8,128)(2,1)S(1)}, u32[]{:S(2)}, u32[]{:S(2)}) collective-permute-start(bf16[4,88,512]{2,1,0:T(8,128)(2,1)S(1)} %get-tuple-element.133), channel_id=1, source_target_pairs={{0,17},{1,16},{2,19},{3,18},{4,21},{5,20},{6,23},{7,22},{8,25},{9,... | collective-permute-start | bytes 1081352 | tf_op jit(solution)/shard_map/ppermute | solution.py:639
  63.6 6.5 %collective-permute-start.7 = (bf16[16,48,512]{2,1,0:T(8,128)(2,1)S(1)}, bf16[16,48,512]{2,1,0:T(8,128)(2,1)S(1)}, u32[]{:S(2)}, u32[]{:S(2)}) collective-permute-start(bf16[16,48,512]{2,1,0:T(8,128)(2,1)S(1)} %get-tuple-element.136), channel_id=1, source_target_pairs={{0,8},{1,9},{2,10},{3,11},{4,12},{5,13},{6,14},{7,15},{8,0},{9,1},... | collective-permute-start | bytes 2359304 | tf_op jit(solution)/shard_map/ppermute | solution.py:639
  63.7 19.7 %collective-permute-start.12 = (bf16[6,64,512]{2,1,0:T(8,128)(2,1)S(1)}, bf16[6,64,512]{2,1,0:T(8,128)(2,1)S(1)}, u32[]{:S(2)}, u32[]{:S(2)}) collective-permute-start(bf16[6,64,512]{2,1,0:T(8,128)(2,1)S(1)} %get-tuple-element.142), channel_id=1, source_target_pairs={{0,1},{1,0},{2,3},{3,2},{4,5},{5,4},{6,7},{7,6},{8,9},{9,8},{10,11... | collective-permute-start | bytes 1179656 | tf_op jit(solution)/shard_map/ppermute | solution.py:625
  65.7 8.6 %collective-permute-start.8 = (bf16[1,88,512]{2,1,0:T(8,128)(2,1)S(1)}, bf16[1,88,512]{2,1,0:T(8,128)(2,1)S(1)}, u32[]{:S(2)}, u32[]{:S(2)}) collective-permute-start(bf16[1,88,512]{2,1,0:T(8,128)(2,1)S(1)} %get-tuple-element.139), channel_id=1, source_target_pairs={{0,4},{1,5},{2,6},{3,7},{4,0},{5,1},{6,2},{7,3},{8,12},{9,13},{10,... | collective-permute-start | bytes 270344 | tf_op jit(solution)/shard_map/ppermute | solution.py:639
  68.2 7.5 %collective-permute-start.9 = (bf16[1,88,512]{2,1,0:T(8,128)(2,1)S(1)}, bf16[1,88,512]{2,1,0:T(8,128)(2,1)S(1)}, u32[]{:S(2)}, u32[]{:S(2)}) collective-permute-start(bf16[1,88,512]{2,1,0:T(8,128)(2,1)S(1)} %get-tuple-element.140), channel_id=1, source_target_pairs={{0,2},{1,3},{2,0},{3,1},{4,6},{5,7},{6,4},{7,5},{8,10},{9,11},{10,... | collective-permute-start | bytes 270344 | tf_op jit(solution)/shard_map/ppermute | solution.py:639
  68.2 8.0 %collective-permute-start.10 = (bf16[1,88,512]{2,1,0:T(8,128)(2,1)S(1)}, bf16[1,88,512]{2,1,0:T(8,128)(2,1)S(1)}, u32[]{:S(2)}, u32[]{:S(2)}) collective-permute-start(bf16[1,88,512]{2,1,0:T(8,128)(2,1)S(1)} %get-tuple-element.141), channel_id=1, source_target_pairs={{0,6},{1,7},{2,4},{3,5},{4,2},{5,3},{6,0},{7,1},{8,14},{9,15},{10,... | collective-permute-start | bytes 270344 | tf_op jit(solution)/shard_map/ppermute | solution.py:639
  70.2 13.6 %collective-permute-start.13 = (bf16[4,48,512]{2,1,0:T(8,128)(2,1)S(1)}, bf16[4,48,512]{2,1,0:T(8,128)(2,1)S(1)}, u32[]{:S(2)}, u32[]{:S(2)}) collective-permute-start(bf16[4,48,512]{2,1,0:T(8,128)(2,1)S(1)} %get-tuple-element.143), channel_id=1, source_target_pairs={{0,1},{1,0},{2,3},{3,2},{4,5},{5,4},{6,7},{7,6},{8,9},{9,8},{10,11... | collective-permute-start | bytes 589832 | tf_op jit(solution)/shard_map/ppermute | solution.py:639
  74.3 9.5 %collective-permute-start.14 = (bf16[4,48,512]{2,1,0:T(8,128)(2,1)S(1)}, bf16[4,48,512]{2,1,0:T(8,128)(2,1)S(1)}, u32[]{:S(2)}, u32[]{:S(2)}) collective-permute-start(bf16[4,48,512]{2,1,0:T(8,128)(2,1)S(1)} %get-tuple-element.144), channel_id=1, source_target_pairs={{0,16},{1,17},{2,18},{3,19},{4,20},{5,21},{6,22},{7,23},{8,24},{9,... | collective-permute-start | bytes 589832 | tf_op jit(solution)/shard_map/ppermute | solution.py:639
  75.7 8.1 %collective-permute-start.15 = (bf16[4,48,512]{2,1,0:T(8,128)(2,1)S(1)}, bf16[4,48,512]{2,1,0:T(8,128)(2,1)S(1)}, u32[]{:S(2)}, u32[]{:S(2)}) collective-permute-start(bf16[4,48,512]{2,1,0:T(8,128)(2,1)S(1)} %get-tuple-element.145), channel_id=1, source_target_pairs={{0,17},{1,16},{2,19},{3,18},{4,21},{5,20},{6,23},{7,22},{8,25},{9,... | collective-permute-start | bytes 589832 | tf_op jit(solution)/shard_map/ppermute | solution.py:639
  76.3 6.8 %collective-permute-start.11 = (bf16[1,88,512]{2,1,0:T(8,128)(2,1)S(1)}, bf16[1,88,512]{2,1,0:T(8,128)(2,1)S(1)}, u32[]{:S(2)}, u32[]{:S(2)}) collective-permute-start(bf16[1,88,512]{2,1,0:T(8,128)(2,1)S(1)} %add.10.refs_1_), channel_id=1, source_target_pairs={{0,4},{1,5},{2,6},{3,7},{4,0},{5,1},{6,2},{7,3},{8,12},{9,13},{10,... | collective-permute-start | bytes 270344 | tf_op jit(solution)/shard_map/ppermute | solution.py:639
  83.1 7.3 %collective-permute-start.20 = (bf16[2,88,512]{2,1,0:T(8,128)(2,1)S(1)}, bf16[2,88,512]{2,1,0:T(8,128)(2,1)S(1)}, u32[]{:S(2)}, u32[]{:S(2)}) collective-permute-start(bf16[2,88,512]{2,1,0:T(8,128)(2,1)S(1)} %join.6.refs_0_.refs_1_), channel_id=1, source_target_pairs={{0,2},{1,3},{2,0},{3,1},{4,6},{5,7},{6,4},{7,5},{8,10},{9,11},{10,... | collective-permute-start | bytes 540680 | tf_op jit(solution)/shard_map/ppermute | solution.py:639
  83.9 6.5 %collective-permute-start.16 = (bf16[2,48,512]{2,1,0:T(8,128)(2,1)S(1)}, bf16[2,48,512]{2,1,0:T(8,128)(2,1)S(1)}, u32[]{:S(2)}, u32[]{:S(2)}) collective-permute-start(bf16[2,48,512]{2,1,0:T(8,128)(2,1)S(1)} %get-tuple-element.147), channel_id=1, source_target_pairs={{0,2},{1,3},{2,0},{3,1},{4,6},{5,7},{6,4},{7,5},{8,10},{9,11},{10,... | collective-permute-start | bytes 294920 | tf_op jit(solution)/shard_map/ppermute | solution.py:639
  85.6 26.3 %collective-permute-start.3 = (bf16[6,64,512]{2,1,0:T(8,128)(2,1)S(1)}, bf16[6,64,512]{2,1,0:T(8,128)(2,1)S(1)}, u32[]{:S(2)}, u32[]{:S(2)}) collective-permute-start(bf16[6,64,512]{2,1,0:T(8,128)(2,1)S(1)} %get-tuple-element.124), channel_id=1, source_target_pairs={{1,2},{2,1},{3,4},{4,3},{5,6},{6,5},{9,10},{10,9},{11,12},{12,11},... | collective-permute-start | bytes 1179656 | tf_op jit(solution)/shard_map/ppermute | solution.py:625
  90.5 24.2 %collective-permute-start.23 = (bf16[4,88,512]{2,1,0:T(8,128)(2,1)S(1)}, bf16[4,88,512]{2,1,0:T(8,128)(2,1)S(1)}, u32[]{:S(2)}, u32[]{:S(2)}) collective-permute-start(bf16[4,88,512]{2,1,0:T(8,128)(2,1)S(1)} %join.9.refs_1_), channel_id=1, source_target_pairs={{0,17},{1,16},{2,19},{3,18},{4,21},{5,20},{6,23},{7,22},{8,25},{9,... | collective-permute-start | bytes 1081352 | tf_op jit(solution)/shard_map/ppermute | solution.py:639
  92.6 22.1 %collective-permute-start.22 = (bf16[4,88,512]{2,1,0:T(8,128)(2,1)S(1)}, bf16[4,88,512]{2,1,0:T(8,128)(2,1)S(1)}, u32[]{:S(2)}, u32[]{:S(2)}) collective-permute-start(bf16[4,88,512]{2,1,0:T(8,128)(2,1)S(1)} %join.9.refs_1_), channel_id=1, source_target_pairs={{0,16},{1,17},{2,18},{3,19},{4,20},{5,21},{6,22},{7,23},{8,24},{9,... | collective-permute-start | bytes 1081352 | tf_op jit(solution)/shard_map/ppermute | solution.py:639
  93.6 21.1 %collective-permute-start.21 = (bf16[4,88,512]{2,1,0:T(8,128)(2,1)S(1)}, bf16[4,88,512]{2,1,0:T(8,128)(2,1)S(1)}, u32[]{:S(2)}, u32[]{:S(2)}) collective-permute-start(bf16[4,88,512]{2,1,0:T(8,128)(2,1)S(1)} %join.9.refs_1_), channel_id=1, source_target_pairs={{0,1},{1,0},{2,3},{3,2},{4,5},{5,4},{6,7},{7,6},{8,9},{9,8},{10,11... | collective-permute-start | bytes 1081352 | tf_op jit(solution)/shard_map/ppermute | solution.py:639
  94.0 10.8 %collective-permute-start.17 = (bf16[1,48,512]{2,1,0:T(8,128)(2,1)S(1)}, bf16[1,48,512]{2,1,0:T(8,128)(2,1)S(1)}, u32[]{:S(2)}, u32[]{:S(2)}) collective-permute-start(bf16[1,48,512]{2,1,0:T(8,128)(2,1)S(1)} %get-tuple-element.149), channel_id=1, source_target_pairs={{0,4},{1,5},{2,6},{3,7},{4,0},{5,1},{6,2},{7,3},{8,12},{9,13},{10,... | collective-permute-start | bytes 147464 | tf_op jit(solution)/shard_map/ppermute | solution.py:639
  104.9 5.1 %collective-permute-start.18 = (bf16[1,48,512]{2,1,0:T(8,128)(2,1)S(1)}, bf16[1,48,512]{2,1,0:T(8,128)(2,1)S(1)}, u32[]{:S(2)}, u32[]{:S(2)}) collective-permute-start(bf16[1,48,512]{2,1,0:T(8,128)(2,1)S(1)} %add.13.refs_0_), channel_id=1, source_target_pairs={{0,4},{1,5},{2,6},{3,7},{4,0},{5,1},{6,2},{7,3},{8,12},{9,13},{10,... | collective-permute-start | bytes 147464 | tf_op jit(solution)/shard_map/ppermute | solution.py:639
  110.0 4.7 %collective-permute-start.19 = (bf16[2,48,512]{2,1,0:T(8,128)(2,1)S(1)}, bf16[2,48,512]{2,1,0:T(8,128)(2,1)S(1)}, u32[]{:S(2)}, u32[]{:S(2)}) collective-permute-start(bf16[2,48,512]{2,1,0:T(8,128)(2,1)S(1)} %join.7.refs_1_), channel_id=1, source_target_pairs={{0,2},{1,3},{2,0},{3,1},{4,6},{5,7},{6,4},{7,5},{8,10},{9,11},{10,... | collective-permute-start | bytes 294920 | tf_op jit(solution)/shard_map/ppermute | solution.py:639
  114.8 7.5 %collective-permute-start.24 = (bf16[16,88,512]{2,1,0:T(8,128)(2,1)S(1)}, bf16[16,88,512]{2,1,0:T(8,128)(2,1)S(1)}, u32[]{:S(2)}, u32[]{:S(2)}) collective-permute-start(bf16[16,88,512]{2,1,0:T(8,128)(2,1)S(1)} %join.10.refs_0_), channel_id=1, source_target_pairs={{0,8},{1,9},{2,10},{3,11},{4,12},{5,13},{6,14},{7,15},{8,0},{9,1},... | collective-permute-start | bytes 4325384 | tf_op jit(solution)/shard_map/ppermute | solution.py:639
  114.9 10.5 %collective-permute-start.27 = (bf16[4,48,512]{2,1,0:T(8,128)(2,1)S(1)}, bf16[4,48,512]{2,1,0:T(8,128)(2,1)S(1)}, u32[]{:S(2)}, u32[]{:S(2)}) collective-permute-start(bf16[4,48,512]{2,1,0:T(8,128)(2,1)S(1)} %join.8.refs_0_.refs_2_), channel_id=1, source_target_pairs={{0,17},{1,16},{2,19},{3,18},{4,21},{5,20},{6,23},{7,22},{8,25},{9,... | collective-permute-start | bytes 589832 | tf_op jit(solution)/shard_map/ppermute | solution.py:639
  117.1 10.0 %collective-permute-start.26 = (bf16[4,48,512]{2,1,0:T(8,128)(2,1)S(1)}, bf16[4,48,512]{2,1,0:T(8,128)(2,1)S(1)}, u32[]{:S(2)}, u32[]{:S(2)}) collective-permute-start(bf16[4,48,512]{2,1,0:T(8,128)(2,1)S(1)} %join.8.refs_0_.refs_2_), channel_id=1, source_target_pairs={{0,16},{1,17},{2,18},{3,19},{4,20},{5,21},{6,22},{7,23},{8,24},{9,... | collective-permute-start | bytes 589832 | tf_op jit(solution)/shard_map/ppermute | solution.py:639
  117.7 9.7 %collective-permute-start.25 = (bf16[4,48,512]{2,1,0:T(8,128)(2,1)S(1)}, bf16[4,48,512]{2,1,0:T(8,128)(2,1)S(1)}, u32[]{:S(2)}, u32[]{:S(2)}) collective-permute-start(bf16[4,48,512]{2,1,0:T(8,128)(2,1)S(1)} %join.8.refs_0_.refs_2_), channel_id=1, source_target_pairs={{0,1},{1,0},{2,3},{3,2},{4,5},{5,4},{6,7},{7,6},{8,9},{9,8},{10,11... | collective-permute-start | bytes 589832 | tf_op jit(solution)/shard_map/ppermute | solution.py:639
  127.4 2.4 %collective-permute-start.28 = (bf16[16,48,512]{2,1,0:T(8,128)(2,1)S(1)}, bf16[16,48,512]{2,1,0:T(8,128)(2,1)S(1)}, u32[]{:S(2)}, u32[]{:S(2)}) collective-permute-start(bf16[16,48,512]{2,1,0:T(8,128)(2,1)S(1)} %join.11.refs_0_), channel_id=1, source_target_pairs={{0,8},{1,9},{2,10},{3,11},{4,12},{5,13},{6,14},{7,15},{8,0},{9,1},... | collective-permute-start | bytes 2359304 | tf_op jit(solution)/shard_map/ppermute | solution.py:639
